TPU v7x, 512 devices: a whole 4x8x8 slice. The times are simulated.
512 devices in a mesh: tm: 32 (over y_lo, z), dp: 16 (over x, y_hi, core).
Axes of the slice: x: 4, y: 8 (y_hi: 2, y_lo: 4; y = y_hi * 4 + y_lo), z: 8, core: 2. Of those that a mesh axis runs over, the one named last changes fastest.
Arguments:
- query_raw: bfloat16 [16, 4096, 1536], P('dp', 'tm'), may hold values from -500 to 500
- key_raw: bfloat16 [16, 4096, 1536], P('dp', 'tm'), may hold values from -500 to 500
- value_rows: bfloat16 [16, 4096, 1536], P('dp', 'tm'), may hold values from -6 to 6
- grad_output: bfloat16 [16, 4096, 1536], P('dp', 'tm'), may hold values from -1200 to 1200
- log_normalizer: float32 [16, 12, 4096], P('dp', None, 'tm'), may hold values from 6 to 8
- output_dot: float32 [16, 12, 4096], P('dp', None, 'tm'), may hold values from -384 to 384
- query_gain: float32 [128], replicated, may hold values from 0.1 to 1.9
- key_gain: float32 [128], replicated, may hold values from 0.1 to 1.9
- route_blocks: int32 [16, 32, 2], P('dp'), may hold values from 0 to 2, as said below
- route_count: int32 [16, 32], P('dp'), may hold values from 1 to 2, as said below
- query_reach: int32 [16, 64], P('dp'), may hold values from 1 to 12, as said below
Outputs:
- query_grad: bfloat16 [16, 4096, 1536], P('dp', 'tm')
- key_grad: bfloat16 [16, 4096, 1536], P('dp', 'tm')
- value_grad: bfloat16 [16, 4096, 1536], P('dp', 'tm')
- query_gain_grad: float32 [128], replicated
- key_gain_grad: float32 [128], replicated
Inputs may be any that keep to these rules, and one draw needn't show every extreme that they name: `route_blocks`: for each clip and shard, 2 different blocks of the shard; only the first route_count of them are routed. `route_count`: in every clip some shard routes 2 blocks. `query_reach`: in every clip some slot block has reach 12.
All inputs are finite; a program needn't handle non-finite values.
Results may differ from a plain program's by a relative error of at most 0.0083.
Values may be sent and summed in bfloat16 or wider, within the bound.
No kernel may reach another device: no remote copies, remote signals or barrier semaphores. Data moves between devices by JAX's collectives and lax.ppermute only.
A program may use at most 64 MiB of HBM per device.

v0:
```python
import jax
import jax.numpy as jnp
from jax import lax
from jax.sharding import PartitionSpec as P

BLK = 64
NBLK = 3
ROUTE_MOST = 2
STEPS = 4


norm_eps = 1e-06


def passed_along(value, axis, steps):
    count = lax.axis_size(axis)
    pairs = [(source, (source + steps) % count) for source in range(count)]
    return lax.ppermute(value, axis, pairs)


def prepare(raw_heads, gain_vector):
    widened = raw_heads.astype(jnp.float32)
    inverse = lax.rsqrt(jnp.mean(widened * widened, axis=-1, keepdims=True) + norm_eps)
    normal_unit = widened * inverse
    return (normal_unit, inverse, (normal_unit * gain_vector).astype(jnp.bfloat16))


def norm_back(grad_normed, normal_unit, inverse, gain_vector):
    scaled = grad_normed * gain_vector
    grad_raw = inverse * (
        scaled - normal_unit * jnp.mean(scaled * normal_unit, axis=-1, keepdims=True)
    )
    summed_axes = tuple(range(normal_unit.ndim - 1))
    return (grad_raw, jnp.sum(grad_normed * normal_unit, axis=summed_axes))


def allowed_pairs(tables, query_src, key_src, offset):
    blocks, counts, reaches = tables
    slot_index = jnp.arange(ROUTE_MOST * BLK, dtype=jnp.int32)
    query_blocks = jnp.repeat(lax.dynamic_index_in_dim(blocks, query_src, 0, False), BLK)
    key_blocks = jnp.repeat(lax.dynamic_index_in_dim(blocks, key_src, 0, False), BLK)
    reach_rows = jnp.repeat(
        lax.dynamic_slice_in_dim(reaches, query_src * ROUTE_MOST, ROUTE_MOST), BLK
    )
    query_live = slot_index < lax.dynamic_index_in_dim(counts, query_src, 0, False) * BLK
    key_live = slot_index < lax.dynamic_index_in_dim(counts, key_src, 0, False) * BLK
    within_reach = offset * NBLK + query_blocks[:, None] - key_blocks[None, :] < reach_rows[:, None]
    return query_live[:, None] & key_live[None, :] & within_reach


def pair_terms(query_side, key_side, allowed):
    query_normed, output_heads, log_rows, dot_rows = query_side
    key_normed, value_heads = key_side
    score_scale = query_normed.shape[-1] ** (-0.5)
    scores = (
        jnp.einsum("qhd,khd->hqk", query_normed, key_normed, preferred_element_type=jnp.float32)
        * score_scale
    )
    probability = jnp.where(allowed[None], jnp.exp(scores - log_rows[:, :, None]), 0.0)
    weights_low = probability.astype(jnp.bfloat16)
    grad_values = jnp.einsum(
        "hqk,qhd->khd", weights_low, output_heads, preferred_element_type=jnp.float32
    )
    grad_weights = jnp.einsum(
        "qhd,khd->hqk", output_heads, value_heads, preferred_element_type=jnp.float32
    )
    grad_scores = (probability * (grad_weights - dot_rows[:, :, None])).astype(jnp.bfloat16)
    grad_query = (
        jnp.einsum("hqk,khd->qhd", grad_scores, key_normed, preferred_element_type=jnp.float32)
        * score_scale
    )
    grad_key = (
        jnp.einsum("hqk,qhd->khd", grad_scores, query_normed, preferred_element_type=jnp.float32)
        * score_scale
    )
    return (grad_query, grad_key, grad_values)


def guarded(query_side, key_side, allowed):
    return pair_terms(query_side, key_side, allowed)


def body(
    query_raw,
    key_raw,
    value_rows,
    grad_output,
    log_normalizer,
    output_dot,
    query_gain,
    key_gain,
    route_blocks,
    route_count,
    query_reach,
):
    slot_rows = query_raw.shape[1]
    head_count = log_normalizer.shape[1]
    head_width = query_raw.shape[2] // head_count
    head_shape = (slot_rows, head_count, head_width)
    flat_shape = (slot_rows, head_count * head_width)
    shard_count = lax.axis_size("tm")
    shard_here = lax.axis_index("tm")
    tables = (route_blocks[0], route_count[0], query_reach[0])
    query_unit, query_inverse, query_normed = prepare(query_raw[0].reshape(head_shape), query_gain)
    key_unit, key_inverse, key_normed = prepare(key_raw[0].reshape(head_shape), key_gain)
    output_heads = grad_output[0].reshape(head_shape)
    key_flat = key_normed.reshape(flat_shape)
    own_query = (query_normed, output_heads, log_normalizer[0], output_dot[0])
    held_keys = passed_along((key_flat, value_rows[0]), "tm", STEPS - 1)
    query_total = jnp.zeros(head_shape, jnp.float32)
    carried = (jnp.zeros(flat_shape, jnp.float32), jnp.zeros(flat_shape, jnp.float32))
    for step_index in range(STEPS):
        offset = STEPS - 1 - step_index
        source = (shard_here - offset) % shard_count
        key_side = (held_keys[0].reshape(head_shape), held_keys[1].reshape(head_shape))
        query_part, key_part, value_part = guarded(
            own_query, key_side, allowed_pairs(tables, shard_here, source, offset)
        )
        query_total = query_total + query_part
        carried = (
            carried[0] + key_part.reshape(flat_shape),
            carried[1] + value_part.reshape(flat_shape),
        )
        if offset > 0:
            carried = passed_along((carried[0], carried[1]), "tm", -1)
            if offset > 1:
                held_keys = passed_along((held_keys[0], held_keys[1]), "tm", -1)
            else:
                held_keys = (key_flat, value_rows[0])
    key_total, value_total = carried
    query_grad, query_term = norm_back(query_total, query_unit, query_inverse, query_gain)
    key_grad, key_term = norm_back(key_total.reshape(head_shape), key_unit, key_inverse, key_gain)
    gain_totals = lax.psum((query_term, key_term), ("tm", "dp"))
    divisor = shard_count * lax.axis_size("dp")
    return (
        query_grad.reshape(1, slot_rows, -1).astype(jnp.bfloat16),
        key_grad.reshape(1, slot_rows, -1).astype(jnp.bfloat16),
        value_total.reshape(1, slot_rows, -1).astype(jnp.bfloat16),
        gain_totals[0] / divisor,
        gain_totals[1] / divisor,
    )


def solution(mesh):
    placed = (
        P("dp", "tm", None),
        P("dp", "tm", None),
        P("dp", "tm", None),
        P("dp", "tm", None),
        P("dp", None, "tm"),
        P("dp", None, "tm"),
        P(),
        P(),
        P("dp", None, None),
        P("dp", None),
        P("dp", None),
    )
    return jax.shard_map(
        body,
        mesh=mesh,
        in_specs=placed,
        out_specs=(P("dp", "tm", None), P("dp", "tm", None), P("dp", "tm", None), P(), P()),
        check_vma=False,
    )
```

profile of v0, /device:TPU:1, one launch (start us, length us, event | category | flops | bytes accessed | tf_op | source)
XLA Modules:
  0.0 309.3 jit_solution(12900735789684020791)
XLA Ops:
  0.6 1.2 copy.75
  2.7 1.0 multiply_convert_fusion.3
  3.7 8.6 %collective-permute-start = (bf16[128,1536]{0,1:T(8,128)(2,1)}, bf16[128,1536]{0,1:T(8,128)(2,1)}, u32[]{:S(2)}, u32[]{:S(2)}) collective-permute-start(bf16[128,1536]{0,1:T(8,128)(2,1)} %multiply_convert_fusion.3), channel_id=1, source_target_pairs={{0,48},{16,64},{32,80},{48,96},{64,112},{80,128},{96,144},{112,160... | collective-permute-start | bytes 1179656 | tf_op jit(solution)/shard_map/ppermute | solution.py:18
  12.5 7.0 %collective-permute-start.1 = (bf16[128,1536]{0,1:T(8,128)(2,1)S(1)}, bf16[128,1536]{0,1:T(8,128)(2,1)}, u32[]{:S(2)}, u32[]{:S(2)}) collective-permute-start(bf16[128,1536]{0,1:T(8,128)(2,1)S(1)} %bitcast.147), channel_id=1, source_target_pairs={{0,48},{16,64},{32,80},{48,96},{64,112},{80,128},{96,144},{112,160... | collective-permute-start | bytes 1179656 | tf_op jit(solution)/shard_map/ppermute | solution.py:18
  28.6 0.8 fusion.36
  29.9 1.2 fusion.26
  31.5 1.2 convolution_multiply_fusion
  32.7 2.3 copy.98
  35.0 1.3 fusion.44
  36.3 4.8 %collective-permute-done = bf16[128,1536]{0,1:T(8,128)(2,1)} collective-permute-done((bf16[128,1536]{0,1:T(8,128)(2,1)}, bf16[128,1536]{0,1:T(8,128)(2,1)}, u32[]{:S(2)}, u32[]{:S(2)}) %collective-permute-start) | collective-permute-done | bytes 393248 | tf_op jit(solution)/shard_map/ppermute | solution.py:18
  41.1 1.4 fusion.2
  42.6 1.1 fusion.32
  43.7 24.1 %collective-permute-done.1 = bf16[128,1536]{0,1:T(8,128)(2,1)} collective-permute-done((bf16[128,1536]{0,1:T(8,128)(2,1)S(1)}, bf16[128,1536]{0,1:T(8,128)(2,1)}, u32[]{:S(2)}, u32[]{:S(2)}) %collective-permute-start.1) | collective-permute-done | bytes 393248 | tf_op jit(solution)/shard_map/ppermute | solution.py:18
  67.9 1.4 fusion.22
  69.3 11.4 %collective-permute-start.2 = (bf16[128,1536]{0,1:T(8,128)(2,1)}, bf16[128,1536]{0,1:T(8,128)(2,1)S(1)}, u32[]{:S(2)}, u32[]{:S(2)}) collective-permute-start(bf16[128,1536]{0,1:T(8,128)(2,1)} %collective-permute-done), channel_id=1, source_target_pairs={{0,496},{16,0},{32,16},{48,32},{64,48},{80,64},{96,80},{112,96},{1... | collective-permute-start | bytes 1179656 | tf_op jit(solution)/shard_map/ppermute | solution.py:18
  80.7 1.2 convolution_multiply_fusion.3
  81.9 1.9 collective-permute-start.6
  83.8 2.3 copy.95
  86.1 2.0 collective-permute-start.9
  88.2 1.9 collective-permute-start.3
  90.1 2.3 fusion.45
  92.4 0.7 copy-done.6
  93.2 1.4 fusion.6
  94.6 1.1 fusion.30
  95.8 2.3 copy.96
  98.1 3.2 %collective-permute-start.4 = (bf16[128,1536]{0,1:T(8,128)(2,1)}, bf16[128,1536]{0,1:T(8,128)(2,1)S(1)}, u32[]{:S(2)}, u32[]{:S(2)}) collective-permute-start(bf16[128,1536]{0,1:T(8,128)(2,1)} %copy-done.6), channel_id=1, source_target_pairs={{0,496},{16,0},{32,16},{48,32},{64,48},{80,64},{96,80},{112,96},{1... | collective-permute-start | bytes 1179656 | tf_op jit(solution)/shard_map/ppermute | solution.py:18
  101.3 28.6 %collective-permute-done.3 = bf16[128,1536]{0,1:T(8,128)(2,1)} collective-permute-done((bf16[128,1536]{0,1:T(8,128)(2,1)}, bf16[128,1536]{0,1:T(8,128)(2,1)}, u32[]{:S(2)}, u32[]{:S(2)}) %collective-permute-start.3) | collective-permute-done | bytes 393248 | tf_op jit(solution)/shard_map/ppermute | solution.py:18
  129.9 8.0 %collective-permute-start.5 = (bf16[128,1536]{0,1:T(8,128)(2,1)}, bf16[128,1536]{0,1:T(8,128)(2,1)S(1)}, u32[]{:S(2)}, u32[]{:S(2)}) collective-permute-start(bf16[128,1536]{0,1:T(8,128)(2,1)} %collective-permute-done.3), channel_id=1, source_target_pairs={{0,496},{16,0},{32,16},{48,32},{64,48},{80,64},{96,80},{112,96},{1... | collective-permute-start | bytes 1179656 | tf_op jit(solution)/shard_map/ppermute | solution.py:18
  137.9 1.5 fusion.21
  140.2 1.3 bitcast_add_fusion.2
  141.5 1.9 collective-permute-start.7
  143.4 2.2 add.160
  145.6 1.9 collective-permute-start.10
  149.0 13.2 %collective-permute-done.7 = f32[128,1536]{0,1:T(8,128)S(1)} collective-permute-done((f32[128,1536]{0,1:T(8,128)S(1)}, f32[128,1536]{0,1:T(8,128)S(1)}, u32[]{:S(2)}, u32[]{:S(2)}) %collective-permute-start.7) | collective-permute-done | bytes 786464 | tf_op jit(solution)/shard_map/ppermute | solution.py:18
  162.2 1.0 bitcast_add_fusion.1
  163.2 8.0 %collective-permute-start.8 = (f32[128,1536]{0,1:T(8,128)}, f32[128,1536]{0,1:T(8,128)}, u32[]{:S(2)}, u32[]{:S(2)}) collective-permute-start(f32[128,1536]{0,1:T(8,128)} %bitcast_add_fusion.1), channel_id=1, source_target_pairs={{0,496},{16,0},{32,16},{48,32},{64,48},{80,64},{96,80},{112,96},{1... | collective-permute-start | bytes 2359304 | tf_op jit(solution)/shard_map/ppermute | solution.py:18
  171.2 1.1 multiply_reduce_fusion.1
  172.5 0.9 copy.99
  173.5 1.2 fusion.28
  174.6 1.4 copy.97
  176.1 3.1 %collective-permute-done.10 = f32[128,1536]{1,0:T(8,128)} collective-permute-done((f32[128,1536]{1,0:T(8,128)}, f32[128,1536]{1,0:T(8,128)}, u32[]{:S(2)}, u32[]{:S(2)}) %collective-permute-start.10) | collective-permute-done | bytes 786464 | tf_op jit(solution)/shard_map/ppermute | solution.py:18
  179.2 1.3 add.161
  180.4 8.0 %collective-permute-start.11 = (f32[128,1536]{1,0:T(8,128)S(1)}, f32[128,1536]{1,0:T(8,128)S(1)}, u32[]{:S(2)}, u32[]{:S(2)}) collective-permute-start(f32[128,1536]{1,0:T(8,128)S(1)} %add.161), channel_id=1, source_target_pairs={{0,496},{16,0},{32,16},{48,32},{64,48},{80,64},{96,80},{112,96},{1... | collective-permute-start | bytes 2359304 | tf_op jit(solution)/shard_map/ppermute | solution.py:18
  188.5 7.6 %collective-permute-done.8 = f32[128,1536]{0,1:T(8,128)} collective-permute-done((f32[128,1536]{0,1:T(8,128)}, f32[128,1536]{0,1:T(8,128)}, u32[]{:S(2)}, u32[]{:S(2)}) %collective-permute-start.8) | collective-permute-done | bytes 786464 | tf_op jit(solution)/shard_map/ppermute | solution.py:18
  196.0 1.4 multiply_reduce_fusion
  198.7 0.9 copy.100
  200.3 107.1 %all-reduce = (f32[128]{0:T(128)S(1)}, f32[128]{0:T(128)S(1)}) all-reduce(f32[128]{0:T(128)S(1)} %copy-done.32, f32[128]{0:T(128)S(1)} %bitcast_reduce_fusion), channel_id=1, replica_groups=mesh['tm'=32,'dp'=16] {'tm','dp'}, use_global_device_ids=true, to_apply=%region_5.6 | all-reduce | flops 256 | bytes 2048 | tf_op jit(solution)/shard_map/psum | solution.py:133
  308.5 0.8 fusion.25
  (116 shorter events, 12.7 us)
Async XLA Ops:
  0.6 21.2 %copy-start = (s32[1,64]{1,0:T(1,128)S(1)}, s32[1,64]{1,0:T(1,128)}, u32[]{:S(2)}) copy-start(s32[1,64]{1,0:T(1,128)} %param.21) | copy-start | bytes 772
  2.0 0.7 copy-start.27
  2.6 1.0 copy-start.20
  2.6 9.6 %copy-start.8 = (bf16[1,128,1536]{2,1,0:T(8,128)(2,1)S(1)}, bf16[1,128,1536]{2,1,0:T(8,128)(2,1)}, u32[]{:S(2)}) copy-start(bf16[1,128,1536]{2,1,0:T(8,128)(2,1)} %param.13) | copy-start | bytes 1179652
  3.7 15.9 %copy-start.10 = (bf16[1,128,1536]{2,1,0:T(8,128)(2,1)S(1)}, bf16[1,128,1536]{2,1,0:T(8,128)(2,1)}, u32[]{:S(2)}) copy-start(bf16[1,128,1536]{2,1,0:T(8,128)(2,1)} %param.11) | copy-start | bytes 1179652
  3.7 37.4 %collective-permute-start = (bf16[128,1536]{0,1:T(8,128)(2,1)}, bf16[128,1536]{0,1:T(8,128)(2,1)}, u32[]{:S(2)}, u32[]{:S(2)}) collective-permute-start(bf16[128,1536]{0,1:T(8,128)(2,1)} %multiply_convert_fusion.3), channel_id=1, source_target_pairs={{0,48},{16,64},{32,80},{48,96},{64,112},{80,128},{96,144},{112,160... | collective-permute-start | bytes 1179656 | tf_op jit(solution)/shard_map/ppermute | solution.py:18
  12.5 55.4 %collective-permute-start.1 = (bf16[128,1536]{0,1:T(8,128)(2,1)S(1)}, bf16[128,1536]{0,1:T(8,128)(2,1)}, u32[]{:S(2)}, u32[]{:S(2)}) collective-permute-start(bf16[128,1536]{0,1:T(8,128)(2,1)S(1)} %bitcast.147), channel_id=1, source_target_pairs={{0,48},{16,64},{32,80},{48,96},{64,112},{80,128},{96,144},{112,160... | collective-permute-start | bytes 1179656 | tf_op jit(solution)/shard_map/ppermute | solution.py:18
  19.8 7.3 %copy-start.9 = (bf16[1,128,1536]{2,1,0:T(8,128)(2,1)S(1)}, bf16[1,128,1536]{2,1,0:T(8,128)(2,1)}, u32[]{:S(2)}) copy-start(bf16[1,128,1536]{2,1,0:T(8,128)(2,1)} %param.14) | copy-start | bytes 1179652
  19.9 0.7 copy-start.28
  20.6 7.2 %copy-start.18 = (f32[128,12]{0,1:T(8,128)}, f32[128,12]{0,1:T(8,128)S(1)}, u32[]{:S(2)}) copy-start(f32[128,12]{0,1:T(8,128)S(1)} %add_rsqrt_fusion.1) | copy-start | bytes 18436
  20.6 8.8 %copy-start.11 = (f32[1,12,128]{2,1,0:T(8,128)}, f32[1,12,128]{2,1,0:T(8,128)S(1)}, u32[]{:S(2)}) copy-start(f32[1,12,128]{2,1,0:T(8,128)S(1)} %copy.122) | copy-start | bytes 18436
  20.6 0.7 copy-start.25
  22.0 0.7 copy-start.26
  27.1 0.7 copy-start.29
  27.8 0.7 copy-start.30
  28.4 2.6 copy-start.15
  35.0 6.1 %copy-start.12 = (f32[1,12,128]{2,1,0:T(8,128)S(1)}, f32[1,12,128]{2,1,0:T(8,128)}, u32[]{:S(2)}) copy-start(f32[1,12,128]{2,1,0:T(8,128)} %copy-done.11) | copy-start | bytes 18436
  35.0 6.1 %copy-start.24 = (pred[128,128]{1,0:T(8,128)(4,1)S(1)}, pred[128,128]{1,0:T(8,128)(4,1)}, u32[]{:S(2)}) copy-start(pred[128,128]{1,0:T(8,128)(4,1)} %get-tuple-element.36) | copy-start | bytes 49156
  42.6 25.3 %copy-start.16 = (f32[1,12,128]{2,1,0:T(8,128)S(1)}, f32[1,12,128]{2,1,0:T(8,128)}, u32[]{:S(2)}) copy-start(f32[1,12,128]{2,1,0:T(8,128)} %copy-done.15) | copy-start | bytes 18436
  69.3 23.1 %collective-permute-start.2 = (bf16[128,1536]{0,1:T(8,128)(2,1)}, bf16[128,1536]{0,1:T(8,128)(2,1)S(1)}, u32[]{:S(2)}, u32[]{:S(2)}) collective-permute-start(bf16[128,1536]{0,1:T(8,128)(2,1)} %collective-permute-done), channel_id=1, source_target_pairs={{0,496},{16,0},{32,16},{48,32},{64,48},{80,64},{96,80},{112,96},{1... | collective-permute-start | bytes 1179656 | tf_op jit(solution)/shard_map/ppermute | solution.py:18
  81.9 58.3 %collective-permute-start.6 = (f32[128,1536]{0,1:T(8,128)}, f32[128,1536]{0,1:T(8,128)}, u32[]{:S(2)}, u32[]{:S(2)}) collective-permute-start(f32[128,1536]{0,1:T(8,128)} %bitcast.23), channel_id=1, source_target_pairs={{0,496},{16,0},{32,16},{48,32},{64,48},{80,64},{96,80},{112,96},{1... | collective-permute-start | bytes 2359304 | tf_op jit(solution)/shard_map/ppermute | solution.py:18
  86.1 7.0 %copy-start.23 = (pred[128,128]{1,0:T(8,128)(4,1)S(1)}, pred[128,128]{1,0:T(8,128)(4,1)}, u32[]{:S(2)}) copy-start(pred[128,128]{1,0:T(8,128)(4,1)} %get-tuple-element.34) | copy-start | bytes 49156
  86.1 57.3 %collective-permute-start.9 = (f32[128,1536]{1,0:T(8,128)}, f32[128,1536]{1,0:T(8,128)}, u32[]{:S(2)}, u32[]{:S(2)}) collective-permute-start(f32[128,1536]{1,0:T(8,128)} %copy.95), channel_id=1, source_target_pairs={{0,496},{16,0},{32,16},{48,32},{64,48},{80,64},{96,80},{112,96},{1... | collective-permute-start | bytes 2359304 | tf_op jit(solution)/shard_map/ppermute | solution.py:18
  88.2 41.7 %collective-permute-start.3 = (bf16[128,1536]{0,1:T(8,128)(2,1)}, bf16[128,1536]{0,1:T(8,128)(2,1)}, u32[]{:S(2)}, u32[]{:S(2)}) collective-permute-start(bf16[128,1536]{0,1:T(8,128)(2,1)} %collective-permute-done.1), channel_id=1, source_target_pairs={{0,496},{16,0},{32,16},{48,32},{64,48},{80,64},{96,80},{112,96},{1... | collective-permute-start | bytes 1179656 | tf_op jit(solution)/shard_map/ppermute | solution.py:18
  90.1 3.1 copy-start.13
  92.4 0.7 copy-start.6
  98.1 49.5 %collective-permute-start.4 = (bf16[128,1536]{0,1:T(8,128)(2,1)}, bf16[128,1536]{0,1:T(8,128)(2,1)S(1)}, u32[]{:S(2)}, u32[]{:S(2)}) collective-permute-start(bf16[128,1536]{0,1:T(8,128)(2,1)} %copy-done.6), channel_id=1, source_target_pairs={{0,496},{16,0},{32,16},{48,32},{64,48},{80,64},{96,80},{112,96},{1... | collective-permute-start | bytes 1179656 | tf_op jit(solution)/shard_map/ppermute | solution.py:18
  129.9 18.1 %collective-permute-start.5 = (bf16[128,1536]{0,1:T(8,128)(2,1)}, bf16[128,1536]{0,1:T(8,128)(2,1)S(1)}, u32[]{:S(2)}, u32[]{:S(2)}) collective-permute-start(bf16[128,1536]{0,1:T(8,128)(2,1)} %collective-permute-done.3), channel_id=1, source_target_pairs={{0,496},{16,0},{32,16},{48,32},{64,48},{80,64},{96,80},{112,96},{1... | collective-permute-start | bytes 1179656 | tf_op jit(solution)/shard_map/ppermute | solution.py:18
  137.9 1.6 copy-start.5
  137.9 1.6 copy-start.7
  140.2 3.3 %copy-start.4 = (f32[128,1536]{1,0:T(8,128)S(1)}, f32[128,1536]{1,0:T(8,128)}, u32[]{:S(2)}) copy-start(f32[128,1536]{1,0:T(8,128)} %copy.96) | copy-start | bytes 2359300
  141.5 6.1 %copy-start.22 = (pred[128,128]{1,0:T(8,128)(4,1)S(1)}, pred[128,128]{1,0:T(8,128)(4,1)}, u32[]{:S(2)}) copy-start(pred[128,128]{1,0:T(8,128)(4,1)} %get-tuple-element.33) | copy-start | bytes 49156
  141.5 20.7 %collective-permute-start.7 = (f32[128,1536]{0,1:T(8,128)S(1)}, f32[128,1536]{0,1:T(8,128)S(1)}, u32[]{:S(2)}, u32[]{:S(2)}) collective-permute-start(f32[128,1536]{0,1:T(8,128)S(1)} %bitcast_add_fusion.2), channel_id=1, source_target_pairs={{0,496},{16,0},{32,16},{48,32},{64,48},{80,64},{96,80},{112,96},{1... | collective-permute-start | bytes 2359304 | tf_op jit(solution)/shard_map/ppermute | solution.py:18
  143.4 4.1 %copy-start.14 = (f32[1,12,128]{2,1,0:T(8,128)S(1)}, f32[1,12,128]{2,1,0:T(8,128)}, u32[]{:S(2)}) copy-start(f32[1,12,128]{2,1,0:T(8,128)} %copy-done.11) | copy-start | bytes 18436
  145.6 33.6 %collective-permute-start.10 = (f32[128,1536]{1,0:T(8,128)}, f32[128,1536]{1,0:T(8,128)}, u32[]{:S(2)}, u32[]{:S(2)}) collective-permute-start(f32[128,1536]{1,0:T(8,128)} %add.160), channel_id=1, source_target_pairs={{0,496},{16,0},{32,16},{48,32},{64,48},{80,64},{96,80},{112,96},{1... | collective-permute-start | bytes 2359304 | tf_op jit(solution)/shard_map/ppermute | solution.py:18
  147.6 0.7 copy-start.17
  149.0 22.3 %copy-start.3 = (f32[12,128,128]{2,1,0:T(8,128)S(1)}, f32[12,128,128]{2,1,0:T(8,128)}, u32[]{:S(2)}) copy-start(f32[12,128,128]{2,1,0:T(8,128)} %fusion.44) | copy-start | bytes 2359300
  149.0 22.3 %copy-start.19 = (f32[128,12]{0,1:T(8,128)S(1)}, f32[128,12]{0,1:T(8,128)}, u32[]{:S(2)}) copy-start(f32[128,12]{0,1:T(8,128)} %copy-done.18) | copy-start | bytes 18436
  149.0 22.3 %copy-start.31 = (f32[128]{0:T(128)S(1)}, f32[128]{0:T(128)}, u32[]{:S(2)}) copy-start(f32[128]{0:T(128)} %param.17) | copy-start | bytes 1540
  163.2 32.8 %collective-permute-start.8 = (f32[128,1536]{0,1:T(8,128)}, f32[128,1536]{0,1:T(8,128)}, u32[]{:S(2)}, u32[]{:S(2)}) collective-permute-start(f32[128,1536]{0,1:T(8,128)} %bitcast_add_fusion.1), channel_id=1, source_target_pairs={{0,496},{16,0},{32,16},{48,32},{64,48},{80,64},{96,80},{112,96},{1... | collective-permute-start | bytes 2359304 | tf_op jit(solution)/shard_map/ppermute | solution.py:18
  176.0 20.0 %copy-start.2 = (f32[12,128,128]{2,1,0:T(8,128)S(1)}, f32[12,128,128]{2,1,0:T(8,128)}, u32[]{:S(2)}) copy-start(f32[12,128,128]{2,1,0:T(8,128)} %convolution_multiply_fusion) | copy-start | bytes 2359300
  180.4 128.0 %collective-permute-start.11 = (f32[128,1536]{1,0:T(8,128)S(1)}, f32[128,1536]{1,0:T(8,128)S(1)}, u32[]{:S(2)}, u32[]{:S(2)}) collective-permute-start(f32[128,1536]{1,0:T(8,128)S(1)} %add.161), channel_id=1, source_target_pairs={{0,496},{16,0},{32,16},{48,32},{64,48},{80,64},{96,80},{112,96},{1... | collective-permute-start | bytes 2359304 | tf_op jit(solution)/shard_map/ppermute | solution.py:18
  197.7 0.7 copy-start.21
  198.7 109.8 %copy-start.1 = (f32[128,1536]{1,0:T(8,128)S(1)}, f32[128,1536]{1,0:T(8,128)}, u32[]{:S(2)}) copy-start(f32[128,1536]{1,0:T(8,128)} %copy.98) | copy-start | bytes 2359300
  199.6 0.7 copy-start.32
where the time goes:
time: 311 us; the launch traced here: 309 us
  blocking collectives  107 us (34%)
  waiting for transfers between devices  81.4 us (26%)
  starting transfers between devices  64 us (21%)
  matrix products  20.2 us (6%)
  local copies, waits for them, and re-layouts  20.1 us (6%)
  other arithmetic  11.9 us (4%)
  between operations  4.57 us (1%)
    psum x1, blocking collectives, body(): gain_totals = lax.psum((query_term, key_term), ('tm', 'dp'))  107 us
    ppermute x12, waiting for transfers between devices, passed_along(): return lax.ppermute(value, axis, pairs)  81.4 us
    ppermute x12, starting transfers between devices, passed_along(): return lax.ppermute(value, axis, pairs)  64 us
    unnamed x73, local copies, waits for them, and re-layouts  9.68 us
    reshape x4, local copies, waits for them, and re-layouts, body(): value_part.reshape(flat_shape)  8.3 us
  transfers between devices with their start and end apart: 12, of which 6 were waited for; matrix products, arithmetic and copies ran while one was open for 13% of the time, Pallas kernels for 0%

commit v1 on v0

v1 whole, which is shorter than its diff:
```python
import functools

import jax
import jax.numpy as jnp
from jax import lax
from jax.experimental import pallas as pl
from jax.experimental.pallas import tpu as pltpu
from jax.sharding import PartitionSpec as P

BLK = 64
NBLK = 3
ROUTE_MOST = 2
STEPS = 4
HEADS = 12
WIDTH = 128
CAP = ROUTE_MOST * BLK
HD = HEADS * WIDTH
STAT_ROWS = 16
LOG2E = 1.4426950408889634
SCALE = WIDTH**-0.5
CLOSED = -1e30
norm_eps = 1e-06

f32 = jnp.float32
bf16 = jnp.bfloat16


def head_lanes(h):
    return pl.ds(pl.multiple_of(h * WIDTH, WIDTH), WIDTH)


def over_heads(step, unroll=2):
    lax.fori_loop(0, HEADS, lambda h, none: step(h), None, unroll=unroll)


def unit_of(raw):
    widened = raw.astype(f32)
    inverse = lax.rsqrt(jnp.mean(widened * widened, axis=-1, keepdims=True) + norm_eps)
    return widened * inverse, inverse


def three_parts(row):
    high = row.astype(bf16)
    rest = row - high.astype(f32)
    middle = rest.astype(bf16)
    low = (rest - middle.astype(f32)).astype(bf16)
    return high, middle, low


def prep_kernel(
    blocks_ref, counts_ref, reach_ref, query_ref, key_ref, log_ref, dot_ref, qgain_ref, kgain_ref,
    qx_ref, kn_ref, bias_ref,
):
    shards = counts_ref.shape[1]
    here = lax.axis_index("tm")
    lane = lax.broadcasted_iota(jnp.int32, (1, CAP), 1)

    def pair_rows(query_shard, key_shard, offset):
        rows = []
        for kj in range(ROUTE_MOST):
            values = []
            for qi in range(ROUTE_MOST):
                near = (
                    offset * NBLK
                    + blocks_ref[0, query_shard, qi]
                    - blocks_ref[0, key_shard, kj]
                    < reach_ref[0, query_shard * ROUTE_MOST + qi]
                )
                live = (qi < counts_ref[0, query_shard]) & (kj < counts_ref[0, key_shard])
                values.append(jnp.where(near & live, 0.0, CLOSED).astype(f32))
            rows.append(jnp.where(lane < BLK, values[0], values[1]))
        return rows

    rows = []
    for offset in range(STEPS):
        rows += pair_rows(here, lax.rem(here - offset + shards, shards), offset)
    for offset in range(1, STEPS):
        rows += pair_rows(lax.rem(here + offset, shards), here, offset)
    for at, row in enumerate(rows):
        bias_ref[at : at + 1, :] = row
    bias_ref[len(rows) :, :] = jnp.zeros((bias_ref.shape[0] - len(rows), CAP), f32)

    def one_head(h):
        lanes = head_lanes(h)
        unit, _ = unit_of(query_ref[:, lanes])
        qx_ref[:CAP, lanes] = (unit * qgain_ref[...]).astype(bf16)
        unit, _ = unit_of(key_ref[:, lanes])
        kn_ref[:, lanes] = (unit * kgain_ref[...]).astype(bf16)
        log_row = log_ref[pl.ds(h, 1), :] * -LOG2E
        dot_row = dot_ref[pl.ds(h, 1), :]
        parts = [p.astype(f32) for p in three_parts(log_row) + three_parts(dot_row)]
        parts.append(jnp.zeros((STAT_ROWS - len(parts), CAP), f32))
        qx_ref[CAP:, lanes] = jnp.concatenate(parts, axis=0).astype(bf16)

    over_heads(one_head)


def stat_rows(qx_ref, lanes):
    stats = qx_ref[CAP:, lanes].astype(f32)
    log_row = stats[0:1] + stats[1:2] + stats[2:3]
    dot_row = stats[3:4] + stats[4:5] + stats[5:6]
    return log_row, dot_row


def dot_nt(a, b):
    return lax.dot_general(a, b, (((1,), (1,)), ((), ())), preferred_element_type=f32)


def dot_nn(a, b):
    return lax.dot_general(a, b, (((1,), (0,)), ((), ())), preferred_element_type=f32)


def dot_tn(a, b):
    return lax.dot_general(a, b, (((0,), (0,)), ((), ())), preferred_element_type=f32)


def pair_core(qx_ref, do_ref, kn_ref, v_ref, bias_ref, at, lanes):
    log_row, dot_row = stat_rows(qx_ref, lanes)
    scores = dot_nt(kn_ref[:, lanes], qx_ref[:CAP, lanes])
    half = [
        jnp.exp2(
            scores[j * BLK : (j + 1) * BLK] * (SCALE * LOG2E)
            + (log_row + bias_ref[at + j : at + j + 1, :])
        )
        for j in range(ROUTE_MOST)
    ]
    probability = jnp.concatenate(half, axis=0)
    grad_weights = dot_nt(v_ref[:, lanes], do_ref[:, lanes])
    grad_scores = (probability * (grad_weights - dot_row)).astype(bf16)
    return probability.astype(bf16), grad_scores


def own_kernel(qx_ref, do_ref, kn_ref, v_ref, bias_ref, dq_ref, dk_ref, dv_ref):
    def one_head(h):
        lanes = head_lanes(h)
        weights, grad_scores = pair_core(qx_ref, do_ref, kn_ref, v_ref, bias_ref, 0, lanes)
        dq_ref[:, lanes] = dot_tn(grad_scores, kn_ref[:, lanes])
        dk_ref[:, lanes] = dot_nn(grad_scores, qx_ref[:CAP, lanes])
        dv_ref[:, lanes] = dot_nn(weights, do_ref[:, lanes])

    over_heads(one_head)


def step_kernel(
    offset,
    qx_ref, do_ref, kn_ref, v_ref, far_qx_ref, far_do_ref, far_kn_ref, far_v_ref, bias_ref,
    dq_in, dk_in, dv_in, dq_ref, dk_ref, dv_ref,
):
    def one_head(h):
        lanes = head_lanes(h)
        _, grad_scores = pair_core(
            qx_ref, do_ref, far_kn_ref, far_v_ref, bias_ref, offset * ROUTE_MOST, lanes
        )
        dq_ref[:, lanes] = dq_in[:, lanes] + dot_tn(grad_scores, far_kn_ref[:, lanes])
        weights, grad_scores = pair_core(
            far_qx_ref, far_do_ref, kn_ref, v_ref, bias_ref, (STEPS - 1 + offset) * ROUTE_MOST, lanes
        )
        dk_ref[:, lanes] = dk_in[:, lanes] + dot_nn(grad_scores, far_qx_ref[:CAP, lanes])
        dv_ref[:, lanes] = dv_in[:, lanes] + dot_nn(weights, far_do_ref[:, lanes])

    over_heads(one_head)


def norm_back(total, raw, gain):
    unit, inverse = unit_of(raw)
    grad_normed = total * SCALE
    scaled = grad_normed * gain
    grad_raw = inverse * (scaled - unit * jnp.mean(scaled * unit, axis=-1, keepdims=True))
    return grad_raw.astype(bf16), jnp.sum(grad_normed * unit, axis=0, keepdims=True)


def last_kernel(
    copies,
    qx_ref, do_ref, kn_ref, v_ref, far_qx_ref, far_do_ref, far_kn_ref, far_v_ref, bias_ref,
    dq_in, dk_in, dv_in, query_ref, key_ref, qgain_ref, kgain_ref,
    query_grad_ref, key_grad_ref, value_grad_ref, terms_ref,
):
    offset = STEPS - 1

    def one_head(h, terms):
        lanes = head_lanes(h)
        _, grad_scores = pair_core(
            qx_ref, do_ref, far_kn_ref, far_v_ref, bias_ref, offset * ROUTE_MOST, lanes
        )
        total = dq_in[:, lanes] + dot_tn(grad_scores, far_kn_ref[:, lanes])
        query_grad_ref[:, lanes], query_term = norm_back(total, query_ref[:, lanes], qgain_ref[...])
        weights, grad_scores = pair_core(
            far_qx_ref, far_do_ref, kn_ref, v_ref, bias_ref, (STEPS - 1 + offset) * ROUTE_MOST, lanes
        )
        total = dk_in[:, lanes] + dot_nn(grad_scores, far_qx_ref[:CAP, lanes])
        key_grad_ref[:, lanes], key_term = norm_back(total, key_ref[:, lanes], kgain_ref[...])
        total = dv_in[:, lanes] + dot_nn(weights, far_do_ref[:, lanes])
        value_grad_ref[:, lanes] = total.astype(bf16)
        return terms[0] + query_term, terms[1] + key_term

    none = jnp.zeros((1, WIDTH), f32)
    query_term, key_term = lax.fori_loop(0, HEADS, one_head, (none, none), unroll=2)
    both = jnp.concatenate([query_term, key_term], axis=0)
    terms_ref[...] = jnp.broadcast_to(both[None], (copies, 2, WIDTH))


def sum_kernel(divisor, parts_ref, out_ref):
    total = jnp.sum(parts_ref[...], axis=0)
    out_ref[...] = jnp.broadcast_to((total / divisor)[None], out_ref.shape)


VMEM = pl.BlockSpec(memory_space=pltpu.VMEM)
SMEM = pl.BlockSpec(memory_space=pltpu.SMEM)


def call(kernel, outs, specs, flops, **options):
    return pl.pallas_call(
        kernel,
        out_shape=outs,
        in_specs=specs,
        out_specs=jax.tree.map(lambda _: VMEM, outs),
        cost_estimate=pl.CostEstimate(flops=flops, bytes_accessed=1 << 20, transcendentals=0),
        compiler_params=pltpu.CompilerParams(vmem_limit_bytes=32 << 20),
        **options,
    )


def passed_along(value, steps):
    count = lax.axis_size("tm")
    pairs = [(source, (source + steps) % count) for source in range(count)]
    return lax.ppermute(value, "tm", pairs)


def body(
    query_raw, key_raw, value_rows, grad_output, log_normalizer, output_dot,
    query_gain, key_gain, route_blocks, route_count, query_reach,
):
    shards, clips = lax.axis_size("tm"), lax.axis_size("dp")
    query, key, value, grad = query_raw[0], key_raw[0], value_rows[0], grad_output[0]
    qgain, kgain = query_gain[None], key_gain[None]

    def like(rows, dtype):
        return jax.ShapeDtypeStruct((rows, HD), dtype)

    far_v, far_do = passed_along(value, 1), passed_along(grad, -1)
    qx, kn, bias = call(
        prep_kernel,
        (like(CAP + STAT_ROWS, bf16), like(CAP, bf16), jax.ShapeDtypeStruct((16, CAP), f32)),
        [SMEM] * 3 + [VMEM] * 6,
        1 << 20,
    )(route_blocks, route_count, query_reach, query, key, log_normalizer[0], output_dot[0], qgain, kgain)
    far_kn, far_qx = passed_along(kn, 1), passed_along(qx, -1)
    totals = (like(CAP, f32),) * 3
    dq, dk, dv = call(own_kernel, totals, [VMEM] * 5, 1 << 30)(qx, grad, kn, value, bias)
    for offset in range(1, STEPS):
        now = (far_qx, far_do, far_kn, far_v)
        if offset < STEPS - 1:
            far_v, far_do = passed_along(far_v, 1), passed_along(far_do, -1)
            far_kn, far_qx = passed_along(far_kn, 1), passed_along(far_qx, -1)
            dq, dk, dv = call(
                functools.partial(step_kernel, offset),
                totals,
                [VMEM] * 12,
                1 << 30,
                input_output_aliases={9: 0, 10: 1, 11: 2},
            )(qx, grad, kn, value, *now, bias, dq, dk, dv)
    query_grad, key_grad, value_grad, terms = call(
        functools.partial(last_kernel, shards),
        (like(CAP, bf16),) * 3 + (jax.ShapeDtypeStruct((shards, 2, WIDTH), f32),),
        [VMEM] * 16,
        1 << 30,
    )(qx, grad, kn, value, *now, bias, dq, dk, dv, query, key, qgain, kgain)
    parts = lax.all_to_all(terms, "tm", 0, 0)
    sums = call(
        functools.partial(sum_kernel, 1.0),
        jax.ShapeDtypeStruct((clips, 2, WIDTH), f32),
        [VMEM],
        1 << 10,
    )(parts)
    parts = lax.all_to_all(sums, "dp", 0, 0)
    sums = jnp.sum(parts, axis=0) / (shards * clips)
    return (query_grad[None], key_grad[None], value_grad[None], sums[0], sums[1])


def solution(mesh):
    rows = P("dp", "tm", None)
    stats = P("dp", None, "tm")
    return jax.shard_map(
        body,
        mesh=mesh,
        in_specs=(
            rows, rows, rows, rows, stats, stats, P(), P(),
            P("dp", None, None), P("dp", None), P("dp", None),
        ),
        out_specs=(rows, rows, rows, P(), P()),
        check_vma=False,
    )
```

time: 311 us -> 126 us (0.41)
  blocking collectives: 107 us -> 32.8 us
  waiting for transfers between devices: 81.4 us -> 7.62 us
  Pallas kernels: 0 us -> 23 us
  matrix products: 20.2 us -> 0 us
  local copies, waits for them, and re-layouts: 20.1 us -> 3.99 us
  other arithmetic: 11.9 us -> 0.03 us
  starting transfers between devices: 64 us -> 56.9 us
  between operations: 4.57 us -> 0.95 us
    psum x1 -> x0, blocking collectives: 107 us -> none  [body(): gain_totals = lax.psum((query_term, key_term), ('tm', 'dp'))]
    ppermute x12, waiting for transfers between devices: 81.4 us -> 7.62 us  [passed_along(): return lax.ppermute(value, 'tm', pairs)]
    all_to_all x0 -> x2, blocking collectives: none -> 32.8 us  [the longest x1 20.8 us: body(): parts = lax.all_to_all(sums, 'dp', 0, 0)]
    pallas_call x0 -> x6, Pallas kernels: none -> 23 us  [the longest x2 10.6 us: body(): call(functools.partial(step_kernel, offset), totals, [VMEM] * 12, 1 << 30...]
    dot_general x20 -> x0, matrix products: 20.2 us -> none  [the longest x4 5.11 us: pair_terms(): jnp.einsum('hqk,khd->qhd', grad_scores, key_normed, preferred_element_typ...]
    reshape x4 -> x0, local copies, waits for them, and re-layouts: 8.3 us -> none  [body(): value_part.reshape(flat_shape)]
    ppermute x12, starting transfers between devices: 64 us -> 56.9 us  [passed_along(): return lax.ppermute(value, 'tm', pairs)]
    unnamed x73 -> x26, local copies, waits for them, and re-layouts: 9.68 us -> 3.47 us
  transfers between devices with their start and end apart: 12 -> 12, of which waited for: 6 -> 2; matrix products, arithmetic and copies ran while one was open for 13% -> 0% of each run, Pallas kernels for 0% -> 11%
where the time goes in v1:
time: 126 us; the launch traced here: 125 us
  starting transfers between devices  56.9 us (45%)
  blocking collectives  32.8 us (26%)
  Pallas kernels  23 us (18%)
  waiting for transfers between devices  7.62 us (6%)
  local copies, waits for them, and re-layouts  3.99 us (3%)
    ppermute x12, starting transfers between devices, passed_along(): return lax.ppermute(value, 'tm', pairs)  56.9 us
    all_to_all x1, blocking collectives, body(): parts = lax.all_to_all(sums, 'dp', 0, 0)  20.8 us
    all_to_all x1, blocking collectives, body(): parts = lax.all_to_all(terms, 'tm', 0, 0)  12 us
    pallas_call x2, Pallas kernels, body(): call(functools.partial(step_kernel, offset), totals, [VMEM] * 12, 1 << 30...  10.6 us
    ppermute x12, waiting for transfers between devices, passed_along(): return lax.ppermute(value, 'tm', pairs)  7.62 us
    pallas_call x1, Pallas kernels, body(): call(functools.partial(last_kernel, shards), (like(CAP, bf16),) * 3 + (ja...  6.87 us
    pallas_call x1, Pallas kernels, body(): call(own_kernel, totals, [VMEM] * 5, 1 << 30)(qx, grad, kn, value, bias)  3.62 us
    unnamed x26, local copies, waits for them, and re-layouts  3.47 us
  transfers between devices with their start and end apart: 12, of which 2 were waited for; matrix products, arithmetic and copies ran while one was open for 0% of the time, Pallas kernels for 11%

profile of v1, /device:TPU:1, one launch (start us, length us, event | category | flops | bytes accessed | tf_op | source)
XLA Modules:
  0.0 125.2 jit_solution(7612078130297875566)
XLA Ops:
  0.7 0.8 copy.22.blocks_ref
  1.4 0.0 copy-done.11
  1.4 0.0 copy-start.9
  1.5 0.0 copy-start.6
  1.5 0.0 copy-start.7
  1.5 0.0 copy-start.8
  1.5 0.6 copy-done.9
  2.1 0.0 copy-done.6
  2.1 0.0 copy-done.7
  2.1 0.0 copy-done.8
  2.1 1.0 copy-done.2
  3.1 1.0 copy-done.4
  4.1 1.9 %shard_map.146 = (bf16[144,1536]{1,0:T(8,128)(2,1)S(1)}, bf16[128,1536]{1,0:T(8,128)(2,1)S(1)}, f32[16,128]{1,0:T(8,128)S(1)}) custom-call(s32[1,32,2]{2,1,0:T(8,128)S(1)} %copy.22.blocks_ref, s32[1,32]{1,0:T(1,128)S(1)} %copy-done.8, s32[1,64]{1,0:T(1,128)S(1)} %copy-done.9, bf16[128,1536]{1,0:T(8,128)(2,1)S(1)} %bitcast.27, ...), custom_call_target="tpu_custom_call" | custom-call | flops 1048576 | bytes 1048576 | tf_op jit(solution)/shard_map/pallas_call | solution.py:241
  6.0 14.5 %collective-permute-start = (bf16[144,1536]{1,0:T(8,128)(2,1)S(1)}, bf16[144,1536]{1,0:T(8,128)(2,1)S(1)}, u32[]{:S(2)}, u32[]{:S(2)}) collective-permute-start(bf16[144,1536]{1,0:T(8,128)(2,1)S(1)} %get-tuple-element.21.qx_ref), channel_id=1, source_target_pairs={{0,496},{16,0},{32,16},{48,32},{64,48},{80,64},{96,80},{112,96},{1... | collective-permute-start | bytes 1327112 | tf_op jit(solution)/shard_map/ppermute | solution.py:226
  20.5 1.9 %collective-permute-start.6 = (bf16[128,1536]{1,0:T(8,128)(2,1)S(1)}, bf16[128,1536]{1,0:T(8,128)(2,1)S(1)}, u32[]{:S(2)}, u32[]{:S(2)}) collective-permute-start(bf16[128,1536]{1,0:T(8,128)(2,1)S(1)} %get-tuple-element.22.kn_ref), channel_id=1, source_target_pairs={{0,16},{16,32},{32,48},{48,64},{64,80},{80,96},{96,112},{112,128},... | collective-permute-start | bytes 1179656 | tf_op jit(solution)/shard_map/ppermute | solution.py:226
  22.5 0.0 copy-done.1
  22.5 1.9 %collective-permute-start.9 = (bf16[128,1536]{1,0:T(8,128)(2,1)S(1)}, bf16[128,1536]{1,0:T(8,128)(2,1)S(1)}, u32[]{:S(2)}, u32[]{:S(2)}) collective-permute-start(bf16[128,1536]{1,0:T(8,128)(2,1)S(1)} %bitcast.22), channel_id=1, source_target_pairs={{0,16},{16,32},{32,48},{48,64},{64,80},{80,96},{96,112},{112,128},... | collective-permute-start | bytes 1179656 | tf_op jit(solution)/shard_map/ppermute | solution.py:226
  24.4 0.0 copy-done
  24.4 7.3 %collective-permute-start.3 = (bf16[128,1536]{1,0:T(8,128)(2,1)S(1)}, bf16[128,1536]{1,0:T(8,128)(2,1)S(1)}, u32[]{:S(2)}, u32[]{:S(2)}) collective-permute-start(bf16[128,1536]{1,0:T(8,128)(2,1)S(1)} %bitcast.17), channel_id=1, source_target_pairs={{0,496},{16,0},{32,16},{48,32},{64,48},{80,64},{96,80},{112,96},{1... | collective-permute-start | bytes 1179656 | tf_op jit(solution)/shard_map/ppermute | solution.py:226
  31.7 0.0 collective-permute-done.far_qx_ref
  31.7 5.7 %collective-permute-start.1 = (bf16[144,1536]{1,0:T(8,128)(2,1)S(1)}, bf16[144,1536]{1,0:T(8,128)(2,1)S(1)}, u32[]{:S(2)}, u32[]{:S(2)}) collective-permute-start(bf16[144,1536]{1,0:T(8,128)(2,1)S(1)} %collective-permute-done.far_qx_ref), channel_id=1, source_target_pairs={{0,496},{16,0},{32,16},{48,32},{64,48},{80,64},{96,80},{112,96},{1... | collective-permute-start | bytes 1327112 | tf_op jit(solution)/shard_map/ppermute | solution.py:226
  37.4 0.0 collective-permute-done.6.far_kn_ref
  37.4 1.9 %collective-permute-start.7 = (bf16[128,1536]{1,0:T(8,128)(2,1)S(1)}, bf16[128,1536]{1,0:T(8,128)(2,1)S(1)}, u32[]{:S(2)}, u32[]{:S(2)}) collective-permute-start(bf16[128,1536]{1,0:T(8,128)(2,1)S(1)} %collective-permute-done.6.far_kn_ref), channel_id=1, source_target_pairs={{0,16},{16,32},{32,48},{48,64},{64,80},{80,96},{96,112},{112,128},... | collective-permute-start | bytes 1179656 | tf_op jit(solution)/shard_map/ppermute | solution.py:226
  39.3 5.1 %collective-permute-done.9.far_v_ref = bf16[128,1536]{1,0:T(8,128)(2,1)S(1)} collective-permute-done((bf16[128,1536]{1,0:T(8,128)(2,1)S(1)}, bf16[128,1536]{1,0:T(8,128)(2,1)S(1)}, u32[]{:S(2)}, u32[]{:S(2)}) %collective-permute-start.9) | collective-permute-done | bytes 393248 | tf_op jit(solution)/shard_map/ppermute | solution.py:226
  44.4 1.9 %collective-permute-start.10 = (bf16[128,1536]{1,0:T(8,128)(2,1)S(1)}, bf16[128,1536]{1,0:T(8,128)(2,1)S(1)}, u32[]{:S(2)}, u32[]{:S(2)}) collective-permute-start(bf16[128,1536]{1,0:T(8,128)(2,1)S(1)} %collective-permute-done.9.far_v_ref), channel_id=1, source_target_pairs={{0,16},{16,32},{32,48},{48,64},{64,80},{80,96},{96,112},{112,128},... | collective-permute-start | bytes 1179656 | tf_op jit(solution)/shard_map/ppermute | solution.py:226
  46.4 0.0 collective-permute-done.3.far_do_ref
  46.4 7.3 %collective-permute-start.4 = (bf16[128,1536]{1,0:T(8,128)(2,1)S(1)}, bf16[128,1536]{1,0:T(8,128)(2,1)S(1)}, u32[]{:S(2)}, u32[]{:S(2)}) collective-permute-start(bf16[128,1536]{1,0:T(8,128)(2,1)S(1)} %collective-permute-done.3.far_do_ref), channel_id=1, source_target_pairs={{0,496},{16,0},{32,16},{48,32},{64,48},{80,64},{96,80},{112,96},{1... | collective-permute-start | bytes 1179656 | tf_op jit(solution)/shard_map/ppermute | solution.py:226
  53.6 0.0 collective-permute-done.1.far_qx_ref
  53.7 2.7 %collective-permute-start.2 = (bf16[144,1536]{1,0:T(8,128)(2,1)S(1)}, bf16[144,1536]{1,0:T(8,128)(2,1)S(1)}, u32[]{:S(2)}, u32[]{:S(2)}) collective-permute-start(bf16[144,1536]{1,0:T(8,128)(2,1)S(1)} %collective-permute-done.1.far_qx_ref), channel_id=1, source_target_pairs={{0,496},{16,0},{32,16},{48,32},{64,48},{80,64},{96,80},{112,96},{1... | collective-permute-start | bytes 1327112 | tf_op jit(solution)/shard_map/ppermute | solution.py:226
  56.3 0.0 collective-permute-done.7.far_kn_ref
  56.3 2.6 %collective-permute-start.8 = (bf16[128,1536]{1,0:T(8,128)(2,1)S(1)}, bf16[128,1536]{1,0:T(8,128)(2,1)S(1)}, u32[]{:S(2)}, u32[]{:S(2)}) collective-permute-start(bf16[128,1536]{1,0:T(8,128)(2,1)S(1)} %collective-permute-done.7.far_kn_ref), channel_id=1, source_target_pairs={{0,16},{16,32},{32,48},{48,64},{64,80},{80,96},{96,112},{112,128},... | collective-permute-start | bytes 1179656 | tf_op jit(solution)/shard_map/ppermute | solution.py:226
  59.0 2.5 %collective-permute-done.10.far_v_ref = bf16[128,1536]{1,0:T(8,128)(2,1)S(1)} collective-permute-done((bf16[128,1536]{1,0:T(8,128)(2,1)S(1)}, bf16[128,1536]{1,0:T(8,128)(2,1)S(1)}, u32[]{:S(2)}, u32[]{:S(2)}) %collective-permute-start.10) | collective-permute-done | bytes 393248 | tf_op jit(solution)/shard_map/ppermute | solution.py:226
  61.4 1.9 %collective-permute-start.11 = (bf16[128,1536]{1,0:T(8,128)(2,1)S(1)}, bf16[128,1536]{1,0:T(8,128)(2,1)S(1)}, u32[]{:S(2)}, u32[]{:S(2)}) collective-permute-start(bf16[128,1536]{1,0:T(8,128)(2,1)S(1)} %collective-permute-done.10.far_v_ref), channel_id=1, source_target_pairs={{0,16},{16,32},{32,48},{48,64},{64,80},{80,96},{96,112},{112,128},... | collective-permute-start | bytes 1179656 | tf_op jit(solution)/shard_map/ppermute | solution.py:226
  63.3 0.0 collective-permute-done.4.far_do_ref
  63.4 7.3 %collective-permute-start.5 = (bf16[128,1536]{1,0:T(8,128)(2,1)S(1)}, bf16[128,1536]{1,0:T(8,128)(2,1)S(1)}, u32[]{:S(2)}, u32[]{:S(2)}) collective-permute-start(bf16[128,1536]{1,0:T(8,128)(2,1)S(1)} %collective-permute-done.4.far_do_ref), channel_id=1, source_target_pairs={{0,496},{16,0},{32,16},{48,32},{64,48},{80,64},{96,80},{112,96},{1... | collective-permute-start | bytes 1179656 | tf_op jit(solution)/shard_map/ppermute | solution.py:226
  70.6 3.6 %shard_map.147 = (f32[128,1536]{1,0:T(8,128)S(1)}, f32[128,1536]{1,0:T(8,128)S(1)}, f32[128,1536]{1,0:T(8,128)S(1)}) custom-call(bf16[144,1536]{1,0:T(8,128)(2,1)S(1)} %get-tuple-element.21.qx_ref, bf16[128,1536]{1,0:T(8,128)(2,1)S(1)} %bitcast.18, bf16[128,1536]{1,0:T(8,128)(2,1)S(1)} %get-tuple-element.22.kn_ref, bf16[128,1536]{1,0:T(8,128)(2,1)S(1)} %bitcast.23, ...), custom_call_target="tpu_custom_call" | custom-call | flops 1073741824 | bytes 1048576 | tf_op jit(solution)/shard_map/pallas_call | solution.py:249
  74.3 5.3 %shard_map.148 = (f32[128,1536]{1,0:T(8,128)S(1)}, f32[128,1536]{1,0:T(8,128)S(1)}, f32[128,1536]{1,0:T(8,128)S(1)}) custom-call(bf16[144,1536]{1,0:T(8,128)(2,1)S(1)} %get-tuple-element.21.qx_ref, bf16[128,1536]{1,0:T(8,128)(2,1)S(1)} %bitcast.19, ...), custom_call_target="tpu_custom_call", output_to_operand_aliasing={{0}: (9, {}), {1}: (10, {}), {2}: (11, {})} | custom-call | flops 1073741824 | bytes 1048576 | tf_op jit(solution)/shard_map/pallas_call | solution.py:255
  79.6 0.0 copy-start.3
  79.6 0.0 copy-start.5
  79.6 5.3 %shard_map.149 = (f32[128,1536]{1,0:T(8,128)S(1)}, f32[128,1536]{1,0:T(8,128)S(1)}, f32[128,1536]{1,0:T(8,128)S(1)}) custom-call(bf16[144,1536]{1,0:T(8,128)(2,1)S(1)} %get-tuple-element.21.qx_ref, bf16[128,1536]{1,0:T(8,128)(2,1)S(1)} %bitcast.20, ...), custom_call_target="tpu_custom_call", output_to_operand_aliasing={{0}: (9, {}), {1}: (10, {}), {2}: (11, {})} | custom-call | flops 1073741824 | bytes 1048576 | tf_op jit(solution)/shard_map/pallas_call | solution.py:255
  84.9 0.0 collective-permute-done.8.far_kn_ref
  84.9 0.0 collective-permute-done.11.far_v_ref
  84.9 0.0 collective-permute-done.5.far_do_ref
  84.9 0.0 collective-permute-done.2.far_qx_ref
  84.9 6.9 %shard_map.150 = (bf16[128,1536]{1,0:T(8,128)(2,1)}, bf16[128,1536]{1,0:T(8,128)(2,1)}, bf16[128,1536]{1,0:T(8,128)(2,1)}, f32[32,2,128]{2,1,0:T(2,128)S(1)}) custom-call(bf16[144,1536]{1,0:T(8,128)(2,1)S(1)} %get-tuple-element.21.qx_ref, bf16[128,1536]{1,0:T(8,128)(2,1)S(1)} %bitcast.21, bf16[128,1536]{1,0:T(8,128)(2,1)S(1)} %get-tuple-element.22.kn_ref, ...), custom_call_target="tpu_custom_call" | custom-call | flops 1073741824 | bytes 1048576 | tf_op jit(solution)/shard_map/pallas_call | solution.py:262
  91.8 12.0 %all_to_all.10.parts_ref = f32[32,2,128]{2,1,0:T(2,128)S(1)} all-to-all(f32[32,2,128]{2,1,0:T(2,128)S(1)} %get-tuple-element.36), channel_id=1, replica_groups=mesh['tm'=32,'dp'=16] {'tm'}, dimensions={0} | all-to-all | bytes 65536 | tf_op jit(solution)/shard_map/all_to_all | solution.py:268
  103.9 20.8 %all_to_all.11 = f32[16,2,128]{2,1,0:T(2,128)S(1)} all-to-all(f32[16,2,128]{2,1,0:T(2,128)S(1)} %shard_map.151), channel_id=1, replica_groups=mesh['tm'=32,'dp'=16] {'dp'}, dimensions={0} | all-to-all | bytes 32768 | tf_op jit(solution)/shard_map/all_to_all | solution.py:275
  124.7 0.5 slice_bitcast_fusion
  (13 shorter events, 0.1 us)
Async XLA Ops:
  0.6 0.8 copy-start.11
  0.6 0.8 copy-start.10
  1.4 0.7 copy-start.9
  1.5 0.7 copy-start.6
  1.5 0.7 copy-start.7
  1.5 0.7 copy-start.8
  2.1 1.0 copy-start.2
  3.1 1.0 copy-start.4
  4.1 18.3 %copy-start.1 = (bf16[1,128,1536]{2,1,0:T(8,128)(2,1)S(1)}, bf16[1,128,1536]{2,1,0:T(8,128)(2,1)}, u32[]{:S(2)}) copy-start(bf16[1,128,1536]{2,1,0:T(8,128)(2,1)} %param.13) | copy-start | bytes 1179652
  4.1 20.3 %copy-start = (bf16[1,128,1536]{2,1,0:T(8,128)(2,1)S(1)}, bf16[1,128,1536]{2,1,0:T(8,128)(2,1)}, u32[]{:S(2)}) copy-start(bf16[1,128,1536]{2,1,0:T(8,128)(2,1)} %param.14) | copy-start | bytes 1179652
  6.0 25.7 %collective-permute-start = (bf16[144,1536]{1,0:T(8,128)(2,1)S(1)}, bf16[144,1536]{1,0:T(8,128)(2,1)S(1)}, u32[]{:S(2)}, u32[]{:S(2)}) collective-permute-start(bf16[144,1536]{1,0:T(8,128)(2,1)S(1)} %get-tuple-element.21.qx_ref), channel_id=1, source_target_pairs={{0,496},{16,0},{32,16},{48,32},{64,48},{80,64},{96,80},{112,96},{1... | collective-permute-start | bytes 1327112 | tf_op jit(solution)/shard_map/ppermute | solution.py:226
  20.5 16.8 %collective-permute-start.6 = (bf16[128,1536]{1,0:T(8,128)(2,1)S(1)}, bf16[128,1536]{1,0:T(8,128)(2,1)S(1)}, u32[]{:S(2)}, u32[]{:S(2)}) collective-permute-start(bf16[128,1536]{1,0:T(8,128)(2,1)S(1)} %get-tuple-element.22.kn_ref), channel_id=1, source_target_pairs={{0,16},{16,32},{32,48},{48,64},{64,80},{80,96},{96,112},{112,128},... | collective-permute-start | bytes 1179656 | tf_op jit(solution)/shard_map/ppermute | solution.py:226
  22.5 22.0 %collective-permute-start.9 = (bf16[128,1536]{1,0:T(8,128)(2,1)S(1)}, bf16[128,1536]{1,0:T(8,128)(2,1)S(1)}, u32[]{:S(2)}, u32[]{:S(2)}) collective-permute-start(bf16[128,1536]{1,0:T(8,128)(2,1)S(1)} %bitcast.22), channel_id=1, source_target_pairs={{0,16},{16,32},{32,48},{48,64},{64,80},{80,96},{96,112},{112,128},... | collective-permute-start | bytes 1179656 | tf_op jit(solution)/shard_map/ppermute | solution.py:226
  24.4 21.9 %collective-permute-start.3 = (bf16[128,1536]{1,0:T(8,128)(2,1)S(1)}, bf16[128,1536]{1,0:T(8,128)(2,1)S(1)}, u32[]{:S(2)}, u32[]{:S(2)}) collective-permute-start(bf16[128,1536]{1,0:T(8,128)(2,1)S(1)} %bitcast.17), channel_id=1, source_target_pairs={{0,496},{16,0},{32,16},{48,32},{64,48},{80,64},{96,80},{112,96},{1... | collective-permute-start | bytes 1179656 | tf_op jit(solution)/shard_map/ppermute | solution.py:226
  31.7 21.9 %collective-permute-start.1 = (bf16[144,1536]{1,0:T(8,128)(2,1)S(1)}, bf16[144,1536]{1,0:T(8,128)(2,1)S(1)}, u32[]{:S(2)}, u32[]{:S(2)}) collective-permute-start(bf16[144,1536]{1,0:T(8,128)(2,1)S(1)} %collective-permute-done.far_qx_ref), channel_id=1, source_target_pairs={{0,496},{16,0},{32,16},{48,32},{64,48},{80,64},{96,80},{112,96},{1... | collective-permute-start | bytes 1327112 | tf_op jit(solution)/shard_map/ppermute | solution.py:226
  37.4 19.0 %collective-permute-start.7 = (bf16[128,1536]{1,0:T(8,128)(2,1)S(1)}, bf16[128,1536]{1,0:T(8,128)(2,1)S(1)}, u32[]{:S(2)}, u32[]{:S(2)}) collective-permute-start(bf16[128,1536]{1,0:T(8,128)(2,1)S(1)} %collective-permute-done.6.far_kn_ref), channel_id=1, source_target_pairs={{0,16},{16,32},{32,48},{48,64},{64,80},{80,96},{96,112},{112,128},... | collective-permute-start | bytes 1179656 | tf_op jit(solution)/shard_map/ppermute | solution.py:226
  44.4 17.0 %collective-permute-start.10 = (bf16[128,1536]{1,0:T(8,128)(2,1)S(1)}, bf16[128,1536]{1,0:T(8,128)(2,1)S(1)}, u32[]{:S(2)}, u32[]{:S(2)}) collective-permute-start(bf16[128,1536]{1,0:T(8,128)(2,1)S(1)} %collective-permute-done.9.far_v_ref), channel_id=1, source_target_pairs={{0,16},{16,32},{32,48},{48,64},{64,80},{80,96},{96,112},{112,128},... | collective-permute-start | bytes 1179656 | tf_op jit(solution)/shard_map/ppermute | solution.py:226
  46.4 17.0 %collective-permute-start.4 = (bf16[128,1536]{1,0:T(8,128)(2,1)S(1)}, bf16[128,1536]{1,0:T(8,128)(2,1)S(1)}, u32[]{:S(2)}, u32[]{:S(2)}) collective-permute-start(bf16[128,1536]{1,0:T(8,128)(2,1)S(1)} %collective-permute-done.3.far_do_ref), channel_id=1, source_target_pairs={{0,496},{16,0},{32,16},{48,32},{64,48},{80,64},{96,80},{112,96},{1... | collective-permute-start | bytes 1179656 | tf_op jit(solution)/shard_map/ppermute | solution.py:226
  53.7 31.3 %collective-permute-start.2 = (bf16[144,1536]{1,0:T(8,128)(2,1)S(1)}, bf16[144,1536]{1,0:T(8,128)(2,1)S(1)}, u32[]{:S(2)}, u32[]{:S(2)}) collective-permute-start(bf16[144,1536]{1,0:T(8,128)(2,1)S(1)} %collective-permute-done.1.far_qx_ref), channel_id=1, source_target_pairs={{0,496},{16,0},{32,16},{48,32},{64,48},{80,64},{96,80},{112,96},{1... | collective-permute-start | bytes 1327112 | tf_op jit(solution)/shard_map/ppermute | solution.py:226
  56.3 28.5 %collective-permute-start.8 = (bf16[128,1536]{1,0:T(8,128)(2,1)S(1)}, bf16[128,1536]{1,0:T(8,128)(2,1)S(1)}, u32[]{:S(2)}, u32[]{:S(2)}) collective-permute-start(bf16[128,1536]{1,0:T(8,128)(2,1)S(1)} %collective-permute-done.7.far_kn_ref), channel_id=1, source_target_pairs={{0,16},{16,32},{32,48},{48,64},{64,80},{80,96},{96,112},{112,128},... | collective-permute-start | bytes 1179656 | tf_op jit(solution)/shard_map/ppermute | solution.py:226
  61.4 23.5 %collective-permute-start.11 = (bf16[128,1536]{1,0:T(8,128)(2,1)S(1)}, bf16[128,1536]{1,0:T(8,128)(2,1)S(1)}, u32[]{:S(2)}, u32[]{:S(2)}) collective-permute-start(bf16[128,1536]{1,0:T(8,128)(2,1)S(1)} %collective-permute-done.10.far_v_ref), channel_id=1, source_target_pairs={{0,16},{16,32},{32,48},{48,64},{64,80},{80,96},{96,112},{112,128},... | collective-permute-start | bytes 1179656 | tf_op jit(solution)/shard_map/ppermute | solution.py:226
  63.4 21.6 %collective-permute-start.5 = (bf16[128,1536]{1,0:T(8,128)(2,1)S(1)}, bf16[128,1536]{1,0:T(8,128)(2,1)S(1)}, u32[]{:S(2)}, u32[]{:S(2)}) collective-permute-start(bf16[128,1536]{1,0:T(8,128)(2,1)S(1)} %collective-permute-done.4.far_do_ref), channel_id=1, source_target_pairs={{0,496},{16,0},{32,16},{48,32},{64,48},{80,64},{96,80},{112,96},{1... | collective-permute-start | bytes 1179656 | tf_op jit(solution)/shard_map/ppermute | solution.py:226
  79.6 5.4 %copy-start.3 = (bf16[1,128,1536]{2,1,0:T(8,128)(2,1)S(1)}, bf16[1,128,1536]{2,1,0:T(8,128)(2,1)}, u32[]{:S(2)}) copy-start(bf16[1,128,1536]{2,1,0:T(8,128)(2,1)} %param.11) | copy-start | bytes 1179652
  79.6 5.4 %copy-start.5 = (bf16[1,128,1536]{2,1,0:T(8,128)(2,1)S(1)}, bf16[1,128,1536]{2,1,0:T(8,128)(2,1)}, u32[]{:S(2)}) copy-start(bf16[1,128,1536]{2,1,0:T(8,128)(2,1)} %param.12) | copy-start | bytes 1179652

commit v2 on v1

v2 whole, which is shorter than its diff:
```python
import functools

import jax
import jax.numpy as jnp
from jax import lax
from jax.experimental import pallas as pl
from jax.experimental.pallas import tpu as pltpu
from jax.sharding import PartitionSpec as P

BLK = 64
NBLK = 3
ROUTE_MOST = 2
STEPS = 4
HEADS = 12
WIDTH = 128
CAP = ROUTE_MOST * BLK
HD = HEADS * WIDTH
STAT_ROWS = 16
ROWS = 2 * CAP + STAT_ROWS
FIRST, SECOND, STATS = slice(0, CAP), slice(CAP, 2 * CAP), slice(2 * CAP, ROWS)
LOG2E = 1.4426950408889634
SCALE = WIDTH**-0.5
CLOSED = -1e30
norm_eps = 1e-06

f32 = jnp.float32
bf16 = jnp.bfloat16


def head_lanes(h):
    return pl.ds(pl.multiple_of(h * WIDTH, WIDTH), WIDTH)


def over_heads(step, unroll=3):
    lax.fori_loop(0, HEADS, lambda h, none: step(h), None, unroll=unroll)


def by_parity(run, *chains):
    odd = lax.rem(lax.axis_index("tm"), 2)
    for parity in range(2):
        refs = []
        for a, b, hop in chains:
            refs += [a, b] if (parity + hop) % 2 == 0 else [b, a]

        @pl.when(odd == parity)
        def _():
            run(*refs)


def unit_of(raw):
    widened = raw.astype(f32)
    inverse = lax.rsqrt(jnp.mean(widened * widened, axis=-1, keepdims=True) + norm_eps)
    return widened * inverse, inverse


def three_parts(row):
    high = row.astype(bf16)
    rest = row - high.astype(f32)
    middle = rest.astype(bf16)
    low = (rest - middle.astype(f32)).astype(bf16)
    return high, middle, low


def prep_kernel(
    query_hbm, key_hbm, value_hbm, grad_hbm, log_hbm, dot_hbm, qgain_hbm, kgain_hbm,
    a_ref, b_ref,
    *scratch,
):
    by_parity(
        lambda up_ref, down_ref: prepare(
            query_hbm, key_hbm, value_hbm, grad_hbm, log_hbm, dot_hbm, qgain_hbm, kgain_hbm,
            up_ref, down_ref,
            *scratch,
        ),
        (a_ref, b_ref, 0),
    )


def prepare(
    query_hbm, key_hbm, value_hbm, grad_hbm, log_hbm, dot_hbm, qgain_hbm, kgain_hbm,
    up_ref, down_ref,
    query_ref, key_ref, log_ref, dot_ref, qgain_ref, kgain_ref, sems,
):
    moves = [
        pltpu.make_async_copy(source, target, sems.at[i])
        for i, (source, target) in enumerate(
            [
                (query_hbm.at[0], query_ref),
                (log_hbm, log_ref),
                (dot_hbm, dot_ref),
                (qgain_hbm, qgain_ref),
                (kgain_hbm, kgain_ref),
                (key_hbm.at[0], key_ref),
                (grad_hbm.at[0], down_ref.at[SECOND]),
                (value_hbm.at[0], up_ref.at[SECOND]),
            ]
        )
    ]
    for move in moves:
        move.start()
    for move in moves[:6]:
        move.wait()

    def one_head(h):
        lanes = head_lanes(h)
        unit, _ = unit_of(query_ref[:, lanes])
        down_ref[FIRST, lanes] = (unit * qgain_ref[...]).astype(bf16)
        unit, _ = unit_of(key_ref[:, lanes])
        up_ref[FIRST, lanes] = (unit * kgain_ref[...]).astype(bf16)
        parts = [
            p.astype(f32) for p in three_parts(log_ref[h] * -LOG2E) + three_parts(dot_ref[h])
        ]
        parts.append(jnp.zeros((STAT_ROWS - len(parts), CAP), f32))
        down_ref[STATS, lanes] = jnp.concatenate(parts, axis=0).astype(bf16)
        up_ref[STATS, lanes] = jnp.zeros((STAT_ROWS, CAP), bf16)

    over_heads(one_head)
    for move in moves[6:]:
        move.wait()


def stat_rows(down_ref, lanes):
    stats = down_ref[STATS, lanes].astype(f32)
    return stats[0:1] + stats[1:2] + stats[2:3], stats[3:4] + stats[4:5] + stats[5:6]


def dot_nt(a, b):
    return lax.dot_general(a, b, (((1,), (1,)), ((), ())), preferred_element_type=f32)


def dot_nn(a, b):
    return lax.dot_general(a, b, (((1,), (0,)), ((), ())), preferred_element_type=f32)


def dot_tn(a, b):
    return lax.dot_general(a, b, (((0,), (0,)), ((), ())), preferred_element_type=f32)


def side_by_side(parts, axis):
    return parts[0] if len(parts) == 1 else jnp.concatenate(parts, axis=axis)


def pair_core(up_ref, downs, lanes):
    logs, dots = zip(*(stat_rows(ref, lanes) for ref, _ in downs))
    queries = side_by_side([ref[FIRST, lanes] for ref, _ in downs], 0)
    cotangents = side_by_side([ref[SECOND, lanes] for ref, _ in downs], 0)
    scores = dot_nt(up_ref[FIRST, lanes], queries)
    half = []
    for j in range(ROUTE_MOST):
        row = side_by_side([log + bias[j : j + 1] for log, (_, bias) in zip(logs, downs)], 1)
        half.append(jnp.exp2(scores[j * BLK : (j + 1) * BLK] * (SCALE * LOG2E) + row))
    probability = jnp.concatenate(half, axis=0)
    grad_weights = dot_nt(up_ref[SECOND, lanes], cotangents)
    grad_scores = (probability * (grad_weights - side_by_side(dots, 1))).astype(bf16)
    return probability.astype(bf16), grad_scores, queries, cotangents


def rows_for_query(bias_ref, offset):
    return bias_ref[offset * ROUTE_MOST : (offset + 1) * ROUTE_MOST, :]


def rows_for_key(bias_ref, offset):
    return rows_for_query(bias_ref, STEPS - 1 + offset)


def rows_between(bias_ref):
    return rows_for_query(bias_ref, 2 * STEPS - 1)


def fill_bias(blocks_ref, counts_ref, reach_ref, bias_ref):
    shards = counts_ref.shape[1]
    here = lax.axis_index("tm")
    lane = lax.broadcasted_iota(jnp.int32, (1, CAP), 1)

    def pair_rows(query_shard, key_shard, offset):
        rows = []
        for kj in range(ROUTE_MOST):
            values = []
            for qi in range(ROUTE_MOST):
                near = (
                    offset * NBLK
                    + blocks_ref[0, qi, query_shard]
                    - blocks_ref[0, kj, key_shard]
                    < reach_ref[0, query_shard * ROUTE_MOST + qi]
                )
                live = (qi < counts_ref[0, query_shard]) & (kj < counts_ref[0, key_shard])
                values.append(jnp.where(near & live, 0.0, CLOSED).astype(f32))
            rows.append(jnp.where(lane < BLK, values[0], values[1]))
        return rows

    rows = []
    for offset in range(STEPS):
        rows += pair_rows(here, lax.rem(here - offset + shards, shards), offset)
    for offset in range(1, STEPS):
        rows += pair_rows(lax.rem(here + offset, shards), here, offset)
    rows += pair_rows(lax.rem(here + 1, shards), lax.rem(here - 2 + shards, shards), STEPS - 1)
    for at, row in enumerate(rows):
        bias_ref[at : at + 1, :] = row


def own_kernel(
    blocks_ref, counts_ref, reach_ref, a_ref, b_ref, query_ref, key_ref,
    dq_ref, dk_ref, dv_ref, bias_ref, query_unit_ref, query_inverse_ref, key_unit_ref, key_inverse_ref,
):
    fill_bias(blocks_ref, counts_ref, reach_ref, bias_ref)

    def run(up_ref, down_ref):
        def one_head(h):
            lanes = head_lanes(h)
            weights, grad_scores, queries, cotangents = pair_core(
                up_ref, [(down_ref, rows_for_query(bias_ref, 0))], lanes
            )
            dq_ref[:, lanes] = dot_tn(grad_scores, up_ref[FIRST, lanes])
            dk_ref[:, lanes] = dot_nn(grad_scores, queries)
            dv_ref[:, lanes] = dot_nn(weights, cotangents)
            for raw_ref, unit_ref, inverse_ref in (
                (query_ref, query_unit_ref, query_inverse_ref),
                (key_ref, key_unit_ref, key_inverse_ref),
            ):
                unit, inverse = unit_of(raw_ref[0, :, lanes])
                unit_ref[:, lanes] = unit
                inverse_ref[:, lanes] = jnp.broadcast_to(inverse, unit.shape)

        over_heads(one_head)

    by_parity(run, (a_ref, b_ref, 0))


def step_kernel(
    a_ref, b_ref, a1_ref, b1_ref, bias_ref, dq_in, dk_in, dv_in, dq_ref, dk_ref, dv_ref, token_ref
):
    def run(up_ref, down_ref, up1_ref, down1_ref):
        def one_head(h):
            lanes = head_lanes(h)
            _, grad_scores, _, _ = pair_core(
                up1_ref, [(down_ref, rows_for_query(bias_ref, 1))], lanes
            )
            dq_ref[:, lanes] = dq_in[:, lanes] + dot_tn(grad_scores, up1_ref[FIRST, lanes])
            weights, grad_scores, queries, cotangents = pair_core(
                up_ref, [(down1_ref, rows_for_key(bias_ref, 1))], lanes
            )
            dk_ref[:, lanes] = dk_in[:, lanes] + dot_nn(grad_scores, queries)
            dv_ref[:, lanes] = dv_in[:, lanes] + dot_nn(weights, cotangents)

        over_heads(one_head)

    by_parity(run, (a_ref, b_ref, 0), (a1_ref, b1_ref, 1))
    token_ref[...] = jnp.zeros(token_ref.shape, f32)


def terms_kernel(
    copies, a_ref, b_ref, a1_ref, b1_ref, a2_ref, b2_ref, bias_ref, dq_in, dk_ref,
    query_unit_ref, key_unit_ref, qgain_ref, kgain_ref, dq_ref, terms_ref,
):
    def run(up_ref, down_ref, up1_ref, down1_ref, up2_ref, down2_ref):
        def one_head(h, sums):
            lanes = head_lanes(h)
            _, grad_scores, queries, _ = pair_core(
                up2_ref,
                [(down_ref, rows_for_query(bias_ref, 2)), (down1_ref, rows_between(bias_ref))],
                lanes,
            )
            parts = dot_tn(grad_scores, up2_ref[FIRST, lanes])
            total = dq_in[:, lanes] + parts[:CAP]
            dq_ref[:, lanes] = total
            products = parts * queries.astype(f32)
            return (
                sums[0] + jnp.sum(total * query_unit_ref[:, lanes], axis=0, keepdims=True),
                sums[1]
                + jnp.sum(dk_ref[:, lanes] * key_unit_ref[:, lanes], axis=0, keepdims=True),
                sums[2] + jnp.sum(products[:CAP], axis=0, keepdims=True),
                sums[3] + jnp.sum(products[CAP:], axis=0, keepdims=True),
            )

        none = jnp.zeros((1, WIDTH), f32)
        for_query, for_key, two, three = lax.fori_loop(0, HEADS, one_head, (none,) * 4, unroll=3)
        for_query = for_query + three / qgain_ref[...]
        for_key = for_key + (two + three) / kgain_ref[...]
        both = jnp.concatenate([for_query, for_key], axis=0) * SCALE
        terms_ref[...] = jnp.broadcast_to(both[None], (copies, 2, WIDTH))

    by_parity(run, (a_ref, b_ref, 0), (a1_ref, b1_ref, 1), (a2_ref, b2_ref, 2))


def norm_back(total, unit, inverse, gain):
    scaled = total * (gain * SCALE)
    return (inverse * (scaled - unit * jnp.mean(scaled * unit, axis=-1, keepdims=True))).astype(bf16)


def last_kernel(
    divisor, a_ref, b_ref, a2_ref, b2_ref, a3_ref, b3_ref, bias_ref, dq_in, dk_in, dv_in,
    query_unit_ref, query_inverse_ref, key_unit_ref, key_inverse_ref, qgain_ref, kgain_ref, parts_ref,
    query_grad_ref, key_grad_ref, value_grad_ref, gains_ref,
):
    gains_ref[...] = jnp.sum(parts_ref[...], axis=0) / divisor

    def run(up_ref, down_ref, up2_ref, down2_ref, up3_ref, down3_ref):
        def one_head(h):
            lanes = head_lanes(h)
            _, grad_scores, _, _ = pair_core(
                up3_ref, [(down_ref, rows_for_query(bias_ref, 3))], lanes
            )
            total = dq_in[:, lanes] + dot_tn(grad_scores, up3_ref[FIRST, lanes])
            query_grad_ref[0, :, lanes] = norm_back(
                total, query_unit_ref[:, lanes], query_inverse_ref[:, lanes], qgain_ref[...]
            )
            weights, grad_scores, queries, cotangents = pair_core(
                up_ref,
                [(down2_ref, rows_for_key(bias_ref, 2)), (down3_ref, rows_for_key(bias_ref, 3))],
                lanes,
            )
            total = dk_in[:, lanes] + dot_nn(grad_scores, queries)
            key_grad_ref[0, :, lanes] = norm_back(
                total, key_unit_ref[:, lanes], key_inverse_ref[:, lanes], kgain_ref[...]
            )
            total = dv_in[:, lanes] + dot_nn(weights, cotangents)
            value_grad_ref[0, :, lanes] = total.astype(bf16)

        over_heads(one_head, 2)

    by_parity(run, (a_ref, b_ref, 0), (a2_ref, b2_ref, 2), (a3_ref, b3_ref, 3))


def sum_kernel(parts_ref, out_ref):
    total = jnp.sum(parts_ref[...], axis=0)
    out_ref[...] = jnp.broadcast_to(total[None], out_ref.shape)


def tie_kernel(chain_ref, token_ref, out_ref):
    pass


VMEM = pl.BlockSpec(memory_space=pltpu.VMEM)
SMEM = pl.BlockSpec(memory_space=pltpu.SMEM)
ANY = pl.BlockSpec(memory_space=pl.ANY)
HBM = pl.BlockSpec(memory_space=pltpu.HBM)


def call(kernel, outs, specs, operands, aliases=None, scratch=(), limit=16 << 20):
    return pl.pallas_call(
        kernel,
        out_shape=tuple(outs),
        in_specs=specs,
        out_specs=(VMEM,) * len(outs),
        scratch_shapes=list(scratch),
        input_output_aliases=aliases or {},
        cost_estimate=pl.CostEstimate(flops=1 << 29, bytes_accessed=1 << 20, transcendentals=0),
        compiler_params=pltpu.CompilerParams(vmem_limit_bytes=limit),
    )(*operands)


def after(chain, token):
    return pl.pallas_call(
        tie_kernel,
        out_shape=jax.ShapeDtypeStruct(chain.shape, chain.dtype),
        in_specs=[ANY, ANY],
        out_specs=ANY,
        input_output_aliases={0: 0},
        compiler_params=pltpu.CompilerParams(vmem_limit_bytes=1 << 20),
    )(chain, token)


def swapped(value, odd):
    count = lax.axis_size("tm")
    pairs = [(i, (i + 1 if i % 2 == odd else i - 1) % count) for i in range(count)]
    return lax.ppermute(value, "tm", pairs)


def body(
    query_raw, key_raw, value_rows, grad_output, log_normalizer, output_dot,
    query_gain, key_gain, route_blocks, route_count, query_reach,
):
    shards, clips = lax.axis_size("tm"), lax.axis_size("dp")
    qgain, kgain = query_gain[None], key_gain[None]

    def like(rows, dtype):
        return jax.ShapeDtypeStruct((rows, HD), dtype)

    total, wide = like(CAP, f32), like(ROWS, bf16)
    lines = jax.ShapeDtypeStruct((16, CAP), f32)
    a, b = call(
        prep_kernel,
        (wide, wide),
        [HBM] * 8,
        (
            query_raw, key_raw, value_rows, grad_output,
            jnp.swapaxes(log_normalizer, 0, 1), jnp.swapaxes(output_dot, 0, 1), qgain, kgain,
        ),
        scratch=(
            pltpu.VMEM((CAP, HD), bf16), pltpu.VMEM((CAP, HD), bf16),
            pltpu.VMEM((HEADS, 1, CAP), f32), pltpu.VMEM((HEADS, 1, CAP), f32),
            pltpu.VMEM((1, WIDTH), f32), pltpu.VMEM((1, WIDTH), f32),
            pltpu.SemaphoreType.DMA((8,)),
        ),
        limit=62 << 20,
    )
    a1, b1 = swapped(a, 0), swapped(b, 1)
    dq, dk, dv, bias, *units = call(
        own_kernel,
        (total, total, total, lines) + (total,) * 4,
        [SMEM] * 3 + [VMEM] * 4,
        (jnp.swapaxes(route_blocks, 1, 2), route_count, query_reach, a, b, query_raw, key_raw),
    )
    a1 = after(a1, bias)
    a2, b2 = swapped(a1, 1), swapped(b1, 0)
    dq, dk, dv, token = call(
        step_kernel,
        (total, total, total, lines),
        [VMEM] * 8,
        (a, b, a1, b1, bias, dq, dk, dv),
        {5: 0, 6: 1, 7: 2},
    )
    a2 = after(a2, token)
    a3, b3 = swapped(a2, 0), swapped(b2, 1)
    dq, terms = call(
        functools.partial(terms_kernel, clips),
        (total, jax.ShapeDtypeStruct((clips, 2, WIDTH), f32)),
        [VMEM] * 13,
        (a, b, a1, b1, a2, b2, bias, dq, dk, units[0], units[2], qgain, kgain),
        {7: 0},
    )
    parts = lax.all_to_all(terms, "dp", 0, 0)
    (sums,) = call(
        sum_kernel, (jax.ShapeDtypeStruct((shards, 2, WIDTH), f32),), [VMEM], (parts,)
    )
    parts = lax.all_to_all(sums, "tm", 0, 0)
    row = jax.ShapeDtypeStruct((1, CAP, HD), bf16)
    query_grad, key_grad, value_grad, gains = call(
        functools.partial(last_kernel, shards * clips),
        (row, row, row, jax.ShapeDtypeStruct((2, WIDTH), f32)),
        [VMEM] * 17,
        (a, b, a2, b2, a3, b3, bias, dq, dk, dv, *units, qgain, kgain, parts),
    )
    return (query_grad, key_grad, value_grad, gains[0], gains[1])


def solution(mesh):
    rows = P("dp", "tm", None)
    stats = P("dp", None, "tm")
    return jax.shard_map(
        body,
        mesh=mesh,
        in_specs=(
            rows, rows, rows, rows, stats, stats, P(), P(),
            P("dp", None, None), P("dp", None), P("dp", None),
        ),
        out_specs=(rows, rows, rows, P(), P()),
        check_vma=False,
    )
```

time: 126 us -> 112 us (0.89)
  starting transfers between devices: 56.9 us -> 39.6 us
  waiting for transfers between devices: 7.62 us -> 11.2 us
    ppermute x12 -> x6, starting transfers between devices: 56.9 us -> 39.6 us  [swapped(): return lax.ppermute(value, 'tm', pairs)]
    ppermute x12 -> x6, waiting for transfers between devices: 7.62 us -> 11.2 us  [swapped(): return lax.ppermute(value, 'tm', pairs)]
    unnamed x26 -> x22, local copies, waits for them, and re-layouts: 3.47 us -> 2.99 us
    pallas_call x6 -> x8, Pallas kernels: 23 us -> 22.9 us  [the longest x6 22.9 us: call(): pl.pallas_call(kernel, out_shape=tuple(outs), in_specs=specs, out_specs=(...]
  transfers between devices with their start and end apart: 12 -> 6, of which waited for: 2 -> 2; matrix products, arithmetic and copies ran while one was open for 0% -> 0% of each run, Pallas kernels for 11% -> 11%
where the time goes in v2:
time: 112 us; the launch traced here: 111 us
  starting transfers between devices  39.6 us (35%)
  blocking collectives  33 us (29%)
  Pallas kernels  22.9 us (20%)
  waiting for transfers between devices  11.2 us (10%)
  local copies, waits for them, and re-layouts  3.5 us (3%)
    ppermute x6, starting transfers between devices, swapped(): return lax.ppermute(value, 'tm', pairs)  39.6 us
    pallas_call x6, Pallas kernels, call(): pl.pallas_call(kernel, out_shape=tuple(outs), in_specs=specs, out_specs=(...  22.9 us
    all_to_all x1, blocking collectives, body(): parts = lax.all_to_all(terms, 'dp', 0, 0)  20.6 us
    all_to_all x1, blocking collectives, body(): parts = lax.all_to_all(sums, 'tm', 0, 0)  12.4 us
    ppermute x6, waiting for transfers between devices, swapped(): return lax.ppermute(value, 'tm', pairs)  11.2 us
    unnamed x22, local copies, waits for them, and re-layouts  2.99 us
  transfers between devices with their start and end apart: 6, of which 2 were waited for; matrix products, arithmetic and copies ran while one was open for 0% of the time, Pallas kernels for 11%

profile of v2, /device:TPU:1, one launch (start us, length us, event | category | flops | bytes accessed | tf_op | source)
XLA Modules:
  0.0 111.1 jit_solution(7670435102853332797)
XLA Ops:
  0.6 0.0 copy-start.4
  0.6 0.0 copy-start.5
  0.7 3.3 %shard_map.146 = (bf16[272,1536]{1,0:T(8,128)(2,1)}, bf16[272,1536]{1,0:T(8,128)(2,1)}) custom-call(bf16[1,128,1536]{2,1,0:T(8,128)(2,1)} %query_ref.1, bf16[1,128,1536]{2,1,0:T(8,128)(2,1)} %key_ref.1, bf16[1,128,1536]{2,1,0:T(8,128)(2,1)} %value_hbm.1, bf16[1,128,1536]{2,1,0:T(8,128)(2,1)} %grad_hbm.1, f32[12,1,128]{2,1,0:T(1,128)} %bitcast.16, ...), custom_call_target="tpu_custom_call" | custom-call | flops 536870912 | bytes 1048576 | tf_op jit(solution)/shard_map/pallas_call | solution.py:340
  4.0 4.8 %collective-permute-start = (bf16[272,1536]{1,0:T(8,128)(2,1)}, bf16[272,1536]{1,0:T(8,128)(2,1)S(1)}, u32[]{:S(2)}, u32[]{:S(2)}) collective-permute-start(bf16[272,1536]{1,0:T(8,128)(2,1)} %get-tuple-element.25.a_ref), channel_id=1, source_target_pairs={{0,16},{16,0},{32,48},{48,32},{64,80},{80,64},{96,112},{112,96},{1... | collective-permute-start | bytes 2506760 | tf_op jit(solution)/shard_map/ppermute | solution.py:366
  8.8 0.0 copy-start.10
  8.8 0.0 copy-start.8
  8.8 0.0 copy-start.9
  8.9 12.0 %collective-permute-start.2 = (bf16[272,1536]{1,0:T(8,128)(2,1)}, bf16[272,1536]{1,0:T(8,128)(2,1)S(1)}, u32[]{:S(2)}, u32[]{:S(2)}) collective-permute-start(bf16[272,1536]{1,0:T(8,128)(2,1)} %get-tuple-element.26.b_ref), channel_id=1, source_target_pairs={{0,496},{16,32},{32,16},{48,64},{64,48},{80,96},{96,80},{112,128},... | collective-permute-start | bytes 2506760 | tf_op jit(solution)/shard_map/ppermute | solution.py:366
  20.9 0.0 copy-done.4
  20.9 0.0 copy-done.5
  20.9 0.0 copy-done.10
  20.9 0.0 copy-done.8
  20.9 0.0 copy-done.9
  20.9 0.0 copy-start
  20.9 1.1 %copy-done = bf16[272,1536]{1,0:T(8,128)(2,1)S(1)} copy-done((bf16[272,1536]{1,0:T(8,128)(2,1)S(1)}, bf16[272,1536]{1,0:T(8,128)(2,1)}, u32[]{:S(2)}) %copy-start) | copy-done | bytes 835608
  22.1 0.0 copy-start.2
  22.1 1.1 %copy-done.2 = bf16[272,1536]{1,0:T(8,128)(2,1)S(1)} copy-done((bf16[272,1536]{1,0:T(8,128)(2,1)S(1)}, bf16[272,1536]{1,0:T(8,128)(2,1)}, u32[]{:S(2)}) %copy-start.2) | copy-done | bytes 835608
  23.2 4.1 %shard_map.147 = (f32[128,1536]{1,0:T(8,128)S(1)}, f32[128,1536]{1,0:T(8,128)S(1)}, f32[128,1536]{1,0:T(8,128)S(1)}, f32[16,128]{1,0:T(8,128)S(1)}, f32[128,1536...) custom-call(s32[1,2,32]{2,1,0:T(2,128)S(1)} %bitcast.15, ...), custom_call_target="tpu_custom_call" | custom-call | flops 536870912 | bytes 1048576 | tf_op jit(solution)/shard_map/pallas_call | solution.py:340
  27.3 0.0 collective-permute-done.chain_ref
  27.3 0.0 copy-start.1
  27.3 0.0 copy-start.3
  27.3 12.9 %collective-permute-start.1 = (bf16[272,1536]{1,0:T(8,128)(2,1)S(1)}, bf16[272,1536]{1,0:T(8,128)(2,1)S(1)}, u32[]{:S(2)}, u32[]{:S(2)}) collective-permute-start(bf16[272,1536]{1,0:T(8,128)(2,1)S(1)} %shard_map.148.a1_ref), channel_id=1, source_target_pairs={{0,496},{16,32},{32,16},{48,64},{64,48},{80,96},{96,80},{112,128},... | collective-permute-start | bytes 2506760 | tf_op jit(solution)/shard_map/ppermute | solution.py:366
  40.2 0.0 collective-permute-done.2.b1_ref
  40.2 1.9 %collective-permute-start.3 = (bf16[272,1536]{1,0:T(8,128)(2,1)S(1)}, bf16[272,1536]{1,0:T(8,128)(2,1)S(1)}, u32[]{:S(2)}, u32[]{:S(2)}) collective-permute-start(bf16[272,1536]{1,0:T(8,128)(2,1)S(1)} %collective-permute-done.2.b1_ref), channel_id=1, source_target_pairs={{0,16},{16,0},{32,48},{48,32},{64,80},{80,64},{96,112},{112,96},{1... | collective-permute-start | bytes 2506760 | tf_op jit(solution)/shard_map/ppermute | solution.py:366
  42.2 0.0 copy-done.1
  42.2 0.0 copy-done.3
  42.2 5.1 %shard_map.149 = (f32[128,1536]{1,0:T(8,128)S(1)}, f32[128,1536]{1,0:T(8,128)S(1)}, f32[128,1536]{1,0:T(8,128)S(1)}, f32[16,128]{1,0:T(8,128)S(1)}) custom-call(bf16[272,1536]{1,0:T(8,128)(2,1)S(1)} %copy-done.1, bf16[272,1536]{1,0:T(8,128)(2,1)S(1)} %copy-done.3, ...), custom_call_target="tpu_custom_call", output_to_operand_aliasing={{0}: (5, {}), {1}: (6, {}), {2}: (7, {})} | custom-call | flops 536870912 | bytes 1048576 | tf_op jit(solution)/shard_map/pallas_call | solution.py:340
  47.3 10.3 %collective-permute-done.1.chain_ref = bf16[272,1536]{1,0:T(8,128)(2,1)S(1)} collective-permute-done((bf16[272,1536]{1,0:T(8,128)(2,1)S(1)}, bf16[272,1536]{1,0:T(8,128)(2,1)S(1)}, u32[]{:S(2)}, u32[]{:S(2)}) %collective-permute-start.1) | collective-permute-done | bytes 835616 | tf_op jit(solution)/shard_map/ppermute | solution.py:366
  57.6 1.9 %collective-permute-start.4 = (bf16[272,1536]{1,0:T(8,128)(2,1)S(1)}, bf16[272,1536]{1,0:T(8,128)(2,1)S(1)}, u32[]{:S(2)}, u32[]{:S(2)}) collective-permute-start(bf16[272,1536]{1,0:T(8,128)(2,1)S(1)} %shard_map.150.a2_ref), channel_id=1, source_target_pairs={{0,16},{16,0},{32,48},{48,32},{64,80},{80,64},{96,112},{112,96},{1... | collective-permute-start | bytes 2506760 | tf_op jit(solution)/shard_map/ppermute | solution.py:366
  59.5 0.9 collective-permute-done.3.b2_ref
  60.4 6.1 %collective-permute-start.5 = (bf16[272,1536]{1,0:T(8,128)(2,1)S(1)}, bf16[272,1536]{1,0:T(8,128)(2,1)S(1)}, u32[]{:S(2)}, u32[]{:S(2)}) collective-permute-start(bf16[272,1536]{1,0:T(8,128)(2,1)S(1)} %collective-permute-done.3.b2_ref), channel_id=1, source_target_pairs={{0,496},{16,32},{32,16},{48,64},{64,48},{80,96},{96,80},{112,128},... | collective-permute-start | bytes 2506760 | tf_op jit(solution)/shard_map/ppermute | solution.py:366
  66.5 0.0 copy-start.6
  66.5 0.0 copy-start.7
  66.5 0.6 copy-done.6
  67.1 0.0 copy-done.7
  67.2 3.4 %shard_map.151 = (f32[128,1536]{1,0:T(8,128)S(1)}, f32[16,2,128]{2,1,0:T(2,128)S(1)}) custom-call(bf16[272,1536]{1,0:T(8,128)(2,1)S(1)} %copy-done.1, bf16[272,1536]{1,0:T(8,128)(2,1)S(1)} %copy-done.3, bf16[272,1536]{1,0:T(8,128)(2,1)S(1)} %shard_map.148.a1_ref, ...), custom_call_target="tpu_custom_call", output_to_operand_aliasing={{0}: (7, {})} | custom-call | flops 536870912 | bytes 1048576 | tf_op jit(solution)/shard_map/pallas_call | solution.py:340
  70.5 20.6 %all_to_all.10.parts_ref = f32[16,2,128]{2,1,0:T(2,128)S(1)} all-to-all(f32[16,2,128]{2,1,0:T(2,128)S(1)} %get-tuple-element.40), channel_id=1, replica_groups=mesh['tm'=32,'dp'=16] {'dp'}, dimensions={0} | all-to-all | bytes 32768 | tf_op jit(solution)/shard_map/all_to_all | solution.py:422
  91.1 12.4 %all_to_all.11.parts_ref = f32[32,2,128]{2,1,0:T(2,128)S(1)} all-to-all(f32[32,2,128]{2,1,0:T(2,128)S(1)} %shard_map.152), channel_id=1, replica_groups=mesh['tm'=32,'dp'=16] {'tm'}, dimensions={0} | all-to-all | bytes 65536 | tf_op jit(solution)/shard_map/all_to_all | solution.py:426
  103.6 0.0 collective-permute-done.4.a3_ref
  103.6 0.0 collective-permute-done.5.b3_ref
  103.6 7.0 %shard_map.153 = (bf16[1,128,1536]{2,1,0:T(8,128)(2,1)}, bf16[1,128,1536]{2,1,0:T(8,128)(2,1)}, bf16[1,128,1536]{2,1,0:T(8,128)(2,1)}, f32[2,128]{1,0:T(2,128)S(1)}) custom-call(bf16[272,1536]{1,0:T(8,128)(2,1)S(1)} %copy-done.1, bf16[272,1536]{1,0:T(8,128)(2,1)S(1)} %copy-done.3, bf16[272,1536]{1,0:T(8,128)(2,1)S(1)} %shard_map.150.a2_ref, ...), custom_call_target="tpu_custom_call" | custom-call | flops 536870912 | bytes 1048576 | tf_op jit(solution)/shard_map/pallas_call | solution.py:340
  110.5 0.5 slice_bitcast_fusion
  (3 shorter events, 0.0 us)
Async XLA Ops:
  0.6 20.2 %copy-start.4 = (bf16[1,128,1536]{2,1,0:T(8,128)(2,1)S(1)}, bf16[1,128,1536]{2,1,0:T(8,128)(2,1)}, u32[]{:S(2)}) copy-start(bf16[1,128,1536]{2,1,0:T(8,128)(2,1)} %query_ref.1) | copy-start | bytes 1179652
  0.6 20.2 %copy-start.5 = (bf16[1,128,1536]{2,1,0:T(8,128)(2,1)S(1)}, bf16[1,128,1536]{2,1,0:T(8,128)(2,1)}, u32[]{:S(2)}) copy-start(bf16[1,128,1536]{2,1,0:T(8,128)(2,1)} %key_ref.1) | copy-start | bytes 1179652
  4.0 23.3 %collective-permute-start = (bf16[272,1536]{1,0:T(8,128)(2,1)}, bf16[272,1536]{1,0:T(8,128)(2,1)S(1)}, u32[]{:S(2)}, u32[]{:S(2)}) collective-permute-start(bf16[272,1536]{1,0:T(8,128)(2,1)} %get-tuple-element.25.a_ref), channel_id=1, source_target_pairs={{0,16},{16,0},{32,48},{48,32},{64,80},{80,64},{96,112},{112,96},{1... | collective-permute-start | bytes 2506760 | tf_op jit(solution)/shard_map/ppermute | solution.py:366
  8.8 12.1 %copy-start.10 = (s32[1,64]{1,0:T(1,128)S(1)}, s32[1,64]{1,0:T(1,128)}, u32[]{:S(2)}) copy-start(s32[1,64]{1,0:T(1,128)} %reach_ref.1) | copy-start | bytes 772
  8.8 12.1 %copy-start.8 = (s32[1,32,2]{1,2,0:T(2,128)S(1)}, s32[1,32,2]{1,2,0:T(2,128)}, u32[]{:S(2)}) copy-start(s32[1,32,2]{1,2,0:T(2,128)} %param.19) | copy-start | bytes 772
  8.8 12.1 %copy-start.9 = (s32[1,32]{1,0:T(1,128)S(1)}, s32[1,32]{1,0:T(1,128)}, u32[]{:S(2)}) copy-start(s32[1,32]{1,0:T(1,128)} %counts_ref.1) | copy-start | bytes 388
  8.9 31.4 %collective-permute-start.2 = (bf16[272,1536]{1,0:T(8,128)(2,1)}, bf16[272,1536]{1,0:T(8,128)(2,1)S(1)}, u32[]{:S(2)}, u32[]{:S(2)}) collective-permute-start(bf16[272,1536]{1,0:T(8,128)(2,1)} %get-tuple-element.26.b_ref), channel_id=1, source_target_pairs={{0,496},{16,32},{32,16},{48,64},{64,48},{80,96},{96,80},{112,128},... | collective-permute-start | bytes 2506760 | tf_op jit(solution)/shard_map/ppermute | solution.py:366
  20.9 1.2 %copy-start = (bf16[272,1536]{1,0:T(8,128)(2,1)S(1)}, bf16[272,1536]{1,0:T(8,128)(2,1)}, u32[]{:S(2)}) copy-start(bf16[272,1536]{1,0:T(8,128)(2,1)} %get-tuple-element.25.a_ref) | copy-start | bytes 2506756
  22.1 1.1 %copy-start.2 = (bf16[272,1536]{1,0:T(8,128)(2,1)S(1)}, bf16[272,1536]{1,0:T(8,128)(2,1)}, u32[]{:S(2)}) copy-start(bf16[272,1536]{1,0:T(8,128)(2,1)} %get-tuple-element.26.b_ref) | copy-start | bytes 2506756
  27.3 14.8 %copy-start.1 = (bf16[272,1536]{1,0:T(8,128)(2,1)S(1)}, bf16[272,1536]{1,0:T(8,128)(2,1)}, u32[]{:S(2)}) copy-start(bf16[272,1536]{1,0:T(8,128)(2,1)} %get-tuple-element.25.a_ref) | copy-start | bytes 2506756
  27.3 14.8 %copy-start.3 = (bf16[272,1536]{1,0:T(8,128)(2,1)S(1)}, bf16[272,1536]{1,0:T(8,128)(2,1)}, u32[]{:S(2)}) copy-start(bf16[272,1536]{1,0:T(8,128)(2,1)} %get-tuple-element.26.b_ref) | copy-start | bytes 2506756
  27.3 30.2 %collective-permute-start.1 = (bf16[272,1536]{1,0:T(8,128)(2,1)S(1)}, bf16[272,1536]{1,0:T(8,128)(2,1)S(1)}, u32[]{:S(2)}, u32[]{:S(2)}) collective-permute-start(bf16[272,1536]{1,0:T(8,128)(2,1)S(1)} %shard_map.148.a1_ref), channel_id=1, source_target_pairs={{0,496},{16,32},{32,16},{48,64},{64,48},{80,96},{96,80},{112,128},... | collective-permute-start | bytes 2506760 | tf_op jit(solution)/shard_map/ppermute | solution.py:366
  40.2 20.2 %collective-permute-start.3 = (bf16[272,1536]{1,0:T(8,128)(2,1)S(1)}, bf16[272,1536]{1,0:T(8,128)(2,1)S(1)}, u32[]{:S(2)}, u32[]{:S(2)}) collective-permute-start(bf16[272,1536]{1,0:T(8,128)(2,1)S(1)} %collective-permute-done.2.b1_ref), channel_id=1, source_target_pairs={{0,16},{16,0},{32,48},{48,32},{64,80},{80,64},{96,112},{112,96},{1... | collective-permute-start | bytes 2506760 | tf_op jit(solution)/shard_map/ppermute | solution.py:366
  57.6 46.0 %collective-permute-start.4 = (bf16[272,1536]{1,0:T(8,128)(2,1)S(1)}, bf16[272,1536]{1,0:T(8,128)(2,1)S(1)}, u32[]{:S(2)}, u32[]{:S(2)}) collective-permute-start(bf16[272,1536]{1,0:T(8,128)(2,1)S(1)} %shard_map.150.a2_ref), channel_id=1, source_target_pairs={{0,16},{16,0},{32,48},{48,32},{64,80},{80,64},{96,112},{112,96},{1... | collective-permute-start | bytes 2506760 | tf_op jit(solution)/shard_map/ppermute | solution.py:366
  60.4 43.2 %collective-permute-start.5 = (bf16[272,1536]{1,0:T(8,128)(2,1)S(1)}, bf16[272,1536]{1,0:T(8,128)(2,1)S(1)}, u32[]{:S(2)}, u32[]{:S(2)}) collective-permute-start(bf16[272,1536]{1,0:T(8,128)(2,1)S(1)} %collective-permute-done.3.b2_ref), channel_id=1, source_target_pairs={{0,496},{16,32},{32,16},{48,64},{64,48},{80,96},{96,80},{112,128},... | collective-permute-start | bytes 2506760 | tf_op jit(solution)/shard_map/ppermute | solution.py:366
  66.5 0.7 copy-start.6
  66.5 0.7 copy-start.7

commit v3 on v2

--- a/solution.py
+++ b/solution.py
@@ -15,7 +15,7 @@
 WIDTH = 128
 CAP = ROUTE_MOST * BLK
 HD = HEADS * WIDTH
-STAT_ROWS = 16
+STAT_ROWS = 8
 ROWS = 2 * CAP + STAT_ROWS
 FIRST, SECOND, STATS = slice(0, CAP), slice(CAP, 2 * CAP), slice(2 * CAP, ROWS)
 LOG2E = 1.4426950408889634
@@ -31,7 +31,7 @@
     return pl.ds(pl.multiple_of(h * WIDTH, WIDTH), WIDTH)
 
 
-def over_heads(step, unroll=3):
+def over_heads(step, unroll=HEADS):
     lax.fori_loop(0, HEADS, lambda h, none: step(h), None, unroll=unroll)
 
 
@@ -163,8 +163,30 @@
     return rows_for_query(bias_ref, STEPS - 1 + offset)
 
 
-def rows_between(bias_ref):
-    return rows_for_query(bias_ref, 2 * STEPS - 1)
+def by_query(bias_ref, which):
+    at = (2 * STEPS - 1 + which) * ROUTE_MOST
+    return bias_ref[at : at + ROUTE_MOST, :]
+
+
+def as_column(row):
+    return jnp.transpose(jnp.broadcast_to(row, (CAP, CAP)))
+
+
+def with_bias(column, bias):
+    return jnp.concatenate(
+        [column[i * BLK : (i + 1) * BLK] + bias[i : i + 1] for i in range(ROUTE_MOST)], axis=0
+    )
+
+
+def grad_query_core(up_ref, downs, lanes):
+    queries = side_by_side([ref[FIRST, lanes] for ref, _, _ in downs], 0)
+    cotangents = side_by_side([ref[SECOND, lanes] for ref, _, _ in downs], 0)
+    known = side_by_side([ref[:, lanes] for _, ref, _ in downs], 0)
+    dots = side_by_side([ref[:, lanes] for _, _, ref in downs], 0)
+    probability = jnp.exp2(dot_nt(queries, up_ref[FIRST, lanes]) * (SCALE * LOG2E) + known)
+    grad_weights = dot_nt(cotangents, up_ref[SECOND, lanes])
+    grad_scores = (probability * (grad_weights - dots)).astype(bf16)
+    return dot_nn(grad_scores, up_ref[FIRST, lanes]), queries
 
 
 def fill_bias(blocks_ref, counts_ref, reach_ref, bias_ref):
@@ -172,11 +194,12 @@
     here = lax.axis_index("tm")
     lane = lax.broadcasted_iota(jnp.int32, (1, CAP), 1)
 
-    def pair_rows(query_shard, key_shard, offset):
+    def pair_rows(query_shard, key_shard, offset, by_query=False):
         rows = []
-        for kj in range(ROUTE_MOST):
+        for outer in range(ROUTE_MOST):
             values = []
-            for qi in range(ROUTE_MOST):
+            for inner in range(ROUTE_MOST):
+                qi, kj = (outer, inner) if by_query else (inner, outer)
                 near = (
                     offset * NBLK
                     + blocks_ref[0, qi, query_shard]
@@ -193,7 +216,11 @@
         rows += pair_rows(here, lax.rem(here - offset + shards, shards), offset)
     for offset in range(1, STEPS):
         rows += pair_rows(lax.rem(here + offset, shards), here, offset)
-    rows += pair_rows(lax.rem(here + 1, shards), lax.rem(here - 2 + shards, shards), STEPS - 1)
+    two_back = lax.rem(here - 2 + shards, shards)
+    rows += pair_rows(here, two_back, 2, True)
+    rows += pair_rows(here, lax.rem(here - 3 + shards, shards), 3, True)
+    rows += pair_rows(lax.rem(here + 1, shards), two_back, 3, True)
+    rows += [jnp.zeros((1, CAP), f32)] * (bias_ref.shape[0] - len(rows))
     for at, row in enumerate(rows):
         bias_ref[at : at + 1, :] = row
 
@@ -201,6 +228,7 @@
 def own_kernel(
     blocks_ref, counts_ref, reach_ref, a_ref, b_ref, query_ref, key_ref,
     dq_ref, dk_ref, dv_ref, bias_ref, query_unit_ref, query_inverse_ref, key_unit_ref, key_inverse_ref,
+    two_ref, three_ref, dot_ref,
 ):
     fill_bias(blocks_ref, counts_ref, reach_ref, bias_ref)
 
@@ -220,6 +248,11 @@
                 unit, inverse = unit_of(raw_ref[0, :, lanes])
                 unit_ref[:, lanes] = unit
                 inverse_ref[:, lanes] = jnp.broadcast_to(inverse, unit.shape)
+            log_row, dot_row = stat_rows(down_ref, lanes)
+            column = as_column(log_row)
+            two_ref[:, lanes] = with_bias(column, by_query(bias_ref, 0))
+            three_ref[:, lanes] = with_bias(column, by_query(bias_ref, 1))
+            dot_ref[:, lanes] = as_column(dot_row)
 
         over_heads(one_head)
 
@@ -227,7 +260,8 @@
 
 
 def step_kernel(
-    a_ref, b_ref, a1_ref, b1_ref, bias_ref, dq_in, dk_in, dv_in, dq_ref, dk_ref, dv_ref, token_ref
+    a_ref, b_ref, a1_ref, b1_ref, bias_ref, dq_in, dk_in, dv_in, dq_ref, dk_ref, dv_ref, token_ref,
+    next_three_ref, next_dot_ref,
 ):
     def run(up_ref, down_ref, up1_ref, down1_ref):
         def one_head(h):
@@ -241,6 +275,9 @@
             )
             dk_ref[:, lanes] = dk_in[:, lanes] + dot_nn(grad_scores, queries)
             dv_ref[:, lanes] = dv_in[:, lanes] + dot_nn(weights, cotangents)
+            log_row, dot_row = stat_rows(down1_ref, lanes)
+            next_three_ref[:, lanes] = with_bias(as_column(log_row), by_query(bias_ref, 2))
+            next_dot_ref[:, lanes] = as_column(dot_row)
 
         over_heads(one_head)
 
@@ -249,18 +286,18 @@
 
 
 def terms_kernel(
-    copies, a_ref, b_ref, a1_ref, b1_ref, a2_ref, b2_ref, bias_ref, dq_in, dk_ref,
-    query_unit_ref, key_unit_ref, qgain_ref, kgain_ref, dq_ref, terms_ref,
+    copies, a_ref, b_ref, a1_ref, b1_ref, a2_ref, b2_ref, dq_in, dk_ref,
+    query_unit_ref, key_unit_ref, qgain_ref, kgain_ref, two_ref, dot_ref, next_three_ref, next_dot_ref,
+    dq_ref, terms_ref,
 ):
     def run(up_ref, down_ref, up1_ref, down1_ref, up2_ref, down2_ref):
         def one_head(h, sums):
             lanes = head_lanes(h)
-            _, grad_scores, queries, _ = pair_core(
+            parts, queries = grad_query_core(
                 up2_ref,
-                [(down_ref, rows_for_query(bias_ref, 2)), (down1_ref, rows_between(bias_ref))],
+                [(down_ref, two_ref, dot_ref), (down1_ref, next_three_ref, next_dot_ref)],
                 lanes,
             )
-            parts = dot_tn(grad_scores, up2_ref[FIRST, lanes])
             total = dq_in[:, lanes] + parts[:CAP]
             dq_ref[:, lanes] = total
             products = parts * queries.astype(f32)
@@ -273,7 +310,7 @@
             )
 
         none = jnp.zeros((1, WIDTH), f32)
-        for_query, for_key, two, three = lax.fori_loop(0, HEADS, one_head, (none,) * 4, unroll=3)
+        for_query, for_key, two, three = lax.fori_loop(0, HEADS, one_head, (none,) * 4, unroll=HEADS)
         for_query = for_query + three / qgain_ref[...]
         for_key = for_key + (two + three) / kgain_ref[...]
         both = jnp.concatenate([for_query, for_key], axis=0) * SCALE
@@ -289,7 +326,8 @@
 
 def last_kernel(
     divisor, a_ref, b_ref, a2_ref, b2_ref, a3_ref, b3_ref, bias_ref, dq_in, dk_in, dv_in,
-    query_unit_ref, query_inverse_ref, key_unit_ref, key_inverse_ref, qgain_ref, kgain_ref, parts_ref,
+    query_unit_ref, query_inverse_ref, key_unit_ref, key_inverse_ref, qgain_ref, kgain_ref,
+    three_ref, dot_ref, parts_ref,
     query_grad_ref, key_grad_ref, value_grad_ref, gains_ref,
 ):
     gains_ref[...] = jnp.sum(parts_ref[...], axis=0) / divisor
@@ -297,10 +335,8 @@
     def run(up_ref, down_ref, up2_ref, down2_ref, up3_ref, down3_ref):
         def one_head(h):
             lanes = head_lanes(h)
-            _, grad_scores, _, _ = pair_core(
-                up3_ref, [(down_ref, rows_for_query(bias_ref, 3))], lanes
-            )
-            total = dq_in[:, lanes] + dot_tn(grad_scores, up3_ref[FIRST, lanes])
+            part, _ = grad_query_core(up3_ref, [(down_ref, three_ref, dot_ref)], lanes)
+            total = dq_in[:, lanes] + part
             query_grad_ref[0, :, lanes] = norm_back(
                 total, query_unit_ref[:, lanes], query_inverse_ref[:, lanes], qgain_ref[...]
             )
@@ -316,7 +352,7 @@
             total = dv_in[:, lanes] + dot_nn(weights, cotangents)
             value_grad_ref[0, :, lanes] = total.astype(bf16)
 
-        over_heads(one_head, 2)
+        over_heads(one_head)
 
     by_parity(run, (a_ref, b_ref, 0), (a2_ref, b2_ref, 2), (a3_ref, b3_ref, 3))
 
@@ -377,7 +413,7 @@
         return jax.ShapeDtypeStruct((rows, HD), dtype)
 
     total, wide = like(CAP, f32), like(ROWS, bf16)
-    lines = jax.ShapeDtypeStruct((16, CAP), f32)
+    lines = jax.ShapeDtypeStruct((24, CAP), f32)
     a, b = call(
         prep_kernel,
         (wide, wide),
@@ -395,41 +431,55 @@
         limit=62 << 20,
     )
     a1, b1 = swapped(a, 0), swapped(b, 1)
-    dq, dk, dv, bias, *units = call(
+    dq, dk, dv, bias, *units, two, three, dots = call(
         own_kernel,
-        (total, total, total, lines) + (total,) * 4,
+        (total, total, total, lines) + (total,) * 7,
         [SMEM] * 3 + [VMEM] * 4,
         (jnp.swapaxes(route_blocks, 1, 2), route_count, query_reach, a, b, query_raw, key_raw),
     )
     a1 = after(a1, bias)
     a2, b2 = swapped(a1, 1), swapped(b1, 0)
-    dq, dk, dv, token = call(
+    dq, dk, dv, token, next_three, next_dots = call(
         step_kernel,
-        (total, total, total, lines),
+        (total, total, total, lines, total, total),
         [VMEM] * 8,
         (a, b, a1, b1, bias, dq, dk, dv),
         {5: 0, 6: 1, 7: 2},
     )
-    a2 = after(a2, token)
-    a3, b3 = swapped(a2, 0), swapped(b2, 1)
+    b2 = after(b2, token)
+    b3, a3 = swapped(b2, 1), swapped(a2, 0)
+    ends = 2 if clips % 4 == 0 else 1
+    first = [
+        [clip for clip in range(clips) if clip // 2 % ends == end] for end in range(ends)
+    ]
+    second = [
+        [shard * clips + clip for shard in range(shards) for clip in column]
+        for column in zip(*first)
+    ]
     dq, terms = call(
-        functools.partial(terms_kernel, clips),
-        (total, jax.ShapeDtypeStruct((clips, 2, WIDTH), f32)),
-        [VMEM] * 13,
-        (a, b, a1, b1, a2, b2, bias, dq, dk, units[0], units[2], qgain, kgain),
-        {7: 0},
-    )
-    parts = lax.all_to_all(terms, "dp", 0, 0)
+        functools.partial(terms_kernel, len(first[0])),
+        (total, jax.ShapeDtypeStruct((len(first[0]), 2, WIDTH), f32)),
+        [VMEM] * 16,
+        (
+            a, b, a1, b1, a2, b2, dq, dk, units[0], units[2], qgain, kgain,
+            two, dots, next_three, next_dots,
+        ),
+        {6: 0},
+    )
+    parts = lax.all_to_all(terms, "dp", 0, 0, axis_index_groups=first)
     (sums,) = call(
-        sum_kernel, (jax.ShapeDtypeStruct((shards, 2, WIDTH), f32),), [VMEM], (parts,)
-    )
-    parts = lax.all_to_all(sums, "tm", 0, 0)
+        sum_kernel, (jax.ShapeDtypeStruct((len(second[0]), 2, WIDTH), f32),), [VMEM], (parts,)
+    )
+    parts = lax.all_to_all(sums, ("tm", "dp"), 0, 0, axis_index_groups=second)
     row = jax.ShapeDtypeStruct((1, CAP, HD), bf16)
     query_grad, key_grad, value_grad, gains = call(
         functools.partial(last_kernel, shards * clips),
         (row, row, row, jax.ShapeDtypeStruct((2, WIDTH), f32)),
-        [VMEM] * 17,
-        (a, b, a2, b2, a3, b3, bias, dq, dk, dv, *units, qgain, kgain, parts),
+        [VMEM] * 19,
+        (
+            a, b, a2, b2, a3, b3, bias, dq, dk, dv, *units, qgain, kgain,
+            three, dots, parts,
+        ),
     )
     return (query_grad, key_grad, value_grad, gains[0], gains[1])
 

time: 112 us -> 104 us (0.929)
  starting transfers between devices: 39.6 us -> 33.2 us
  waiting for transfers between devices: 11.2 us -> 17.4 us
  Pallas kernels: 22.9 us -> 18.6 us
  blocking collectives: 33 us -> 29.7 us
    ppermute x6, starting transfers between devices: 39.6 us -> 33.2 us  [swapped(): return lax.ppermute(value, 'tm', pairs)]
    ppermute x6, waiting for transfers between devices: 11.2 us -> 17.4 us  [swapped(): return lax.ppermute(value, 'tm', pairs)]
    pallas_call x6, Pallas kernels: 22.9 us -> 18.6 us  [call(): pl.pallas_call(kernel, out_shape=tuple(outs), in_specs=specs, out_specs=(...]
    all_to_all x2, blocking collectives: 33 us -> 29.7 us  [the longest x1 18 us: body(): parts = lax.all_to_all(sums, ('tm', 'dp'), 0, 0, axis_index_groups=second)]
  transfers between devices with their start and end apart: 6 -> 6, of which waited for: 2 -> 3; matrix products, arithmetic and copies ran while one was open for 0% -> 0% of each run, Pallas kernels for 11% -> 10%
where the time goes in v3:
time: 104 us; the launch traced here: 103 us
  starting transfers between devices  33.2 us (32%)
  blocking collectives  29.7 us (29%)
  Pallas kernels  18.6 us (18%)
  waiting for transfers between devices  17.4 us (17%)
  local copies, waits for them, and re-layouts  3.49 us (3%)
    ppermute x6, starting transfers between devices, swapped(): return lax.ppermute(value, 'tm', pairs)  33.2 us
    pallas_call x6, Pallas kernels, call(): pl.pallas_call(kernel, out_shape=tuple(outs), in_specs=specs, out_specs=(...  18.6 us
    all_to_all x1, blocking collectives, body(): parts = lax.all_to_all(sums, ('tm', 'dp'), 0, 0, axis_index_groups=second)  18 us
    ppermute x6, waiting for transfers between devices, swapped(): return lax.ppermute(value, 'tm', pairs)  17.4 us
    all_to_all x1, blocking collectives, body(): parts = lax.all_to_all(terms, 'dp', 0, 0, axis_index_groups=first)  11.8 us
    unnamed x22, local copies, waits for them, and re-layouts  2.97 us
  transfers between devices with their start and end apart: 6, of which 3 were waited for; matrix products, arithmetic and copies ran while one was open for 0% of the time, Pallas kernels for 10%

profile of v3, /device:TPU:1, one launch (start us, length us, event | category | flops | bytes accessed | tf_op | source)
XLA Modules:
  0.0 103.3 jit_solution(9183983192486273824)
XLA Ops:
  0.6 0.0 copy-start.4
  0.6 0.0 copy-start.5
  0.7 3.1 %shard_map.146 = (bf16[264,1536]{1,0:T(8,128)(2,1)}, bf16[264,1536]{1,0:T(8,128)(2,1)}) custom-call(bf16[1,128,1536]{2,1,0:T(8,128)(2,1)} %query_ref.1, bf16[1,128,1536]{2,1,0:T(8,128)(2,1)} %key_ref.1, bf16[1,128,1536]{2,1,0:T(8,128)(2,1)} %value_hbm.1, bf16[1,128,1536]{2,1,0:T(8,128)(2,1)} %grad_hbm.1, f32[12,1,128]{2,1,0:T(1,128)} %bitcast.16, ...), custom_call_target="tpu_custom_call" | custom-call | flops 536870912 | bytes 1048576 | tf_op jit(solution)/shard_map/pallas_call | solution.py:376
  3.7 14.5 %collective-permute-start.2 = (bf16[264,1536]{1,0:T(8,128)(2,1)}, bf16[264,1536]{1,0:T(8,128)(2,1)S(1)}, u32[]{:S(2)}, u32[]{:S(2)}) collective-permute-start(bf16[264,1536]{1,0:T(8,128)(2,1)} %get-tuple-element.31.b_ref), channel_id=1, source_target_pairs={{0,496},{16,32},{32,16},{48,64},{64,48},{80,96},{96,80},{112,128},... | collective-permute-start | bytes 2433032 | tf_op jit(solution)/shard_map/ppermute | solution.py:402
  18.3 0.0 copy-start.10
  18.3 0.0 copy-start.8
  18.3 0.0 copy-start.9
  18.3 2.1 %collective-permute-start = (bf16[264,1536]{1,0:T(8,128)(2,1)}, bf16[264,1536]{1,0:T(8,128)(2,1)S(1)}, u32[]{:S(2)}, u32[]{:S(2)}) collective-permute-start(bf16[264,1536]{1,0:T(8,128)(2,1)} %get-tuple-element.30.a_ref), channel_id=1, source_target_pairs={{0,16},{16,0},{32,48},{48,32},{64,80},{80,64},{96,112},{112,96},{1... | collective-permute-start | bytes 2433032 | tf_op jit(solution)/shard_map/ppermute | solution.py:402
  20.4 0.0 copy-done.4
  20.4 0.0 copy-done.5
  20.4 0.0 copy-done.10
  20.4 0.0 copy-done.8
  20.4 0.0 copy-done.9
  20.4 0.0 copy-start
  20.4 1.1 %copy-done = bf16[264,1536]{1,0:T(8,128)(2,1)S(1)} copy-done((bf16[264,1536]{1,0:T(8,128)(2,1)S(1)}, bf16[264,1536]{1,0:T(8,128)(2,1)}, u32[]{:S(2)}) %copy-start) | copy-done | bytes 811032
  21.6 0.0 copy-start.2
  21.6 1.1 %copy-done.2 = bf16[264,1536]{1,0:T(8,128)(2,1)S(1)} copy-done((bf16[264,1536]{1,0:T(8,128)(2,1)S(1)}, bf16[264,1536]{1,0:T(8,128)(2,1)}, u32[]{:S(2)}) %copy-start.2) | copy-done | bytes 811032
  22.7 3.6 %shard_map.147 = (f32[128,1536]{1,0:T(8,128)S(1)}, f32[128,1536]{1,0:T(8,128)S(1)}, f32[128,1536]{1,0:T(8,128)S(1)}, f32[24,128]{1,0:T(8,128)S(1)}, f32[128,1536...) custom-call(s32[1,2,32]{2,1,0:T(2,128)S(1)} %bitcast.15, ...), custom_call_target="tpu_custom_call" | custom-call | flops 536870912 | bytes 1048576 | tf_op jit(solution)/shard_map/pallas_call | solution.py:376
  26.4 9.9 %collective-permute-done.2.b1_ref = bf16[264,1536]{1,0:T(8,128)(2,1)S(1)} collective-permute-done((bf16[264,1536]{1,0:T(8,128)(2,1)}, bf16[264,1536]{1,0:T(8,128)(2,1)S(1)}, u32[]{:S(2)}, u32[]{:S(2)}) %collective-permute-start.2) | collective-permute-done | bytes 811040 | tf_op jit(solution)/shard_map/ppermute | solution.py:402
  36.3 1.9 %collective-permute-start.3 = (bf16[264,1536]{1,0:T(8,128)(2,1)S(1)}, bf16[264,1536]{1,0:T(8,128)(2,1)S(1)}, u32[]{:S(2)}, u32[]{:S(2)}) collective-permute-start(bf16[264,1536]{1,0:T(8,128)(2,1)S(1)} %collective-permute-done.2.b1_ref), channel_id=1, source_target_pairs={{0,16},{16,0},{32,48},{48,32},{64,80},{80,64},{96,112},{112,96},{1... | collective-permute-start | bytes 2433032 | tf_op jit(solution)/shard_map/ppermute | solution.py:402
  38.2 1.0 collective-permute-done.chain_ref
  39.2 0.0 copy-start.1
  39.2 0.0 copy-start.3
  39.2 6.1 %collective-permute-start.1 = (bf16[264,1536]{1,0:T(8,128)(2,1)S(1)}, bf16[264,1536]{1,0:T(8,128)(2,1)S(1)}, u32[]{:S(2)}, u32[]{:S(2)}) collective-permute-start(bf16[264,1536]{1,0:T(8,128)(2,1)S(1)} %shard_map.148.a1_ref), channel_id=1, source_target_pairs={{0,496},{16,32},{32,16},{48,64},{64,48},{80,96},{96,80},{112,128},... | collective-permute-start | bytes 2433032 | tf_op jit(solution)/shard_map/ppermute | solution.py:402
  45.3 0.0 copy-done.1
  45.3 0.0 copy-done.3
  45.3 4.6 %shard_map.149 = (f32[128,1536]{1,0:T(8,128)S(1)}, f32[128,1536]{1,0:T(8,128)S(1)}, f32[128,1536]{1,0:T(8,128)S(1)}, f32[24,128]{1,0:T(8,128)S(1)}, f32[128,1536]{1,0:T(8,128)S(1)}, /*index=5*/f32[128,1536]{1,0:T(8,128)S(1)}) custom-call(bf16[264,1536]{1,0:T(8,128)(2,1)S(1)} %copy-done.1, ...), custom_call_target="tpu_custom_call", output_to_operand_aliasing={{0}: (5, {}), {1}: (6, {}), {2}: (7, {})} | custom-call | flops 536870912 | bytes 1048576 | tf_op jit(solution)/shard_map/pallas_call | solution.py:376
  50.0 6.5 %collective-permute-done.3.chain_ref = bf16[264,1536]{1,0:T(8,128)(2,1)S(1)} collective-permute-done((bf16[264,1536]{1,0:T(8,128)(2,1)S(1)}, bf16[264,1536]{1,0:T(8,128)(2,1)S(1)}, u32[]{:S(2)}, u32[]{:S(2)}) %collective-permute-start.3) | collective-permute-done | bytes 811040 | tf_op jit(solution)/shard_map/ppermute | solution.py:402
  56.5 6.6 %collective-permute-start.5 = (bf16[264,1536]{1,0:T(8,128)(2,1)S(1)}, bf16[264,1536]{1,0:T(8,128)(2,1)S(1)}, u32[]{:S(2)}, u32[]{:S(2)}) collective-permute-start(bf16[264,1536]{1,0:T(8,128)(2,1)S(1)} %shard_map.150.b2_ref), channel_id=1, source_target_pairs={{0,496},{16,32},{32,16},{48,64},{64,48},{80,96},{96,80},{112,128},... | collective-permute-start | bytes 2433032 | tf_op jit(solution)/shard_map/ppermute | solution.py:402
  63.1 0.0 collective-permute-done.1.a2_ref
  63.1 1.9 %collective-permute-start.4 = (bf16[264,1536]{1,0:T(8,128)(2,1)S(1)}, bf16[264,1536]{1,0:T(8,128)(2,1)S(1)}, u32[]{:S(2)}, u32[]{:S(2)}) collective-permute-start(bf16[264,1536]{1,0:T(8,128)(2,1)S(1)} %collective-permute-done.1.a2_ref), channel_id=1, source_target_pairs={{0,16},{16,0},{32,48},{48,32},{64,80},{80,64},{96,112},{112,96},{1... | collective-permute-start | bytes 2433032 | tf_op jit(solution)/shard_map/ppermute | solution.py:402
  65.0 0.0 copy-start.6
  65.1 0.0 copy-start.7
  65.1 0.6 copy-done.6
  65.7 0.0 copy-done.7
  65.7 2.1 %shard_map.151 = (f32[128,1536]{1,0:T(8,128)S(1)}, f32[8,2,128]{2,1,0:T(2,128)S(1)}) custom-call(bf16[264,1536]{1,0:T(8,128)(2,1)S(1)} %copy-done.1, bf16[264,1536]{1,0:T(8,128)(2,1)S(1)} %copy-done.3, bf16[264,1536]{1,0:T(8,128)(2,1)S(1)} %shard_map.148.a1_ref, ...), custom_call_target="tpu_custom_call", output_to_operand_aliasing={{0}: (6, {})} | custom-call | flops 536870912 | bytes 1048576 | tf_op jit(solution)/shard_map/pallas_call | solution.py:376
  67.8 11.8 %all_to_all.10.parts_ref = f32[8,2,128]{2,1,0:T(2,128)S(1)} all-to-all(f32[8,2,128]{2,1,0:T(2,128)S(1)} %get-tuple-element.50), channel_id=1, replica_groups={{0,1,4,5,8,9,12,13},{2,3,6,7,10,11,14,15},{16,17,20,21,24,25,28,29},{18..., dimensions={0} | all-to-all | bytes 16384 | tf_op jit(solution)/shard_map/all_to_all | solution.py:469
  79.6 18.0 %all_to_all.11.parts_ref = f32[64,2,128]{2,1,0:T(2,128)S(1)} all-to-all(f32[64,2,128]{2,1,0:T(2,128)S(1)} %shard_map.152), channel_id=1, replica_groups={{0,2,16,18,32,34,48,50,64,66,80,82,96,98,112,114,128,130,144,146,160,16..., dimensions={0} | all-to-all | bytes 131072 | tf_op jit(solution)/shard_map/all_to_all | solution.py:473
  97.6 0.0 collective-permute-done.5.b3_ref
  97.6 0.0 collective-permute-done.4.a3_ref
  97.6 5.1 %shard_map.153 = (bf16[1,128,1536]{2,1,0:T(8,128)(2,1)}, bf16[1,128,1536]{2,1,0:T(8,128)(2,1)}, bf16[1,128,1536]{2,1,0:T(8,128)(2,1)}, f32[2,128]{1,0:T(2,128)S(1)}) custom-call(bf16[264,1536]{1,0:T(8,128)(2,1)S(1)} %copy-done.1, bf16[264,1536]{1,0:T(8,128)(2,1)S(1)} %copy-done.3, bf16[264,1536]{1,0:T(8,128)(2,1)S(1)} %collective-permute-done.1.a2_ref, ...), custom_call_target="tpu_custom_call" | custom-call | flops 536870912 | bytes 1048576 | tf_op jit(solution)/shard_map/pallas_call | solution.py:376
  102.7 0.5 slice_bitcast_fusion
  (3 shorter events, 0.0 us)
Async XLA Ops:
  0.6 19.7 %copy-start.4 = (bf16[1,128,1536]{2,1,0:T(8,128)(2,1)S(1)}, bf16[1,128,1536]{2,1,0:T(8,128)(2,1)}, u32[]{:S(2)}) copy-start(bf16[1,128,1536]{2,1,0:T(8,128)(2,1)} %query_ref.1) | copy-start | bytes 1179652
  0.6 19.7 %copy-start.5 = (bf16[1,128,1536]{2,1,0:T(8,128)(2,1)S(1)}, bf16[1,128,1536]{2,1,0:T(8,128)(2,1)}, u32[]{:S(2)}) copy-start(bf16[1,128,1536]{2,1,0:T(8,128)(2,1)} %key_ref.1) | copy-start | bytes 1179652
  3.7 32.5 %collective-permute-start.2 = (bf16[264,1536]{1,0:T(8,128)(2,1)}, bf16[264,1536]{1,0:T(8,128)(2,1)S(1)}, u32[]{:S(2)}, u32[]{:S(2)}) collective-permute-start(bf16[264,1536]{1,0:T(8,128)(2,1)} %get-tuple-element.31.b_ref), channel_id=1, source_target_pairs={{0,496},{16,32},{32,16},{48,64},{64,48},{80,96},{96,80},{112,128},... | collective-permute-start | bytes 2433032 | tf_op jit(solution)/shard_map/ppermute | solution.py:402
  18.3 2.1 %copy-start.10 = (s32[1,64]{1,0:T(1,128)S(1)}, s32[1,64]{1,0:T(1,128)}, u32[]{:S(2)}) copy-start(s32[1,64]{1,0:T(1,128)} %reach_ref.1) | copy-start | bytes 772
  18.3 2.1 %copy-start.8 = (s32[1,32,2]{1,2,0:T(2,128)S(1)}, s32[1,32,2]{1,2,0:T(2,128)}, u32[]{:S(2)}) copy-start(s32[1,32,2]{1,2,0:T(2,128)} %param.19) | copy-start | bytes 772
  18.3 2.1 %copy-start.9 = (s32[1,32]{1,0:T(1,128)S(1)}, s32[1,32]{1,0:T(1,128)}, u32[]{:S(2)}) copy-start(s32[1,32]{1,0:T(1,128)} %counts_ref.1) | copy-start | bytes 388
  18.3 20.9 %collective-permute-start = (bf16[264,1536]{1,0:T(8,128)(2,1)}, bf16[264,1536]{1,0:T(8,128)(2,1)S(1)}, u32[]{:S(2)}, u32[]{:S(2)}) collective-permute-start(bf16[264,1536]{1,0:T(8,128)(2,1)} %get-tuple-element.30.a_ref), channel_id=1, source_target_pairs={{0,16},{16,0},{32,48},{48,32},{64,80},{80,64},{96,112},{112,96},{1... | collective-permute-start | bytes 2433032 | tf_op jit(solution)/shard_map/ppermute | solution.py:402
  20.4 1.1 %copy-start = (bf16[264,1536]{1,0:T(8,128)(2,1)S(1)}, bf16[264,1536]{1,0:T(8,128)(2,1)}, u32[]{:S(2)}) copy-start(bf16[264,1536]{1,0:T(8,128)(2,1)} %get-tuple-element.30.a_ref) | copy-start | bytes 2433028
  21.6 1.1 %copy-start.2 = (bf16[264,1536]{1,0:T(8,128)(2,1)S(1)}, bf16[264,1536]{1,0:T(8,128)(2,1)}, u32[]{:S(2)}) copy-start(bf16[264,1536]{1,0:T(8,128)(2,1)} %get-tuple-element.31.b_ref) | copy-start | bytes 2433028
  36.3 20.2 %collective-permute-start.3 = (bf16[264,1536]{1,0:T(8,128)(2,1)S(1)}, bf16[264,1536]{1,0:T(8,128)(2,1)S(1)}, u32[]{:S(2)}, u32[]{:S(2)}) collective-permute-start(bf16[264,1536]{1,0:T(8,128)(2,1)S(1)} %collective-permute-done.2.b1_ref), channel_id=1, source_target_pairs={{0,16},{16,0},{32,48},{48,32},{64,80},{80,64},{96,112},{112,96},{1... | collective-permute-start | bytes 2433032 | tf_op jit(solution)/shard_map/ppermute | solution.py:402
  39.2 6.1 %copy-start.1 = (bf16[264,1536]{1,0:T(8,128)(2,1)S(1)}, bf16[264,1536]{1,0:T(8,128)(2,1)}, u32[]{:S(2)}) copy-start(bf16[264,1536]{1,0:T(8,128)(2,1)} %get-tuple-element.30.a_ref) | copy-start | bytes 2433028
  39.2 6.2 %copy-start.3 = (bf16[264,1536]{1,0:T(8,128)(2,1)S(1)}, bf16[264,1536]{1,0:T(8,128)(2,1)}, u32[]{:S(2)}) copy-start(bf16[264,1536]{1,0:T(8,128)(2,1)} %get-tuple-element.31.b_ref) | copy-start | bytes 2433028
  39.2 23.9 %collective-permute-start.1 = (bf16[264,1536]{1,0:T(8,128)(2,1)S(1)}, bf16[264,1536]{1,0:T(8,128)(2,1)S(1)}, u32[]{:S(2)}, u32[]{:S(2)}) collective-permute-start(bf16[264,1536]{1,0:T(8,128)(2,1)S(1)} %shard_map.148.a1_ref), channel_id=1, source_target_pairs={{0,496},{16,32},{32,16},{48,64},{64,48},{80,96},{96,80},{112,128},... | collective-permute-start | bytes 2433032 | tf_op jit(solution)/shard_map/ppermute | solution.py:402
  56.5 41.1 %collective-permute-start.5 = (bf16[264,1536]{1,0:T(8,128)(2,1)S(1)}, bf16[264,1536]{1,0:T(8,128)(2,1)S(1)}, u32[]{:S(2)}, u32[]{:S(2)}) collective-permute-start(bf16[264,1536]{1,0:T(8,128)(2,1)S(1)} %shard_map.150.b2_ref), channel_id=1, source_target_pairs={{0,496},{16,32},{32,16},{48,64},{64,48},{80,96},{96,80},{112,128},... | collective-permute-start | bytes 2433032 | tf_op jit(solution)/shard_map/ppermute | solution.py:402
  63.1 34.5 %collective-permute-start.4 = (bf16[264,1536]{1,0:T(8,128)(2,1)S(1)}, bf16[264,1536]{1,0:T(8,128)(2,1)S(1)}, u32[]{:S(2)}, u32[]{:S(2)}) collective-permute-start(bf16[264,1536]{1,0:T(8,128)(2,1)S(1)} %collective-permute-done.1.a2_ref), channel_id=1, source_target_pairs={{0,16},{16,0},{32,48},{48,32},{64,80},{80,64},{96,112},{112,96},{1... | collective-permute-start | bytes 2433032 | tf_op jit(solution)/shard_map/ppermute | solution.py:402
  65.0 0.7 copy-start.6
  65.1 0.7 copy-start.7

commit v4 on v3

--- a/solution.py
+++ b/solution.py
@@ -22,6 +22,8 @@
 SCALE = WIDTH**-0.5
 CLOSED = -1e30
 norm_eps = 1e-06
+LAST_GROUPS = 3
+LAST_LIMIT = 60 << 20
 
 f32 = jnp.float32
 bf16 = jnp.bfloat16
@@ -226,11 +228,12 @@
 
 
 def own_kernel(
-    blocks_ref, counts_ref, reach_ref, a_ref, b_ref, query_ref, key_ref,
+    blocks_ref, counts_ref, reach_ref, a_ref, b_ref, query_ref, key_ref, qgain_ref, kgain_ref,
     dq_ref, dk_ref, dv_ref, bias_ref, query_unit_ref, query_inverse_ref, key_unit_ref, key_inverse_ref,
-    two_ref, three_ref, dot_ref,
+    two_ref, three_ref, dot_ref, gains_ref,
 ):
     fill_bias(blocks_ref, counts_ref, reach_ref, bias_ref)
+    gains_ref[...] = jnp.concatenate([qgain_ref[...], kgain_ref[...]], axis=0)
 
     def run(up_ref, down_ref):
         def one_head(h):
@@ -287,7 +290,7 @@
 
 def terms_kernel(
     copies, a_ref, b_ref, a1_ref, b1_ref, a2_ref, b2_ref, dq_in, dk_ref,
-    query_unit_ref, key_unit_ref, qgain_ref, kgain_ref, two_ref, dot_ref, next_three_ref, next_dot_ref,
+    query_unit_ref, key_unit_ref, gains_ref, two_ref, dot_ref, next_three_ref, next_dot_ref,
     dq_ref, terms_ref,
 ):
     def run(up_ref, down_ref, up1_ref, down1_ref, up2_ref, down2_ref):
@@ -311,8 +314,8 @@
 
         none = jnp.zeros((1, WIDTH), f32)
         for_query, for_key, two, three = lax.fori_loop(0, HEADS, one_head, (none,) * 4, unroll=HEADS)
-        for_query = for_query + three / qgain_ref[...]
-        for_key = for_key + (two + three) / kgain_ref[...]
+        for_query = for_query + three / gains_ref[0:1]
+        for_key = for_key + (two + three) / gains_ref[1:2]
         both = jnp.concatenate([for_query, for_key], axis=0) * SCALE
         terms_ref[...] = jnp.broadcast_to(both[None], (copies, 2, WIDTH))
 
@@ -325,20 +328,52 @@
 
 
 def last_kernel(
-    divisor, a_ref, b_ref, a2_ref, b2_ref, a3_ref, b3_ref, bias_ref, dq_in, dk_in, dv_in,
-    query_unit_ref, query_inverse_ref, key_unit_ref, key_inverse_ref, qgain_ref, kgain_ref,
-    three_ref, dot_ref, parts_ref,
-    query_grad_ref, key_grad_ref, value_grad_ref, gains_ref,
-):
-    gains_ref[...] = jnp.sum(parts_ref[...], axis=0) / divisor
-
-    def run(up_ref, down_ref, up2_ref, down2_ref, up3_ref, down3_ref):
+    a_hbm, b_hbm, a2_hbm, b2_hbm, a3_hbm, b3_hbm, bias_hbm, gains_hbm,
+    dq_hbm, dk_hbm, dv_hbm, query_unit_hbm, query_inverse_hbm, key_unit_hbm, key_inverse_hbm,
+    three_hbm, dot_hbm, sums_ref,
+    query_grad_ref, key_grad_ref, value_grad_ref, token_ref,
+    *scratch,
+):
+    (
+        up_ref, down_ref, down2_ref, up3_ref, down3_ref,
+        dq_in, dk_in, dv_in, query_unit_ref, query_inverse_ref, key_unit_ref, key_inverse_ref,
+        three_ref, dot_ref, bias_ref, gains_ref, sems,
+    ) = scratch
+    token_ref[...] = jnp.zeros(token_ref.shape, f32)
+
+    def run(up_hbm, down_hbm, up2_hbm, down2_hbm, up3_hbm, down3_hbm):
+        small = [
+            pltpu.make_async_copy(bias_hbm, bias_ref, sems.at[LAST_GROUPS, 0]),
+            pltpu.make_async_copy(gains_hbm, gains_ref, sems.at[LAST_GROUPS, 1]),
+        ]
+        wide = [
+            (up_hbm, up_ref), (down_hbm, down_ref), (up3_hbm, up3_ref),
+            (three_hbm, three_ref), (dot_hbm, dot_ref), (dq_hbm, dq_in),
+            (query_unit_hbm, query_unit_ref), (query_inverse_hbm, query_inverse_ref),
+            (down2_hbm, down2_ref), (down3_hbm, down3_ref), (dk_hbm, dk_in),
+            (key_unit_hbm, key_unit_ref), (key_inverse_hbm, key_inverse_ref), (dv_hbm, dv_in),
+        ]
+        each = HEADS // LAST_GROUPS
+        moves = []
+        for group in range(LAST_GROUPS):
+            lanes = slice(group * each * WIDTH, (group + 1) * each * WIDTH)
+            moves.append(
+                [
+                    pltpu.make_async_copy(hbm.at[:, lanes], ref.at[:, lanes], sems.at[group, i])
+                    for i, (hbm, ref) in enumerate(wide)
+                ]
+            )
+        for move in small + sum(moves, []):
+            move.start()
+        for move in small:
+            move.wait()
+
         def one_head(h):
-            lanes = head_lanes(h)
+            lanes = slice(h * WIDTH, (h + 1) * WIDTH)
             part, _ = grad_query_core(up3_ref, [(down_ref, three_ref, dot_ref)], lanes)
             total = dq_in[:, lanes] + part
             query_grad_ref[0, :, lanes] = norm_back(
-                total, query_unit_ref[:, lanes], query_inverse_ref[:, lanes], qgain_ref[...]
+                total, query_unit_ref[:, lanes], query_inverse_ref[:, lanes], gains_ref[0:1]
             )
             weights, grad_scores, queries, cotangents = pair_core(
                 up_ref,
@@ -347,14 +382,18 @@
             )
             total = dk_in[:, lanes] + dot_nn(grad_scores, queries)
             key_grad_ref[0, :, lanes] = norm_back(
-                total, key_unit_ref[:, lanes], key_inverse_ref[:, lanes], kgain_ref[...]
+                total, key_unit_ref[:, lanes], key_inverse_ref[:, lanes], gains_ref[1:2]
             )
             total = dv_in[:, lanes] + dot_nn(weights, cotangents)
             value_grad_ref[0, :, lanes] = total.astype(bf16)
 
-        over_heads(one_head)
-
-    by_parity(run, (a_ref, b_ref, 0), (a2_ref, b2_ref, 2), (a3_ref, b3_ref, 3))
+        for group in range(LAST_GROUPS):
+            for move in moves[group]:
+                move.wait()
+            for h in range(group * each, (group + 1) * each):
+                one_head(h)
+
+    by_parity(run, (a_hbm, b_hbm, 0), (a2_hbm, b2_hbm, 2), (a3_hbm, b3_hbm, 3))
 
 
 def sum_kernel(parts_ref, out_ref):
@@ -362,8 +401,15 @@
     out_ref[...] = jnp.broadcast_to(total[None], out_ref.shape)
 
 
-def tie_kernel(chain_ref, token_ref, out_ref):
-    pass
+def total_kernel(divisor, parts_ref, token_ref, query_gain_grad_ref, key_gain_grad_ref):
+    total = jnp.sum(parts_ref[...], axis=0) / divisor
+    query_gain_grad_ref[...] = total[0:1]
+    key_gain_grad_ref[...] = total[1:2]
+
+
+def tie_kernel(chain_ref, token_ref, out_ref, *given):
+    for ref in given:
+        ref[...] = jnp.zeros(ref.shape, ref.dtype)
 
 
 VMEM = pl.BlockSpec(memory_space=pltpu.VMEM)
@@ -431,11 +477,14 @@
         limit=62 << 20,
     )
     a1, b1 = swapped(a, 0), swapped(b, 1)
-    dq, dk, dv, bias, *units, two, three, dots = call(
+    dq, dk, dv, bias, *units, two, three, dots, gains = call(
         own_kernel,
-        (total, total, total, lines) + (total,) * 7,
-        [SMEM] * 3 + [VMEM] * 4,
-        (jnp.swapaxes(route_blocks, 1, 2), route_count, query_reach, a, b, query_raw, key_raw),
+        (total, total, total, lines) + (total,) * 7 + (jax.ShapeDtypeStruct((2, WIDTH), f32),),
+        [SMEM] * 3 + [VMEM] * 6,
+        (
+            jnp.swapaxes(route_blocks, 1, 2), route_count, query_reach,
+            a, b, query_raw, key_raw, qgain, kgain,
+        ),
     )
     a1 = after(a1, bias)
     a2, b2 = swapped(a1, 1), swapped(b1, 0)
@@ -459,9 +508,9 @@
     dq, terms = call(
         functools.partial(terms_kernel, len(first[0])),
         (total, jax.ShapeDtypeStruct((len(first[0]), 2, WIDTH), f32)),
-        [VMEM] * 16,
+        [VMEM] * 15,
         (
-            a, b, a1, b1, a2, b2, dq, dk, units[0], units[2], qgain, kgain,
+            a, b, a1, b1, a2, b2, dq, dk, units[0], units[2], gains,
             two, dots, next_three, next_dots,
         ),
         {6: 0},
@@ -472,16 +521,25 @@
     )
     parts = lax.all_to_all(sums, ("tm", "dp"), 0, 0, axis_index_groups=second)
     row = jax.ShapeDtypeStruct((1, CAP, HD), bf16)
-    query_grad, key_grad, value_grad, gains = call(
-        functools.partial(last_kernel, shards * clips),
-        (row, row, row, jax.ShapeDtypeStruct((2, WIDTH), f32)),
-        [VMEM] * 19,
-        (
-            a, b, a2, b2, a3, b3, bias, dq, dk, dv, *units, qgain, kgain,
-            three, dots, parts,
-        ),
-    )
-    return (query_grad, key_grad, value_grad, gains[0], gains[1])
+    query_grad, key_grad, value_grad, token = call(
+        last_kernel,
+        (row, row, row, jax.ShapeDtypeStruct((8, WIDTH), f32)),
+        [HBM] * 17 + [VMEM],
+        (a, b, a2, b2, a3, b3, bias, gains, dq, dk, dv, *units, three, dots, sums),
+        scratch=[pltpu.VMEM((ROWS, HD), bf16)] * 5 + [pltpu.VMEM((CAP, HD), f32)] * 9
+        + [pltpu.VMEM((24, CAP), f32), pltpu.VMEM((2, WIDTH), f32)]
+        + [pltpu.SemaphoreType.DMA((LAST_GROUPS + 1, 14))],
+        limit=LAST_LIMIT,
+    )
+    gain = jax.ShapeDtypeStruct((1, WIDTH), f32)
+    query_gain_grad, key_gain_grad = call(
+        functools.partial(total_kernel, shards * clips),
+        (gain, gain),
+        [VMEM, VMEM],
+        (parts, token),
+        limit=1 << 20,
+    )
+    return (query_grad, key_grad, value_grad, query_gain_grad[0], key_gain_grad[0])
 
 
 def solution(mesh):

time: 104 us -> 101 us (0.971)
  blocking collectives: 29.7 us -> 11.8 us
  starting transfers between devices: 33.2 us -> 40.4 us
  Pallas kernels: 18.6 us -> 24.8 us
  local copies, waits for them, and re-layouts: 3.49 us -> 6.39 us
  waiting for transfers between devices: 17.4 us -> 16 us
    all_to_all x1 -> x0, blocking collectives: 18 us -> none  [body(): parts = lax.all_to_all(sums, ('tm', 'dp'), 0, 0, axis_index_groups=second)]
    all_to_all x0 -> x1, starting transfers between devices: none -> 7.24 us  [body(): parts = lax.all_to_all(sums, ('tm', 'dp'), 0, 0, axis_index_groups=second)]
    pallas_call x6 -> x7, Pallas kernels: 18.6 us -> 24.8 us  [call(): pl.pallas_call(kernel, out_shape=tuple(outs), in_specs=specs, out_specs=(...]
    unnamed x22 -> x48, local copies, waits for them, and re-layouts: 2.97 us -> 6.39 us
    ppermute x6, waiting for transfers between devices: 17.4 us -> 14.1 us  [swapped(): return lax.ppermute(value, 'tm', pairs)]
    all_to_all x0 -> x1, waiting for transfers between devices: none -> 1.84 us  [body(): parts = lax.all_to_all(sums, ('tm', 'dp'), 0, 0, axis_index_groups=second)]
  transfers between devices with their start and end apart: 6 -> 7, of which waited for: 3 -> 4; matrix products, arithmetic and copies ran while one was open for 0% -> 0% of each run, Pallas kernels for 10% -> 21%
where the time goes in v4:
time: 101 us; the launch traced here: 100 us
  starting transfers between devices  40.4 us (40%)
  Pallas kernels  24.8 us (25%)
  waiting for transfers between devices  16 us (16%)
  blocking collectives  11.8 us (12%)
  local copies, waits for them, and re-layouts  6.39 us (6%)
    ppermute x6, starting transfers between devices, swapped(): return lax.ppermute(value, 'tm', pairs)  33.2 us
    pallas_call x7, Pallas kernels, call(): pl.pallas_call(kernel, out_shape=tuple(outs), in_specs=specs, out_specs=(...  24.8 us
    ppermute x6, waiting for transfers between devices, swapped(): return lax.ppermute(value, 'tm', pairs)  14.1 us
    all_to_all x1, blocking collectives, body(): parts = lax.all_to_all(terms, 'dp', 0, 0, axis_index_groups=first)  11.8 us
    all_to_all x1, starting transfers between devices, body(): parts = lax.all_to_all(sums, ('tm', 'dp'), 0, 0, axis_index_groups=second)  7.24 us
    unnamed x48, local copies, waits for them, and re-layouts  6.39 us
  transfers between devices with their start and end apart: 7, of which 4 were waited for; matrix products, arithmetic and copies ran while one was open for 0% of the time, Pallas kernels for 21%

profile of v4, /device:TPU:1, one launch (start us, length us, event | category | flops | bytes accessed | tf_op | source)
XLA Modules:
  0.0 100.3 jit_solution(15227597002304690623)
XLA Ops:
  0.6 0.0 copy-start.14
  0.6 0.0 copy-start.15
  0.7 3.1 %shard_map.146 = (bf16[264,1536]{1,0:T(8,128)(2,1)}, bf16[264,1536]{1,0:T(8,128)(2,1)}) custom-call(bf16[1,128,1536]{2,1,0:T(8,128)(2,1)} %query_ref.1, bf16[1,128,1536]{2,1,0:T(8,128)(2,1)} %key_ref.1, bf16[1,128,1536]{2,1,0:T(8,128)(2,1)} %value_hbm.1, bf16[1,128,1536]{2,1,0:T(8,128)(2,1)} %grad_hbm.1, f32[12,1,128]{2,1,0:T(1,128)} %bitcast.12, ...), custom_call_target="tpu_custom_call" | custom-call | flops 536870912 | bytes 1048576 | tf_op jit(solution)/shard_map/pallas_call | solution.py:422
  3.7 14.5 %collective-permute-start.2 = (bf16[264,1536]{1,0:T(8,128)(2,1)}, bf16[264,1536]{1,0:T(8,128)(2,1)S(1)}, u32[]{:S(2)}, u32[]{:S(2)}) collective-permute-start(bf16[264,1536]{1,0:T(8,128)(2,1)} %get-tuple-element.34.b_ref.b_hbm), channel_id=1, source_target_pairs={{0,496},{16,32},{32,16},{48,64},{64,48},{80,96},{96,80},{112,128},... | collective-permute-start | bytes 2433032 | tf_op jit(solution)/shard_map/ppermute | solution.py:448
  18.3 0.0 copy-start.20
  18.3 0.0 copy-start.21
  18.3 0.0 copy-start.22
  18.3 0.0 copy-start.18
  18.3 0.0 copy-start.19
  18.3 2.1 %collective-permute-start = (bf16[264,1536]{1,0:T(8,128)(2,1)}, bf16[264,1536]{1,0:T(8,128)(2,1)S(1)}, u32[]{:S(2)}, u32[]{:S(2)}) collective-permute-start(bf16[264,1536]{1,0:T(8,128)(2,1)} %get-tuple-element.33.a_ref.a_hbm), channel_id=1, source_target_pairs={{0,16},{16,0},{32,48},{48,32},{64,80},{80,64},{96,112},{112,96},{1... | collective-permute-start | bytes 2433032 | tf_op jit(solution)/shard_map/ppermute | solution.py:448
  20.4 0.0 copy-done.14
  20.4 0.0 copy-done.15
  20.4 0.0 copy-done.20
  20.4 0.0 copy-done.21
  20.4 0.0 copy-done.22
  20.5 0.0 copy-done.18
  20.5 0.0 copy-done.19
  20.5 0.0 copy-start
  20.5 1.1 %copy-done = bf16[264,1536]{1,0:T(8,128)(2,1)S(1)} copy-done((bf16[264,1536]{1,0:T(8,128)(2,1)S(1)}, bf16[264,1536]{1,0:T(8,128)(2,1)}, u32[]{:S(2)}) %copy-start) | copy-done | bytes 811032
  21.6 1.1 %copy-done.2 = bf16[264,1536]{1,0:T(8,128)(2,1)S(1)} copy-done((bf16[264,1536]{1,0:T(8,128)(2,1)S(1)}, bf16[264,1536]{1,0:T(8,128)(2,1)}, u32[]{:S(2)}) %copy-start.2) | copy-done | bytes 811032
  22.8 3.6 %shard_map.147 = (f32[128,1536]{1,0:T(8,128)S(1)}, f32[128,1536]{1,0:T(8,128)S(1)}, f32[128,1536]{1,0:T(8,128)S(1)}, f32[24,128]{1,0:T(8,128)S(1)}, f32[128,1536...) custom-call(s32[1,2,32]{2,1,0:T(2,128)S(1)} %bitcast.7, ...), custom_call_target="tpu_custom_call" | custom-call | flops 536870912 | bytes 1048576 | tf_op jit(solution)/shard_map/pallas_call | solution.py:422
  26.4 0.0 copy-start.11
  26.4 1.0 copy-done.11
  27.4 0.9 copy-done.12
  28.3 0.9 copy-done.13
  29.2 7.1 %collective-permute-done.2.b1_ref = bf16[264,1536]{1,0:T(8,128)(2,1)S(1)} collective-permute-done((bf16[264,1536]{1,0:T(8,128)(2,1)}, bf16[264,1536]{1,0:T(8,128)(2,1)S(1)}, u32[]{:S(2)}, u32[]{:S(2)}) %collective-permute-start.2) | collective-permute-done | bytes 811040 | tf_op jit(solution)/shard_map/ppermute | solution.py:448
  36.3 1.9 %collective-permute-start.3 = (bf16[264,1536]{1,0:T(8,128)(2,1)S(1)}, bf16[264,1536]{1,0:T(8,128)(2,1)S(1)}, u32[]{:S(2)}, u32[]{:S(2)}) collective-permute-start(bf16[264,1536]{1,0:T(8,128)(2,1)S(1)} %collective-permute-done.2.b1_ref), channel_id=1, source_target_pairs={{0,16},{16,0},{32,48},{48,32},{64,80},{80,64},{96,112},{112,96},{1... | collective-permute-start | bytes 2433032 | tf_op jit(solution)/shard_map/ppermute | solution.py:448
  38.2 1.0 %collective-permute-done.chain_ref = bf16[264,1536]{1,0:T(8,128)(2,1)S(1)} collective-permute-done((bf16[264,1536]{1,0:T(8,128)(2,1)}, bf16[264,1536]{1,0:T(8,128)(2,1)S(1)}, u32[]{:S(2)}, u32[]{:S(2)}) %collective-permute-start) | collective-permute-done | bytes 811040 | tf_op jit(solution)/shard_map/ppermute | solution.py:448
  39.2 6.1 %collective-permute-start.1 = (bf16[264,1536]{1,0:T(8,128)(2,1)S(1)}, bf16[264,1536]{1,0:T(8,128)(2,1)}, u32[]{:S(2)}, u32[]{:S(2)}) collective-permute-start(bf16[264,1536]{1,0:T(8,128)(2,1)S(1)} %shard_map.148.a1_ref), channel_id=1, source_target_pairs={{0,496},{16,32},{32,16},{48,64},{64,48},{80,96},{96,80},{112,128},... | collective-permute-start | bytes 2433032 | tf_op jit(solution)/shard_map/ppermute | solution.py:448
  45.3 0.0 copy-done.1
  45.3 0.0 copy-done.3
  45.3 4.6 %shard_map.149 = (f32[128,1536]{1,0:T(8,128)S(1)}, f32[128,1536]{1,0:T(8,128)S(1)}, f32[128,1536]{1,0:T(8,128)S(1)}, f32[24,128]{1,0:T(8,128)S(1)}, f32[128,1536]{1,0:T(8,128)S(1)}, /*index=5*/f32[128,1536]{1,0:T(8,128)S(1)}) custom-call(bf16[264,1536]{1,0:T(8,128)(2,1)S(1)} %copy-done.1, ...), custom_call_target="tpu_custom_call", output_to_operand_aliasing={{0}: (5, {}), {1}: (6, {}), {2}: (7, {})} | custom-call | flops 536870912 | bytes 1048576 | tf_op jit(solution)/shard_map/pallas_call | solution.py:422
  50.0 0.0 copy-start.16
  50.0 0.6 copy-done.16
  50.6 6.0 %collective-permute-done.3.chain_ref = bf16[264,1536]{1,0:T(8,128)(2,1)S(1)} collective-permute-done((bf16[264,1536]{1,0:T(8,128)(2,1)S(1)}, bf16[264,1536]{1,0:T(8,128)(2,1)S(1)}, u32[]{:S(2)}, u32[]{:S(2)}) %collective-permute-start.3) | collective-permute-done | bytes 811040 | tf_op jit(solution)/shard_map/ppermute | solution.py:448
  56.6 6.6 %collective-permute-start.5 = (bf16[264,1536]{1,0:T(8,128)(2,1)S(1)}, bf16[264,1536]{1,0:T(8,128)(2,1)}, u32[]{:S(2)}, u32[]{:S(2)}) collective-permute-start(bf16[264,1536]{1,0:T(8,128)(2,1)S(1)} %shard_map.150.b2_ref.b2_hbm), channel_id=1, source_target_pairs={{0,496},{16,32},{32,16},{48,64},{64,48},{80,96},{96,80},{112,128},... | collective-permute-start | bytes 2433032 | tf_op jit(solution)/shard_map/ppermute | solution.py:448
  63.2 0.0 collective-permute-done.1.a2_ref.a2_hbm
  63.2 1.9 %collective-permute-start.4 = (bf16[264,1536]{1,0:T(8,128)(2,1)}, bf16[264,1536]{1,0:T(8,128)(2,1)}, u32[]{:S(2)}, u32[]{:S(2)}) collective-permute-start(bf16[264,1536]{1,0:T(8,128)(2,1)} %collective-permute-done.1.a2_ref.a2_hbm), channel_id=1, source_target_pairs={{0,16},{16,0},{32,48},{48,32},{64,80},{80,64},{96,112},{112,96},{1... | collective-permute-start | bytes 2433032 | tf_op jit(solution)/shard_map/ppermute | solution.py:448
  65.2 3.3 %shard_map.151 = (f32[128,1536]{1,0:T(8,128)S(1)}, f32[8,2,128]{2,1,0:T(2,128)S(1)}) custom-call(bf16[264,1536]{1,0:T(8,128)(2,1)S(1)} %copy-done.1, bf16[264,1536]{1,0:T(8,128)(2,1)S(1)} %copy-done.3, bf16[264,1536]{1,0:T(8,128)(2,1)S(1)} %shard_map.148.a1_ref, ...), custom_call_target="tpu_custom_call", output_to_operand_aliasing={{0}: (6, {})} | custom-call | flops 536870912 | bytes 1048576 | tf_op jit(solution)/shard_map/pallas_call | solution.py:422
  68.5 11.8 %all_to_all.10.parts_ref = f32[8,2,128]{2,1,0:T(2,128)S(1)} all-to-all(f32[8,2,128]{2,1,0:T(2,128)S(1)} %get-tuple-element.54), channel_id=1, replica_groups={{0,1,4,5,8,9,12,13},{2,3,6,7,10,11,14,15},{16,17,20,21,24,25,28,29},{18..., dimensions={0} | all-to-all | bytes 16384 | tf_op jit(solution)/shard_map/all_to_all | solution.py:518
  80.3 0.6 shard_map.152.sums_ref
  80.9 7.2 %all-to-all-start.1 = ((f32[64,2,128]{2,1,0:T(2,128)}), f32[64,2,128]{2,1,0:T(2,128)S(1)}, u32[]{:S(2)}, u32[]{:S(2)}) async-start(f32[64,2,128]{2,1,0:T(2,128)} %shard_map.152.sums_ref), calls=%async_computation.1 | async-start | bytes 131072 | tf_op jit(solution)/shard_map/all_to_all | solution.py:522
  88.2 0.0 collective-permute-done.5.b3_hbm
  88.2 0.0 collective-permute-done.4.a3_hbm
  88.2 9.0 %shard_map.153 = (bf16[1,128,1536]{2,1,0:T(8,128)(2,1)}, bf16[1,128,1536]{2,1,0:T(8,128)(2,1)}, bf16[1,128,1536]{2,1,0:T(8,128)(2,1)}, f32[8,128]{1,0:T(8,128)}) custom-call(bf16[264,1536]{1,0:T(8,128)(2,1)} %get-tuple-element.33.a_ref.a_hbm, bf16[264,1536]{1,0:T(8,128)(2,1)} %get-tuple-element.34.b_ref.b_hbm, ...), custom_call_target="tpu_custom_call" | custom-call | flops 536870912 | bytes 1048576 | tf_op jit(solution)/shard_map/pallas_call | solution.py:422
  97.2 1.8 %all-to-all-done.1.parts_ref = f32[64,2,128]{2,1,0:T(2,128)S(1)} async-done(((f32[64,2,128]{2,1,0:T(2,128)}), f32[64,2,128]{2,1,0:T(2,128)S(1)}, u32[]{:S(2)}, u32[]{:S(2)}) %all-to-all-start.1) | async-done | bytes 65568 | tf_op jit(solution)/shard_map/all_to_all | solution.py:522
  99.0 0.7 copy-done.23
  99.7 0.6 shard_map.154
  (24 shorter events, 0.0 us)
Async XLA Ops:
  0.6 19.8 %copy-start.14 = (bf16[1,128,1536]{2,1,0:T(8,128)(2,1)S(1)}, bf16[1,128,1536]{2,1,0:T(8,128)(2,1)}, u32[]{:S(2)}) copy-start(bf16[1,128,1536]{2,1,0:T(8,128)(2,1)} %query_ref.1) | copy-start | bytes 1179652
  0.6 19.8 %copy-start.15 = (bf16[1,128,1536]{2,1,0:T(8,128)(2,1)S(1)}, bf16[1,128,1536]{2,1,0:T(8,128)(2,1)}, u32[]{:S(2)}) copy-start(bf16[1,128,1536]{2,1,0:T(8,128)(2,1)} %key_ref.1) | copy-start | bytes 1179652
  3.7 32.5 %collective-permute-start.2 = (bf16[264,1536]{1,0:T(8,128)(2,1)}, bf16[264,1536]{1,0:T(8,128)(2,1)S(1)}, u32[]{:S(2)}, u32[]{:S(2)}) collective-permute-start(bf16[264,1536]{1,0:T(8,128)(2,1)} %get-tuple-element.34.b_ref.b_hbm), channel_id=1, source_target_pairs={{0,496},{16,32},{32,16},{48,64},{64,48},{80,96},{96,80},{112,128},... | collective-permute-start | bytes 2433032 | tf_op jit(solution)/shard_map/ppermute | solution.py:448
  18.3 2.1 %copy-start.20 = (f32[128]{0:T(128)S(1)}, f32[128]{0:T(128)}, u32[]{:S(2)}) copy-start(f32[128]{0:T(128)} %param.18) | copy-start | bytes 1540
  18.3 2.1 %copy-start.21 = (s32[1,32]{1,0:T(1,128)S(1)}, s32[1,32]{1,0:T(1,128)}, u32[]{:S(2)}) copy-start(s32[1,32]{1,0:T(1,128)} %counts_ref.1) | copy-start | bytes 388
  18.3 2.1 %copy-start.22 = (s32[1,64]{1,0:T(1,128)S(1)}, s32[1,64]{1,0:T(1,128)}, u32[]{:S(2)}) copy-start(s32[1,64]{1,0:T(1,128)} %reach_ref.1) | copy-start | bytes 772
  18.3 2.1 %copy-start.18 = (s32[1,32,2]{1,2,0:T(2,128)S(1)}, s32[1,32,2]{1,2,0:T(2,128)}, u32[]{:S(2)}) copy-start(s32[1,32,2]{1,2,0:T(2,128)} %param.19) | copy-start | bytes 772
  18.3 2.1 %copy-start.19 = (f32[128]{0:T(128)S(1)}, f32[128]{0:T(128)}, u32[]{:S(2)}) copy-start(f32[128]{0:T(128)} %param.17) | copy-start | bytes 1540
  18.3 20.9 %collective-permute-start = (bf16[264,1536]{1,0:T(8,128)(2,1)}, bf16[264,1536]{1,0:T(8,128)(2,1)S(1)}, u32[]{:S(2)}, u32[]{:S(2)}) collective-permute-start(bf16[264,1536]{1,0:T(8,128)(2,1)} %get-tuple-element.33.a_ref.a_hbm), channel_id=1, source_target_pairs={{0,16},{16,0},{32,48},{48,32},{64,80},{80,64},{96,112},{112,96},{1... | collective-permute-start | bytes 2433032 | tf_op jit(solution)/shard_map/ppermute | solution.py:448
  20.5 1.1 %copy-start = (bf16[264,1536]{1,0:T(8,128)(2,1)S(1)}, bf16[264,1536]{1,0:T(8,128)(2,1)}, u32[]{:S(2)}) copy-start(bf16[264,1536]{1,0:T(8,128)(2,1)} %get-tuple-element.33.a_ref.a_hbm) | copy-start | bytes 2433028
  21.6 1.1 %copy-start.2 = (bf16[264,1536]{1,0:T(8,128)(2,1)S(1)}, bf16[264,1536]{1,0:T(8,128)(2,1)}, u32[]{:S(2)}) copy-start(bf16[264,1536]{1,0:T(8,128)(2,1)} %get-tuple-element.34.b_ref.b_hbm) | copy-start | bytes 2433028
  26.4 1.0 copy-start.11
  27.4 0.9 copy-start.12
  28.3 0.9 copy-start.13
  29.2 36.0 %copy-start.7 = (f32[128,1536]{1,0:T(8,128)}, f32[128,1536]{1,0:T(8,128)S(1)}, u32[]{:S(2)}) copy-start(f32[128,1536]{1,0:T(8,128)S(1)} %get-tuple-element.43.query_unit_ref.query_unit_hbm) | copy-start | bytes 2359300
  29.2 36.0 %copy-start.8 = (f32[128,1536]{1,0:T(8,128)}, f32[128,1536]{1,0:T(8,128)S(1)}, u32[]{:S(2)}) copy-start(f32[128,1536]{1,0:T(8,128)S(1)} %get-tuple-element.44.key_unit_ref.key_unit_hbm) | copy-start | bytes 2359300
  29.2 36.0 %copy-start.9 = (f32[128,1536]{1,0:T(8,128)}, f32[128,1536]{1,0:T(8,128)S(1)}, u32[]{:S(2)}) copy-start(f32[128,1536]{1,0:T(8,128)S(1)} %get-tuple-element.46.dot_ref.dot_hbm) | copy-start | bytes 2359300
  29.2 36.0 %copy-start.17 = (f32[2,128]{1,0:T(2,128)}, f32[2,128]{1,0:T(2,128)S(1)}, u32[]{:S(2)}) copy-start(f32[2,128]{1,0:T(2,128)S(1)} %get-tuple-element.40.gains_ref.gains_hbm) | copy-start | bytes 3076
  36.3 20.3 %collective-permute-start.3 = (bf16[264,1536]{1,0:T(8,128)(2,1)S(1)}, bf16[264,1536]{1,0:T(8,128)(2,1)S(1)}, u32[]{:S(2)}, u32[]{:S(2)}) collective-permute-start(bf16[264,1536]{1,0:T(8,128)(2,1)S(1)} %collective-permute-done.2.b1_ref), channel_id=1, source_target_pairs={{0,16},{16,0},{32,48},{48,32},{64,80},{80,64},{96,112},{112,96},{1... | collective-permute-start | bytes 2433032 | tf_op jit(solution)/shard_map/ppermute | solution.py:448
  39.2 6.1 %copy-start.1 = (bf16[264,1536]{1,0:T(8,128)(2,1)S(1)}, bf16[264,1536]{1,0:T(8,128)(2,1)}, u32[]{:S(2)}) copy-start(bf16[264,1536]{1,0:T(8,128)(2,1)} %get-tuple-element.33.a_ref.a_hbm) | copy-start | bytes 2433028
  39.2 6.1 %copy-start.3 = (bf16[264,1536]{1,0:T(8,128)(2,1)S(1)}, bf16[264,1536]{1,0:T(8,128)(2,1)}, u32[]{:S(2)}) copy-start(bf16[264,1536]{1,0:T(8,128)(2,1)} %get-tuple-element.34.b_ref.b_hbm) | copy-start | bytes 2433028
  39.2 24.0 %collective-permute-start.1 = (bf16[264,1536]{1,0:T(8,128)(2,1)S(1)}, bf16[264,1536]{1,0:T(8,128)(2,1)}, u32[]{:S(2)}, u32[]{:S(2)}) collective-permute-start(bf16[264,1536]{1,0:T(8,128)(2,1)S(1)} %shard_map.148.a1_ref), channel_id=1, source_target_pairs={{0,496},{16,32},{32,16},{48,64},{64,48},{80,96},{96,80},{112,128},... | collective-permute-start | bytes 2433032 | tf_op jit(solution)/shard_map/ppermute | solution.py:448
  50.0 0.6 copy-start.16
  50.6 6.0 %copy-start.10 = (f32[128,1536]{1,0:T(8,128)}, f32[128,1536]{1,0:T(8,128)S(1)}, u32[]{:S(2)}) copy-start(f32[128,1536]{1,0:T(8,128)S(1)} %get-tuple-element.50.dv_hbm) | copy-start | bytes 2359300
  50.6 14.6 %copy-start.6 = (f32[128,1536]{1,0:T(8,128)}, f32[128,1536]{1,0:T(8,128)S(1)}, u32[]{:S(2)}) copy-start(f32[128,1536]{1,0:T(8,128)S(1)} %get-tuple-element.42.dk_ref.dk_hbm) | copy-start | bytes 2359300
  56.6 11.9 %copy-start.4 = (bf16[264,1536]{1,0:T(8,128)(2,1)}, bf16[264,1536]{1,0:T(8,128)(2,1)S(1)}, u32[]{:S(2)}) copy-start(bf16[264,1536]{1,0:T(8,128)(2,1)S(1)} %shard_map.150.b2_ref.b2_hbm) | copy-start | bytes 2433028
  56.6 31.6 %collective-permute-start.5 = (bf16[264,1536]{1,0:T(8,128)(2,1)S(1)}, bf16[264,1536]{1,0:T(8,128)(2,1)}, u32[]{:S(2)}, u32[]{:S(2)}) collective-permute-start(bf16[264,1536]{1,0:T(8,128)(2,1)S(1)} %shard_map.150.b2_ref.b2_hbm), channel_id=1, source_target_pairs={{0,496},{16,32},{32,16},{48,64},{64,48},{80,96},{96,80},{112,128},... | collective-permute-start | bytes 2433032 | tf_op jit(solution)/shard_map/ppermute | solution.py:448
  63.2 24.9 %collective-permute-start.4 = (bf16[264,1536]{1,0:T(8,128)(2,1)}, bf16[264,1536]{1,0:T(8,128)(2,1)}, u32[]{:S(2)}, u32[]{:S(2)}) collective-permute-start(bf16[264,1536]{1,0:T(8,128)(2,1)} %collective-permute-done.1.a2_ref.a2_hbm), channel_id=1, source_target_pairs={{0,16},{16,0},{32,48},{48,32},{64,80},{80,64},{96,112},{112,96},{1... | collective-permute-start | bytes 2433032 | tf_op jit(solution)/shard_map/ppermute | solution.py:448
  68.5 12.4 %copy-start.5 = (f32[128,1536]{1,0:T(8,128)}, f32[128,1536]{1,0:T(8,128)S(1)}, u32[]{:S(2)}) copy-start(f32[128,1536]{1,0:T(8,128)S(1)} %get-tuple-element.49.dq_hbm) | copy-start | bytes 2359300
  80.9 18.1 %all-to-all-start.1 = ((f32[64,2,128]{2,1,0:T(2,128)}), f32[64,2,128]{2,1,0:T(2,128)S(1)}, u32[]{:S(2)}, u32[]{:S(2)}) async-start(f32[64,2,128]{2,1,0:T(2,128)} %shard_map.152.sums_ref), calls=%async_computation.1 | async-start | bytes 131072 | tf_op jit(solution)/shard_map/all_to_all | solution.py:522
  99.0 0.7 copy-start.23

commit v5 on v4

--- a/solution.py
+++ b/solution.py
@@ -15,7 +15,7 @@
 WIDTH = 128
 CAP = ROUTE_MOST * BLK
 HD = HEADS * WIDTH
-STAT_ROWS = 8
+STAT_ROWS = 16
 ROWS = 2 * CAP + STAT_ROWS
 FIRST, SECOND, STATS = slice(0, CAP), slice(CAP, 2 * CAP), slice(2 * CAP, ROWS)
 LOG2E = 1.4426950408889634
@@ -65,23 +65,23 @@
 
 def prep_kernel(
     query_hbm, key_hbm, value_hbm, grad_hbm, log_hbm, dot_hbm, qgain_hbm, kgain_hbm,
-    a_ref, b_ref,
+    a_hbm, b_hbm,
     *scratch,
 ):
     by_parity(
-        lambda up_ref, down_ref: prepare(
+        lambda up_hbm, down_hbm: prepare(
             query_hbm, key_hbm, value_hbm, grad_hbm, log_hbm, dot_hbm, qgain_hbm, kgain_hbm,
-            up_ref, down_ref,
+            up_hbm, down_hbm,
             *scratch,
         ),
-        (a_ref, b_ref, 0),
+        (a_hbm, b_hbm, 0),
     )
 
 
 def prepare(
     query_hbm, key_hbm, value_hbm, grad_hbm, log_hbm, dot_hbm, qgain_hbm, kgain_hbm,
-    up_ref, down_ref,
-    query_ref, key_ref, log_ref, dot_ref, qgain_ref, kgain_ref, sems,
+    up_hbm, down_hbm,
+    query_ref, key_ref, log_ref, dot_ref, qgain_ref, kgain_ref, up_ref, down_ref, sems,
 ):
     moves = [
         pltpu.make_async_copy(source, target, sems.at[i])
@@ -104,7 +104,7 @@
         move.wait()
 
     def one_head(h):
-        lanes = head_lanes(h)
+        lanes = slice(h * WIDTH, (h + 1) * WIDTH)
         unit, _ = unit_of(query_ref[:, lanes])
         down_ref[FIRST, lanes] = (unit * qgain_ref[...]).astype(bf16)
         unit, _ = unit_of(key_ref[:, lanes])
@@ -116,8 +116,22 @@
         down_ref[STATS, lanes] = jnp.concatenate(parts, axis=0).astype(bf16)
         up_ref[STATS, lanes] = jnp.zeros((STAT_ROWS, CAP), bf16)
 
-    over_heads(one_head)
-    for move in moves[6:]:
+    each = HEADS // LAST_GROUPS
+    sent = []
+    for group in range(LAST_GROUPS):
+        for h in range(group * each, (group + 1) * each):
+            one_head(h)
+        if group == 0:
+            for move in moves[6:]:
+                move.wait()
+        lanes = slice(group * each * WIDTH, (group + 1) * each * WIDTH)
+        for i, (ref, hbm) in enumerate([(up_ref, up_hbm), (down_ref, down_hbm)]):
+            move = pltpu.make_async_copy(
+                ref.at[:, lanes], hbm.at[:, lanes], sems.at[8 + 2 * group + i]
+            )
+            move.start()
+            sent.append(move)
+    for move in sent:
         move.wait()
 
 
@@ -418,12 +432,14 @@
 HBM = pl.BlockSpec(memory_space=pltpu.HBM)
 
 
-def call(kernel, outs, specs, operands, aliases=None, scratch=(), limit=16 << 20):
+def call(
+    kernel, outs, specs, operands, aliases=None, scratch=(), limit=16 << 20, out_spec=None
+):
     return pl.pallas_call(
         kernel,
         out_shape=tuple(outs),
         in_specs=specs,
-        out_specs=(VMEM,) * len(outs),
+        out_specs=(out_spec or VMEM,) * len(outs),
         scratch_shapes=list(scratch),
         input_output_aliases=aliases or {},
         cost_estimate=pl.CostEstimate(flops=1 << 29, bytes_accessed=1 << 20, transcendentals=0),
@@ -472,9 +488,11 @@
             pltpu.VMEM((CAP, HD), bf16), pltpu.VMEM((CAP, HD), bf16),
             pltpu.VMEM((HEADS, 1, CAP), f32), pltpu.VMEM((HEADS, 1, CAP), f32),
             pltpu.VMEM((1, WIDTH), f32), pltpu.VMEM((1, WIDTH), f32),
-            pltpu.SemaphoreType.DMA((8,)),
+            pltpu.VMEM((ROWS, HD), bf16), pltpu.VMEM((ROWS, HD), bf16),
+            pltpu.SemaphoreType.DMA((8 + 2 * LAST_GROUPS,)),
         ),
         limit=62 << 20,
+        out_spec=HBM,
     )
     a1, b1 = swapped(a, 0), swapped(b, 1)
     dq, dk, dv, bias, *units, two, three, dots, gains = call(

time: 101 us -> 102 us (level)
  waiting for transfers between devices: 16 us -> 17.1 us
    ppermute x6, waiting for transfers between devices: 14.1 us -> 15.2 us  [swapped(): return lax.ppermute(value, 'tm', pairs)]
where the time goes in v5:
time: 102 us; the launch traced here: 101 us
  starting transfers between devices  40.4 us (40%)
  Pallas kernels  24.6 us (24%)
  waiting for transfers between devices  17.1 us (17%)
  blocking collectives  11.8 us (12%)
  local copies, waits for them, and re-layouts  6.4 us (6%)
    ppermute x6, starting transfers between devices, swapped(): return lax.ppermute(value, 'tm', pairs)  33.2 us
    pallas_call x7, Pallas kernels, call(): pl.pallas_call(kernel, out_shape=tuple(outs), in_specs=specs, out_specs=(...  24.6 us
    ppermute x6, waiting for transfers between devices, swapped(): return lax.ppermute(value, 'tm', pairs)  15.2 us
    all_to_all x1, blocking collectives, body(): parts = lax.all_to_all(terms, 'dp', 0, 0, axis_index_groups=first)  11.8 us
    all_to_all x1, starting transfers between devices, body(): parts = lax.all_to_all(sums, ('tm', 'dp'), 0, 0, axis_index_groups=second)  7.24 us
    unnamed x48, local copies, waits for them, and re-layouts  6.4 us
  transfers between devices with their start and end apart: 7, of which 4 were waited for; matrix products, arithmetic and copies ran while one was open for 0% of the time, Pallas kernels for 21%

profile of v5, /device:TPU:1, one launch (start us, length us, event | category | flops | bytes accessed | tf_op | source)
XLA Modules:
  0.0 101.2 jit_solution(10544716155687024573)
XLA Ops:
  0.6 0.0 copy-start.14
  0.6 0.0 copy-start.15
  0.7 2.9 %shard_map.146 = (bf16[272,1536]{1,0:T(8,128)(2,1)}, bf16[272,1536]{1,0:T(8,128)(2,1)}) custom-call(bf16[1,128,1536]{2,1,0:T(8,128)(2,1)} %query_ref.1, bf16[1,128,1536]{2,1,0:T(8,128)(2,1)} %key_ref.1, bf16[1,128,1536]{2,1,0:T(8,128)(2,1)} %value_hbm.1, bf16[1,128,1536]{2,1,0:T(8,128)(2,1)} %grad_hbm.1, f32[12,1,128]{2,1,0:T(1,128)} %bitcast.12, ...), custom_call_target="tpu_custom_call" | custom-call | flops 536870912 | bytes 1048576 | tf_op jit(solution)/shard_map/pallas_call | solution.py:438
  3.5 14.6 %collective-permute-start.2 = (bf16[272,1536]{1,0:T(8,128)(2,1)}, bf16[272,1536]{1,0:T(8,128)(2,1)S(1)}, u32[]{:S(2)}, u32[]{:S(2)}) collective-permute-start(bf16[272,1536]{1,0:T(8,128)(2,1)} %get-tuple-element.34.b_ref.b_hbm), channel_id=1, source_target_pairs={{0,496},{16,32},{32,16},{48,64},{64,48},{80,96},{96,80},{112,128},... | collective-permute-start | bytes 2506760 | tf_op jit(solution)/shard_map/ppermute | solution.py:464
  18.1 0.0 copy-start.20
  18.1 0.0 copy-start.21
  18.1 0.0 copy-start.22
  18.1 0.0 copy-start.18
  18.1 0.0 copy-start.19
  18.2 2.1 %collective-permute-start = (bf16[272,1536]{1,0:T(8,128)(2,1)}, bf16[272,1536]{1,0:T(8,128)(2,1)S(1)}, u32[]{:S(2)}, u32[]{:S(2)}) collective-permute-start(bf16[272,1536]{1,0:T(8,128)(2,1)} %get-tuple-element.33.a_ref.a_hbm), channel_id=1, source_target_pairs={{0,16},{16,0},{32,48},{48,32},{64,80},{80,64},{96,112},{112,96},{1... | collective-permute-start | bytes 2506760 | tf_op jit(solution)/shard_map/ppermute | solution.py:464
  20.2 0.0 copy-done.14
  20.2 0.0 copy-done.15
  20.2 0.0 copy-done.20
  20.2 0.0 copy-done.21
  20.3 1.1 %copy-done = bf16[272,1536]{1,0:T(8,128)(2,1)S(1)} copy-done((bf16[272,1536]{1,0:T(8,128)(2,1)S(1)}, bf16[272,1536]{1,0:T(8,128)(2,1)}, u32[]{:S(2)}) %copy-start) | copy-done | bytes 835608
  21.4 1.1 %copy-done.2 = bf16[272,1536]{1,0:T(8,128)(2,1)S(1)} copy-done((bf16[272,1536]{1,0:T(8,128)(2,1)S(1)}, bf16[272,1536]{1,0:T(8,128)(2,1)}, u32[]{:S(2)}) %copy-start.2) | copy-done | bytes 835608
  22.6 3.6 %shard_map.147 = (f32[128,1536]{1,0:T(8,128)S(1)}, f32[128,1536]{1,0:T(8,128)S(1)}, f32[128,1536]{1,0:T(8,128)S(1)}, f32[24,128]{1,0:T(8,128)S(1)}, f32[128,1536...) custom-call(s32[1,2,32]{2,1,0:T(2,128)S(1)} %bitcast.7, ...), custom_call_target="tpu_custom_call" | custom-call | flops 536870912 | bytes 1048576 | tf_op jit(solution)/shard_map/pallas_call | solution.py:438
  26.2 1.0 copy-done.11
  27.2 0.9 copy-done.12
  28.1 0.9 copy-done.13
  29.0 7.6 %collective-permute-done.2.b1_ref = bf16[272,1536]{1,0:T(8,128)(2,1)S(1)} collective-permute-done((bf16[272,1536]{1,0:T(8,128)(2,1)}, bf16[272,1536]{1,0:T(8,128)(2,1)S(1)}, u32[]{:S(2)}, u32[]{:S(2)}) %collective-permute-start.2) | collective-permute-done | bytes 835616 | tf_op jit(solution)/shard_map/ppermute | solution.py:464
  36.6 1.9 %collective-permute-start.3 = (bf16[272,1536]{1,0:T(8,128)(2,1)S(1)}, bf16[272,1536]{1,0:T(8,128)(2,1)S(1)}, u32[]{:S(2)}, u32[]{:S(2)}) collective-permute-start(bf16[272,1536]{1,0:T(8,128)(2,1)S(1)} %collective-permute-done.2.b1_ref), channel_id=1, source_target_pairs={{0,16},{16,0},{32,48},{48,32},{64,80},{80,64},{96,112},{112,96},{1... | collective-permute-start | bytes 2506760 | tf_op jit(solution)/shard_map/ppermute | solution.py:464
  38.5 1.0 collective-permute-done.chain_ref
  39.5 6.1 %collective-permute-start.1 = (bf16[272,1536]{1,0:T(8,128)(2,1)S(1)}, bf16[272,1536]{1,0:T(8,128)(2,1)}, u32[]{:S(2)}, u32[]{:S(2)}) collective-permute-start(bf16[272,1536]{1,0:T(8,128)(2,1)S(1)} %shard_map.148.a1_ref), channel_id=1, source_target_pairs={{0,496},{16,32},{32,16},{48,64},{64,48},{80,96},{96,80},{112,128},... | collective-permute-start | bytes 2506760 | tf_op jit(solution)/shard_map/ppermute | solution.py:464
  45.7 0.0 copy-done.1
  45.7 0.0 copy-done.3
  45.7 4.6 %shard_map.149 = (f32[128,1536]{1,0:T(8,128)S(1)}, f32[128,1536]{1,0:T(8,128)S(1)}, f32[128,1536]{1,0:T(8,128)S(1)}, f32[24,128]{1,0:T(8,128)S(1)}, f32[128,1536]{1,0:T(8,128)S(1)}, /*index=5*/f32[128,1536]{1,0:T(8,128)S(1)}) custom-call(bf16[272,1536]{1,0:T(8,128)(2,1)S(1)} %copy-done.1, ...), custom_call_target="tpu_custom_call", output_to_operand_aliasing={{0}: (5, {}), {1}: (6, {}), {2}: (7, {})} | custom-call | flops 536870912 | bytes 1048576 | tf_op jit(solution)/shard_map/pallas_call | solution.py:438
  50.3 0.6 copy-done.16
  50.9 6.5 %collective-permute-done.3.chain_ref = bf16[272,1536]{1,0:T(8,128)(2,1)S(1)} collective-permute-done((bf16[272,1536]{1,0:T(8,128)(2,1)S(1)}, bf16[272,1536]{1,0:T(8,128)(2,1)S(1)}, u32[]{:S(2)}, u32[]{:S(2)}) %collective-permute-start.3) | collective-permute-done | bytes 835616 | tf_op jit(solution)/shard_map/ppermute | solution.py:464
  57.5 6.6 %collective-permute-start.5 = (bf16[272,1536]{1,0:T(8,128)(2,1)S(1)}, bf16[272,1536]{1,0:T(8,128)(2,1)}, u32[]{:S(2)}, u32[]{:S(2)}) collective-permute-start(bf16[272,1536]{1,0:T(8,128)(2,1)S(1)} %shard_map.150.b2_ref.b2_hbm), channel_id=1, source_target_pairs={{0,496},{16,32},{32,16},{48,64},{64,48},{80,96},{96,80},{112,128},... | collective-permute-start | bytes 2506760 | tf_op jit(solution)/shard_map/ppermute | solution.py:464
  64.1 0.0 collective-permute-done.1.a2_ref.a2_hbm
  64.1 1.9 %collective-permute-start.4 = (bf16[272,1536]{1,0:T(8,128)(2,1)}, bf16[272,1536]{1,0:T(8,128)(2,1)}, u32[]{:S(2)}, u32[]{:S(2)}) collective-permute-start(bf16[272,1536]{1,0:T(8,128)(2,1)} %collective-permute-done.1.a2_ref.a2_hbm), channel_id=1, source_target_pairs={{0,16},{16,0},{32,48},{48,32},{64,80},{80,64},{96,112},{112,96},{1... | collective-permute-start | bytes 2506760 | tf_op jit(solution)/shard_map/ppermute | solution.py:464
  66.0 0.0 copy-done.7
  66.0 0.0 copy-done.8
  66.1 0.0 copy-done.9
  66.1 0.0 copy-done.17
  66.1 0.0 copy-done.6
  66.1 3.3 %shard_map.151 = (f32[128,1536]{1,0:T(8,128)S(1)}, f32[8,2,128]{2,1,0:T(2,128)S(1)}) custom-call(bf16[272,1536]{1,0:T(8,128)(2,1)S(1)} %copy-done.1, bf16[272,1536]{1,0:T(8,128)(2,1)S(1)} %copy-done.3, bf16[272,1536]{1,0:T(8,128)(2,1)S(1)} %shard_map.148.a1_ref, ...), custom_call_target="tpu_custom_call", output_to_operand_aliasing={{0}: (6, {})} | custom-call | flops 536870912 | bytes 1048576 | tf_op jit(solution)/shard_map/pallas_call | solution.py:438
  69.4 11.8 %all_to_all.10.parts_ref = f32[8,2,128]{2,1,0:T(2,128)S(1)} all-to-all(f32[8,2,128]{2,1,0:T(2,128)S(1)} %get-tuple-element.54), channel_id=1, replica_groups={{0,1,4,5,8,9,12,13},{2,3,6,7,10,11,14,15},{16,17,20,21,24,25,28,29},{18..., dimensions={0} | all-to-all | bytes 16384 | tf_op jit(solution)/shard_map/all_to_all | solution.py:536
  81.1 0.6 shard_map.152.sums_ref
  81.8 0.0 copy-done.5
  81.8 7.2 %all-to-all-start.1 = ((f32[64,2,128]{2,1,0:T(2,128)}), f32[64,2,128]{2,1,0:T(2,128)S(1)}, u32[]{:S(2)}, u32[]{:S(2)}) async-start(f32[64,2,128]{2,1,0:T(2,128)} %shard_map.152.sums_ref), calls=%async_computation.1 | async-start | bytes 131072 | tf_op jit(solution)/shard_map/all_to_all | solution.py:540
  89.0 0.0 collective-permute-done.5.b3_hbm
  89.0 0.0 collective-permute-done.4.a3_hbm
  89.1 9.0 %shard_map.153 = (bf16[1,128,1536]{2,1,0:T(8,128)(2,1)}, bf16[1,128,1536]{2,1,0:T(8,128)(2,1)}, bf16[1,128,1536]{2,1,0:T(8,128)(2,1)}, f32[8,128]{1,0:T(8,128)}) custom-call(bf16[272,1536]{1,0:T(8,128)(2,1)} %get-tuple-element.33.a_ref.a_hbm, bf16[272,1536]{1,0:T(8,128)(2,1)} %get-tuple-element.34.b_ref.b_hbm, ...), custom_call_target="tpu_custom_call" | custom-call | flops 536870912 | bytes 1048576 | tf_op jit(solution)/shard_map/pallas_call | solution.py:438
  98.0 1.9 %all-to-all-done.1.parts_ref = f32[64,2,128]{2,1,0:T(2,128)S(1)} async-done(((f32[64,2,128]{2,1,0:T(2,128)}), f32[64,2,128]{2,1,0:T(2,128)S(1)}, u32[]{:S(2)}, u32[]{:S(2)}) %all-to-all-start.1) | async-done | bytes 65568 | tf_op jit(solution)/shard_map/all_to_all | solution.py:540
  99.9 0.7 copy-done.23
  100.6 0.6 shard_map.154
  (24 shorter events, 0.0 us)
Async XLA Ops:
  0.6 19.6 %copy-start.14 = (bf16[1,128,1536]{2,1,0:T(8,128)(2,1)S(1)}, bf16[1,128,1536]{2,1,0:T(8,128)(2,1)}, u32[]{:S(2)}) copy-start(bf16[1,128,1536]{2,1,0:T(8,128)(2,1)} %query_ref.1) | copy-start | bytes 1179652
  0.6 19.6 %copy-start.15 = (bf16[1,128,1536]{2,1,0:T(8,128)(2,1)S(1)}, bf16[1,128,1536]{2,1,0:T(8,128)(2,1)}, u32[]{:S(2)}) copy-start(bf16[1,128,1536]{2,1,0:T(8,128)(2,1)} %key_ref.1) | copy-start | bytes 1179652
  3.5 33.1 %collective-permute-start.2 = (bf16[272,1536]{1,0:T(8,128)(2,1)}, bf16[272,1536]{1,0:T(8,128)(2,1)S(1)}, u32[]{:S(2)}, u32[]{:S(2)}) collective-permute-start(bf16[272,1536]{1,0:T(8,128)(2,1)} %get-tuple-element.34.b_ref.b_hbm), channel_id=1, source_target_pairs={{0,496},{16,32},{32,16},{48,64},{64,48},{80,96},{96,80},{112,128},... | collective-permute-start | bytes 2506760 | tf_op jit(solution)/shard_map/ppermute | solution.py:464
  18.1 2.1 %copy-start.20 = (f32[128]{0:T(128)S(1)}, f32[128]{0:T(128)}, u32[]{:S(2)}) copy-start(f32[128]{0:T(128)} %param.18) | copy-start | bytes 1540
  18.1 2.1 %copy-start.21 = (s32[1,32]{1,0:T(1,128)S(1)}, s32[1,32]{1,0:T(1,128)}, u32[]{:S(2)}) copy-start(s32[1,32]{1,0:T(1,128)} %counts_ref.1) | copy-start | bytes 388
  18.1 2.1 %copy-start.22 = (s32[1,64]{1,0:T(1,128)S(1)}, s32[1,64]{1,0:T(1,128)}, u32[]{:S(2)}) copy-start(s32[1,64]{1,0:T(1,128)} %reach_ref.1) | copy-start | bytes 772
  18.1 2.1 %copy-start.18 = (s32[1,32,2]{1,2,0:T(2,128)S(1)}, s32[1,32,2]{1,2,0:T(2,128)}, u32[]{:S(2)}) copy-start(s32[1,32,2]{1,2,0:T(2,128)} %param.19) | copy-start | bytes 772
  18.1 2.1 %copy-start.19 = (f32[128]{0:T(128)S(1)}, f32[128]{0:T(128)}, u32[]{:S(2)}) copy-start(f32[128]{0:T(128)} %param.17) | copy-start | bytes 1540
  18.2 21.4 %collective-permute-start = (bf16[272,1536]{1,0:T(8,128)(2,1)}, bf16[272,1536]{1,0:T(8,128)(2,1)S(1)}, u32[]{:S(2)}, u32[]{:S(2)}) collective-permute-start(bf16[272,1536]{1,0:T(8,128)(2,1)} %get-tuple-element.33.a_ref.a_hbm), channel_id=1, source_target_pairs={{0,16},{16,0},{32,48},{48,32},{64,80},{80,64},{96,112},{112,96},{1... | collective-permute-start | bytes 2506760 | tf_op jit(solution)/shard_map/ppermute | solution.py:464
  20.3 1.2 %copy-start = (bf16[272,1536]{1,0:T(8,128)(2,1)S(1)}, bf16[272,1536]{1,0:T(8,128)(2,1)}, u32[]{:S(2)}) copy-start(bf16[272,1536]{1,0:T(8,128)(2,1)} %get-tuple-element.33.a_ref.a_hbm) | copy-start | bytes 2506756
  21.4 1.1 %copy-start.2 = (bf16[272,1536]{1,0:T(8,128)(2,1)S(1)}, bf16[272,1536]{1,0:T(8,128)(2,1)}, u32[]{:S(2)}) copy-start(bf16[272,1536]{1,0:T(8,128)(2,1)} %get-tuple-element.34.b_ref.b_hbm) | copy-start | bytes 2506756
  26.2 1.0 copy-start.11
  27.2 0.9 copy-start.12
  28.1 0.9 copy-start.13
  29.0 37.0 %copy-start.7 = (f32[128,1536]{1,0:T(8,128)}, f32[128,1536]{1,0:T(8,128)S(1)}, u32[]{:S(2)}) copy-start(f32[128,1536]{1,0:T(8,128)S(1)} %get-tuple-element.43.query_unit_ref.query_unit_hbm) | copy-start | bytes 2359300
  29.0 37.0 %copy-start.8 = (f32[128,1536]{1,0:T(8,128)}, f32[128,1536]{1,0:T(8,128)S(1)}, u32[]{:S(2)}) copy-start(f32[128,1536]{1,0:T(8,128)S(1)} %get-tuple-element.44.key_unit_ref.key_unit_hbm) | copy-start | bytes 2359300
  29.0 37.0 %copy-start.9 = (f32[128,1536]{1,0:T(8,128)}, f32[128,1536]{1,0:T(8,128)S(1)}, u32[]{:S(2)}) copy-start(f32[128,1536]{1,0:T(8,128)S(1)} %get-tuple-element.46.dot_ref.dot_hbm) | copy-start | bytes 2359300
  29.0 37.1 %copy-start.17 = (f32[2,128]{1,0:T(2,128)}, f32[2,128]{1,0:T(2,128)S(1)}, u32[]{:S(2)}) copy-start(f32[2,128]{1,0:T(2,128)S(1)} %get-tuple-element.40.gains_ref.gains_hbm) | copy-start | bytes 3076
  36.6 20.8 %collective-permute-start.3 = (bf16[272,1536]{1,0:T(8,128)(2,1)S(1)}, bf16[272,1536]{1,0:T(8,128)(2,1)S(1)}, u32[]{:S(2)}, u32[]{:S(2)}) collective-permute-start(bf16[272,1536]{1,0:T(8,128)(2,1)S(1)} %collective-permute-done.2.b1_ref), channel_id=1, source_target_pairs={{0,16},{16,0},{32,48},{48,32},{64,80},{80,64},{96,112},{112,96},{1... | collective-permute-start | bytes 2506760 | tf_op jit(solution)/shard_map/ppermute | solution.py:464
  39.5 6.1 %copy-start.1 = (bf16[272,1536]{1,0:T(8,128)(2,1)S(1)}, bf16[272,1536]{1,0:T(8,128)(2,1)}, u32[]{:S(2)}) copy-start(bf16[272,1536]{1,0:T(8,128)(2,1)} %get-tuple-element.33.a_ref.a_hbm) | copy-start | bytes 2506756
  39.5 6.1 %copy-start.3 = (bf16[272,1536]{1,0:T(8,128)(2,1)S(1)}, bf16[272,1536]{1,0:T(8,128)(2,1)}, u32[]{:S(2)}) copy-start(bf16[272,1536]{1,0:T(8,128)(2,1)} %get-tuple-element.34.b_ref.b_hbm) | copy-start | bytes 2506756
  39.5 24.6 %collective-permute-start.1 = (bf16[272,1536]{1,0:T(8,128)(2,1)S(1)}, bf16[272,1536]{1,0:T(8,128)(2,1)}, u32[]{:S(2)}, u32[]{:S(2)}) collective-permute-start(bf16[272,1536]{1,0:T(8,128)(2,1)S(1)} %shard_map.148.a1_ref), channel_id=1, source_target_pairs={{0,496},{16,32},{32,16},{48,64},{64,48},{80,96},{96,80},{112,128},... | collective-permute-start | bytes 2506760 | tf_op jit(solution)/shard_map/ppermute | solution.py:464
  50.3 0.6 copy-start.16
  50.9 6.5 %copy-start.10 = (f32[128,1536]{1,0:T(8,128)}, f32[128,1536]{1,0:T(8,128)S(1)}, u32[]{:S(2)}) copy-start(f32[128,1536]{1,0:T(8,128)S(1)} %get-tuple-element.50.dv_hbm) | copy-start | bytes 2359300
  50.9 15.2 %copy-start.6 = (f32[128,1536]{1,0:T(8,128)}, f32[128,1536]{1,0:T(8,128)S(1)}, u32[]{:S(2)}) copy-start(f32[128,1536]{1,0:T(8,128)S(1)} %get-tuple-element.42.dk_ref.dk_hbm) | copy-start | bytes 2359300
  57.5 11.9 %copy-start.4 = (bf16[272,1536]{1,0:T(8,128)(2,1)}, bf16[272,1536]{1,0:T(8,128)(2,1)S(1)}, u32[]{:S(2)}) copy-start(bf16[272,1536]{1,0:T(8,128)(2,1)S(1)} %shard_map.150.b2_ref.b2_hbm) | copy-start | bytes 2506756
  57.5 31.6 %collective-permute-start.5 = (bf16[272,1536]{1,0:T(8,128)(2,1)S(1)}, bf16[272,1536]{1,0:T(8,128)(2,1)}, u32[]{:S(2)}, u32[]{:S(2)}) collective-permute-start(bf16[272,1536]{1,0:T(8,128)(2,1)S(1)} %shard_map.150.b2_ref.b2_hbm), channel_id=1, source_target_pairs={{0,496},{16,32},{32,16},{48,64},{64,48},{80,96},{96,80},{112,128},... | collective-permute-start | bytes 2506760 | tf_op jit(solution)/shard_map/ppermute | solution.py:464
  64.1 24.9 %collective-permute-start.4 = (bf16[272,1536]{1,0:T(8,128)(2,1)}, bf16[272,1536]{1,0:T(8,128)(2,1)}, u32[]{:S(2)}, u32[]{:S(2)}) collective-permute-start(bf16[272,1536]{1,0:T(8,128)(2,1)} %collective-permute-done.1.a2_ref.a2_hbm), channel_id=1, source_target_pairs={{0,16},{16,0},{32,48},{48,32},{64,80},{80,64},{96,112},{112,96},{1... | collective-permute-start | bytes 2506760 | tf_op jit(solution)/shard_map/ppermute | solution.py:464
  69.4 12.4 %copy-start.5 = (f32[128,1536]{1,0:T(8,128)}, f32[128,1536]{1,0:T(8,128)S(1)}, u32[]{:S(2)}) copy-start(f32[128,1536]{1,0:T(8,128)S(1)} %get-tuple-element.49.dq_hbm) | copy-start | bytes 2359300
  81.8 18.2 %all-to-all-start.1 = ((f32[64,2,128]{2,1,0:T(2,128)}), f32[64,2,128]{2,1,0:T(2,128)S(1)}, u32[]{:S(2)}, u32[]{:S(2)}) async-start(f32[64,2,128]{2,1,0:T(2,128)} %shard_map.152.sums_ref), calls=%async_computation.1 | async-start | bytes 131072 | tf_op jit(solution)/shard_map/all_to_all | solution.py:540
  99.9 0.7 copy-start.23

commit v6 on v5

--- a/solution.py
+++ b/solution.py
@@ -513,8 +513,8 @@
         (a, b, a1, b1, bias, dq, dk, dv),
         {5: 0, 6: 1, 7: 2},
     )
-    b2 = after(b2, token)
-    b3, a3 = swapped(b2, 1), swapped(a2, 0)
+    a2 = after(a2, token)
+    a3, b3 = swapped(a2, 0), swapped(b2, 1)
     ends = 2 if clips % 4 == 0 else 1
     first = [
         [clip for clip in range(clips) if clip // 2 % ends == end] for end in range(ends)

time: 102 us -> 99.9 us (0.979)
  waiting for transfers between devices: 17.1 us -> 13.1 us
  starting transfers between devices: 40.4 us -> 42.3 us
    ppermute x6, waiting for transfers between devices: 15.2 us -> 11.2 us  [swapped(): return lax.ppermute(value, 'tm', pairs)]
    ppermute x6, starting transfers between devices: 33.2 us -> 37.2 us  [swapped(): return lax.ppermute(value, 'tm', pairs)]
    all_to_all x1, starting transfers between devices: 7.24 us -> 5.13 us  [body(): parts = lax.all_to_all(sums, ('tm', 'dp'), 0, 0, axis_index_groups=second)]
  transfers between devices with their start and end apart: 7 -> 7, of which waited for: 4 -> 3; matrix products, arithmetic and copies ran while one was open for 0% -> 0% of each run, Pallas kernels for 21% -> 21%
where the time goes in v6:
time: 99.9 us; the launch traced here: 99.3 us
  starting transfers between devices  42.3 us (42%)
  Pallas kernels  24.6 us (25%)
  waiting for transfers between devices  13.1 us (13%)
  blocking collectives  11.9 us (12%)
  local copies, waits for them, and re-layouts  6.4 us (6%)
  between operations  1 us (1%)
    ppermute x6, starting transfers between devices, swapped(): return lax.ppermute(value, 'tm', pairs)  37.2 us
    pallas_call x7, Pallas kernels, call(): pl.pallas_call(kernel, out_shape=tuple(outs), in_specs=specs, out_specs=(...  24.6 us
    all_to_all x1, blocking collectives, body(): parts = lax.all_to_all(terms, 'dp', 0, 0, axis_index_groups=first)  11.9 us
    ppermute x6, waiting for transfers between devices, swapped(): return lax.ppermute(value, 'tm', pairs)  11.2 us
    unnamed x48, local copies, waits for them, and re-layouts  6.4 us
    all_to_all x1, starting transfers between devices, body(): parts = lax.all_to_all(sums, ('tm', 'dp'), 0, 0, axis_index_groups=second)  5.13 us
  transfers between devices with their start and end apart: 7, of which 3 were waited for; matrix products, arithmetic and copies ran while one was open for 0% of the time, Pallas kernels for 21%

profile of v6, /device:TPU:1, one launch (start us, length us, event | category | flops | bytes accessed | tf_op | source)
XLA Modules:
  0.0 99.3 jit_solution(9462193772038852308)
XLA Ops:
  0.6 0.0 copy-start.14
  0.6 0.0 copy-start.15
  0.7 2.9 %shard_map.146 = (bf16[272,1536]{1,0:T(8,128)(2,1)}, bf16[272,1536]{1,0:T(8,128)(2,1)}) custom-call(bf16[1,128,1536]{2,1,0:T(8,128)(2,1)} %query_ref.1, bf16[1,128,1536]{2,1,0:T(8,128)(2,1)} %key_ref.1, bf16[1,128,1536]{2,1,0:T(8,128)(2,1)} %value_hbm.1, bf16[1,128,1536]{2,1,0:T(8,128)(2,1)} %grad_hbm.1, f32[12,1,128]{2,1,0:T(1,128)} %bitcast.12, ...), custom_call_target="tpu_custom_call" | custom-call | flops 536870912 | bytes 1048576 | tf_op jit(solution)/shard_map/pallas_call | solution.py:438
  3.5 4.9 %collective-permute-start = (bf16[272,1536]{1,0:T(8,128)(2,1)}, bf16[272,1536]{1,0:T(8,128)(2,1)S(1)}, u32[]{:S(2)}, u32[]{:S(2)}) collective-permute-start(bf16[272,1536]{1,0:T(8,128)(2,1)} %get-tuple-element.33.a_ref.a_hbm), channel_id=1, source_target_pairs={{0,16},{16,0},{32,48},{48,32},{64,80},{80,64},{96,112},{112,96},{1... | collective-permute-start | bytes 2506760 | tf_op jit(solution)/shard_map/ppermute | solution.py:464
  8.4 0.0 copy-start.20
  8.4 0.0 copy-start.21
  8.4 0.0 copy-start.22
  8.4 0.0 copy-start.18
  8.4 0.0 copy-start.19
  8.5 12.0 %collective-permute-start.2 = (bf16[272,1536]{1,0:T(8,128)(2,1)}, bf16[272,1536]{1,0:T(8,128)(2,1)S(1)}, u32[]{:S(2)}, u32[]{:S(2)}) collective-permute-start(bf16[272,1536]{1,0:T(8,128)(2,1)} %get-tuple-element.34.b_ref.b_hbm), channel_id=1, source_target_pairs={{0,496},{16,32},{32,16},{48,64},{64,48},{80,96},{96,80},{112,128},... | collective-permute-start | bytes 2506760 | tf_op jit(solution)/shard_map/ppermute | solution.py:464
  20.4 0.0 copy-done.14
  20.5 0.0 copy-done.15
  20.5 0.0 copy-done.20
  20.5 0.0 copy-done.21
  20.5 0.0 copy-done.22
  20.5 0.0 copy-done.18
  20.5 0.0 copy-done.19
  20.5 1.1 %copy-done = bf16[272,1536]{1,0:T(8,128)(2,1)S(1)} copy-done((bf16[272,1536]{1,0:T(8,128)(2,1)S(1)}, bf16[272,1536]{1,0:T(8,128)(2,1)}, u32[]{:S(2)}) %copy-start) | copy-done | bytes 835608
  21.7 1.1 %copy-done.2 = bf16[272,1536]{1,0:T(8,128)(2,1)S(1)} copy-done((bf16[272,1536]{1,0:T(8,128)(2,1)S(1)}, bf16[272,1536]{1,0:T(8,128)(2,1)}, u32[]{:S(2)}) %copy-start.2) | copy-done | bytes 835608
  22.8 3.6 %shard_map.147 = (f32[128,1536]{1,0:T(8,128)S(1)}, f32[128,1536]{1,0:T(8,128)S(1)}, f32[128,1536]{1,0:T(8,128)S(1)}, f32[24,128]{1,0:T(8,128)S(1)}, f32[128,1536...) custom-call(s32[1,2,32]{2,1,0:T(2,128)S(1)} %bitcast.7, ...), custom_call_target="tpu_custom_call" | custom-call | flops 536870912 | bytes 1048576 | tf_op jit(solution)/shard_map/pallas_call | solution.py:438
  26.5 1.0 copy-done.11
  27.4 0.9 copy-done.12
  28.3 0.9 copy-done.13
  29.2 0.0 collective-permute-done.chain_ref
  29.3 10.5 %collective-permute-start.1 = (bf16[272,1536]{1,0:T(8,128)(2,1)S(1)}, bf16[272,1536]{1,0:T(8,128)(2,1)S(1)}, u32[]{:S(2)}, u32[]{:S(2)}) collective-permute-start(bf16[272,1536]{1,0:T(8,128)(2,1)S(1)} %shard_map.148.a1_ref), channel_id=1, source_target_pairs={{0,496},{16,32},{32,16},{48,64},{64,48},{80,96},{96,80},{112,128},... | collective-permute-start | bytes 2506760 | tf_op jit(solution)/shard_map/ppermute | solution.py:464
  39.8 0.0 collective-permute-done.2.b1_ref
  39.8 1.9 %collective-permute-start.3 = (bf16[272,1536]{1,0:T(8,128)(2,1)S(1)}, bf16[272,1536]{1,0:T(8,128)(2,1)}, u32[]{:S(2)}, u32[]{:S(2)}) collective-permute-start(bf16[272,1536]{1,0:T(8,128)(2,1)S(1)} %collective-permute-done.2.b1_ref), channel_id=1, source_target_pairs={{0,16},{16,0},{32,48},{48,32},{64,80},{80,64},{96,112},{112,96},{1... | collective-permute-start | bytes 2506760 | tf_op jit(solution)/shard_map/ppermute | solution.py:464
  41.7 0.0 copy-done.1
  41.7 0.0 copy-done.3
  41.8 4.6 %shard_map.149 = (f32[128,1536]{1,0:T(8,128)S(1)}, f32[128,1536]{1,0:T(8,128)S(1)}, f32[128,1536]{1,0:T(8,128)S(1)}, f32[24,128]{1,0:T(8,128)S(1)}, f32[128,1536]{1,0:T(8,128)S(1)}, /*index=5*/f32[128,1536]{1,0:T(8,128)S(1)}) custom-call(bf16[272,1536]{1,0:T(8,128)(2,1)S(1)} %copy-done.1, ...), custom_call_target="tpu_custom_call", output_to_operand_aliasing={{0}: (5, {}), {1}: (6, {}), {2}: (7, {})} | custom-call | flops 536870912 | bytes 1048576 | tf_op jit(solution)/shard_map/pallas_call | solution.py:438
  46.4 0.6 copy-done.16
  47.0 10.1 %collective-permute-done.1.chain_ref = bf16[272,1536]{1,0:T(8,128)(2,1)S(1)} collective-permute-done((bf16[272,1536]{1,0:T(8,128)(2,1)S(1)}, bf16[272,1536]{1,0:T(8,128)(2,1)S(1)}, u32[]{:S(2)}, u32[]{:S(2)}) %collective-permute-start.1) | collective-permute-done | bytes 835616 | tf_op jit(solution)/shard_map/ppermute | solution.py:464
  57.1 0.0 copy-done.10
  57.1 1.9 %collective-permute-start.4 = (bf16[272,1536]{1,0:T(8,128)(2,1)S(1)}, bf16[272,1536]{1,0:T(8,128)(2,1)}, u32[]{:S(2)}, u32[]{:S(2)}) collective-permute-start(bf16[272,1536]{1,0:T(8,128)(2,1)S(1)} %shard_map.150.a2_ref.a2_hbm), channel_id=1, source_target_pairs={{0,16},{16,0},{32,48},{48,32},{64,80},{80,64},{96,112},{112,96},{1... | collective-permute-start | bytes 2506760 | tf_op jit(solution)/shard_map/ppermute | solution.py:464
  59.1 1.0 %collective-permute-done.3.b2_ref.b2_hbm = bf16[272,1536]{1,0:T(8,128)(2,1)} collective-permute-done((bf16[272,1536]{1,0:T(8,128)(2,1)S(1)}, bf16[272,1536]{1,0:T(8,128)(2,1)}, u32[]{:S(2)}, u32[]{:S(2)}) %collective-permute-start.3) | collective-permute-done | bytes 835616 | tf_op jit(solution)/shard_map/ppermute | solution.py:464
  60.1 6.0 %collective-permute-start.5 = (bf16[272,1536]{1,0:T(8,128)(2,1)}, bf16[272,1536]{1,0:T(8,128)(2,1)}, u32[]{:S(2)}, u32[]{:S(2)}) collective-permute-start(bf16[272,1536]{1,0:T(8,128)(2,1)} %collective-permute-done.3.b2_ref.b2_hbm), channel_id=1, source_target_pairs={{0,496},{16,32},{32,16},{48,64},{64,48},{80,96},{96,80},{112,128},... | collective-permute-start | bytes 2506760 | tf_op jit(solution)/shard_map/ppermute | solution.py:464
  66.1 3.3 %shard_map.151 = (f32[128,1536]{1,0:T(8,128)S(1)}, f32[8,2,128]{2,1,0:T(2,128)S(1)}) custom-call(bf16[272,1536]{1,0:T(8,128)(2,1)S(1)} %copy-done.1, bf16[272,1536]{1,0:T(8,128)(2,1)S(1)} %copy-done.3, bf16[272,1536]{1,0:T(8,128)(2,1)S(1)} %shard_map.148.a1_ref, ...), custom_call_target="tpu_custom_call", output_to_operand_aliasing={{0}: (6, {})} | custom-call | flops 536870912 | bytes 1048576 | tf_op jit(solution)/shard_map/pallas_call | solution.py:438
  69.4 0.0 copy-done.4
  69.4 0.0 copy-start.5
  69.4 11.9 %all_to_all.10.parts_ref = f32[8,2,128]{2,1,0:T(2,128)S(1)} all-to-all(f32[8,2,128]{2,1,0:T(2,128)S(1)} %get-tuple-element.54), channel_id=1, replica_groups={{0,1,4,5,8,9,12,13},{2,3,6,7,10,11,14,15},{16,17,20,21,24,25,28,29},{18..., dimensions={0} | all-to-all | bytes 16384 | tf_op jit(solution)/shard_map/all_to_all | solution.py:536
  81.3 0.6 shard_map.152.sums_ref
  82.0 5.1 %all-to-all-start.1 = ((f32[64,2,128]{2,1,0:T(2,128)}), f32[64,2,128]{2,1,0:T(2,128)S(1)}, u32[]{:S(2)}, u32[]{:S(2)}) async-start(f32[64,2,128]{2,1,0:T(2,128)} %shard_map.152.sums_ref), calls=%async_computation.1 | async-start | bytes 131072 | tf_op jit(solution)/shard_map/all_to_all | solution.py:540
  87.1 0.0 collective-permute-done.4.a3_hbm
  87.1 0.0 collective-permute-done.5.b3_hbm
  87.1 9.0 %shard_map.153 = (bf16[1,128,1536]{2,1,0:T(8,128)(2,1)}, bf16[1,128,1536]{2,1,0:T(8,128)(2,1)}, bf16[1,128,1536]{2,1,0:T(8,128)(2,1)}, f32[8,128]{1,0:T(8,128)}) custom-call(bf16[272,1536]{1,0:T(8,128)(2,1)} %get-tuple-element.33.a_ref.a_hbm, bf16[272,1536]{1,0:T(8,128)(2,1)} %get-tuple-element.34.b_ref.b_hbm, bf16[272,1536]{1,0:T(8,128)(2,1)} %copy-done.4, ...), custom_call_target="tpu_custom_call" | custom-call | flops 536870912 | bytes 1048576 | tf_op jit(solution)/shard_map/pallas_call | solution.py:438
  96.1 1.9 %all-to-all-done.1.parts_ref = f32[64,2,128]{2,1,0:T(2,128)S(1)} async-done(((f32[64,2,128]{2,1,0:T(2,128)}), f32[64,2,128]{2,1,0:T(2,128)S(1)}, u32[]{:S(2)}, u32[]{:S(2)}) %all-to-all-start.1) | async-done | bytes 65568 | tf_op jit(solution)/shard_map/all_to_all | solution.py:540
  98.0 0.7 copy-done.23
  98.7 0.6 shard_map.154
  (24 shorter events, 0.0 us)
Async XLA Ops:
  0.6 19.8 %copy-start.14 = (bf16[1,128,1536]{2,1,0:T(8,128)(2,1)S(1)}, bf16[1,128,1536]{2,1,0:T(8,128)(2,1)}, u32[]{:S(2)}) copy-start(bf16[1,128,1536]{2,1,0:T(8,128)(2,1)} %query_ref.1) | copy-start | bytes 1179652
  0.6 19.8 %copy-start.15 = (bf16[1,128,1536]{2,1,0:T(8,128)(2,1)S(1)}, bf16[1,128,1536]{2,1,0:T(8,128)(2,1)}, u32[]{:S(2)}) copy-start(bf16[1,128,1536]{2,1,0:T(8,128)(2,1)} %key_ref.1) | copy-start | bytes 1179652
  3.5 25.7 %collective-permute-start = (bf16[272,1536]{1,0:T(8,128)(2,1)}, bf16[272,1536]{1,0:T(8,128)(2,1)S(1)}, u32[]{:S(2)}, u32[]{:S(2)}) collective-permute-start(bf16[272,1536]{1,0:T(8,128)(2,1)} %get-tuple-element.33.a_ref.a_hbm), channel_id=1, source_target_pairs={{0,16},{16,0},{32,48},{48,32},{64,80},{80,64},{96,112},{112,96},{1... | collective-permute-start | bytes 2506760 | tf_op jit(solution)/shard_map/ppermute | solution.py:464
  8.4 12.1 %copy-start.20 = (f32[128]{0:T(128)S(1)}, f32[128]{0:T(128)}, u32[]{:S(2)}) copy-start(f32[128]{0:T(128)} %param.18) | copy-start | bytes 1540
  8.4 12.1 %copy-start.21 = (s32[1,32]{1,0:T(1,128)S(1)}, s32[1,32]{1,0:T(1,128)}, u32[]{:S(2)}) copy-start(s32[1,32]{1,0:T(1,128)} %counts_ref.1) | copy-start | bytes 388
  8.4 12.1 %copy-start.22 = (s32[1,64]{1,0:T(1,128)S(1)}, s32[1,64]{1,0:T(1,128)}, u32[]{:S(2)}) copy-start(s32[1,64]{1,0:T(1,128)} %reach_ref.1) | copy-start | bytes 772
  8.4 12.1 %copy-start.18 = (s32[1,32,2]{1,2,0:T(2,128)S(1)}, s32[1,32,2]{1,2,0:T(2,128)}, u32[]{:S(2)}) copy-start(s32[1,32,2]{1,2,0:T(2,128)} %param.19) | copy-start | bytes 772
  8.4 12.1 %copy-start.19 = (f32[128]{0:T(128)S(1)}, f32[128]{0:T(128)}, u32[]{:S(2)}) copy-start(f32[128]{0:T(128)} %param.17) | copy-start | bytes 1540
  8.5 31.3 %collective-permute-start.2 = (bf16[272,1536]{1,0:T(8,128)(2,1)}, bf16[272,1536]{1,0:T(8,128)(2,1)S(1)}, u32[]{:S(2)}, u32[]{:S(2)}) collective-permute-start(bf16[272,1536]{1,0:T(8,128)(2,1)} %get-tuple-element.34.b_ref.b_hbm), channel_id=1, source_target_pairs={{0,496},{16,32},{32,16},{48,64},{64,48},{80,96},{96,80},{112,128},... | collective-permute-start | bytes 2506760 | tf_op jit(solution)/shard_map/ppermute | solution.py:464
  20.5 1.2 %copy-start = (bf16[272,1536]{1,0:T(8,128)(2,1)S(1)}, bf16[272,1536]{1,0:T(8,128)(2,1)}, u32[]{:S(2)}) copy-start(bf16[272,1536]{1,0:T(8,128)(2,1)} %get-tuple-element.33.a_ref.a_hbm) | copy-start | bytes 2506756
  21.7 1.1 %copy-start.2 = (bf16[272,1536]{1,0:T(8,128)(2,1)S(1)}, bf16[272,1536]{1,0:T(8,128)(2,1)}, u32[]{:S(2)}) copy-start(bf16[272,1536]{1,0:T(8,128)(2,1)} %get-tuple-element.34.b_ref.b_hbm) | copy-start | bytes 2506756
  26.5 1.0 copy-start.11
  27.4 0.9 copy-start.12
  28.3 0.9 copy-start.13
  29.2 36.8 %copy-start.7 = (f32[128,1536]{1,0:T(8,128)}, f32[128,1536]{1,0:T(8,128)S(1)}, u32[]{:S(2)}) copy-start(f32[128,1536]{1,0:T(8,128)S(1)} %get-tuple-element.43.query_unit_ref.query_unit_hbm) | copy-start | bytes 2359300
  29.2 36.8 %copy-start.8 = (f32[128,1536]{1,0:T(8,128)}, f32[128,1536]{1,0:T(8,128)S(1)}, u32[]{:S(2)}) copy-start(f32[128,1536]{1,0:T(8,128)S(1)} %get-tuple-element.44.key_unit_ref.key_unit_hbm) | copy-start | bytes 2359300
  29.2 36.9 %copy-start.9 = (f32[128,1536]{1,0:T(8,128)}, f32[128,1536]{1,0:T(8,128)S(1)}, u32[]{:S(2)}) copy-start(f32[128,1536]{1,0:T(8,128)S(1)} %get-tuple-element.46.dot_ref.dot_hbm) | copy-start | bytes 2359300
  29.2 36.9 %copy-start.17 = (f32[2,128]{1,0:T(2,128)}, f32[2,128]{1,0:T(2,128)S(1)}, u32[]{:S(2)}) copy-start(f32[2,128]{1,0:T(2,128)S(1)} %get-tuple-element.40.gains_ref.gains_hbm) | copy-start | bytes 3076
  29.3 12.5 %copy-start.1 = (bf16[272,1536]{1,0:T(8,128)(2,1)S(1)}, bf16[272,1536]{1,0:T(8,128)(2,1)}, u32[]{:S(2)}) copy-start(bf16[272,1536]{1,0:T(8,128)(2,1)} %get-tuple-element.33.a_ref.a_hbm) | copy-start | bytes 2506756
  29.3 12.5 %copy-start.3 = (bf16[272,1536]{1,0:T(8,128)(2,1)S(1)}, bf16[272,1536]{1,0:T(8,128)(2,1)}, u32[]{:S(2)}) copy-start(bf16[272,1536]{1,0:T(8,128)(2,1)} %get-tuple-element.34.b_ref.b_hbm) | copy-start | bytes 2506756
  29.3 27.8 %collective-permute-start.1 = (bf16[272,1536]{1,0:T(8,128)(2,1)S(1)}, bf16[272,1536]{1,0:T(8,128)(2,1)S(1)}, u32[]{:S(2)}, u32[]{:S(2)}) collective-permute-start(bf16[272,1536]{1,0:T(8,128)(2,1)S(1)} %shard_map.148.a1_ref), channel_id=1, source_target_pairs={{0,496},{16,32},{32,16},{48,64},{64,48},{80,96},{96,80},{112,128},... | collective-permute-start | bytes 2506760 | tf_op jit(solution)/shard_map/ppermute | solution.py:464
  39.8 20.3 %collective-permute-start.3 = (bf16[272,1536]{1,0:T(8,128)(2,1)S(1)}, bf16[272,1536]{1,0:T(8,128)(2,1)}, u32[]{:S(2)}, u32[]{:S(2)}) collective-permute-start(bf16[272,1536]{1,0:T(8,128)(2,1)S(1)} %collective-permute-done.2.b1_ref), channel_id=1, source_target_pairs={{0,16},{16,0},{32,48},{48,32},{64,80},{80,64},{96,112},{112,96},{1... | collective-permute-start | bytes 2506760 | tf_op jit(solution)/shard_map/ppermute | solution.py:464
  46.4 0.6 copy-start.16
  47.0 10.2 %copy-start.10 = (f32[128,1536]{1,0:T(8,128)}, f32[128,1536]{1,0:T(8,128)S(1)}, u32[]{:S(2)}) copy-start(f32[128,1536]{1,0:T(8,128)S(1)} %get-tuple-element.50.dv_hbm) | copy-start | bytes 2359300
  47.0 19.1 %copy-start.6 = (f32[128,1536]{1,0:T(8,128)}, f32[128,1536]{1,0:T(8,128)S(1)}, u32[]{:S(2)}) copy-start(f32[128,1536]{1,0:T(8,128)S(1)} %get-tuple-element.42.dk_ref.dk_hbm) | copy-start | bytes 2359300
  57.1 12.3 %copy-start.4 = (bf16[272,1536]{1,0:T(8,128)(2,1)}, bf16[272,1536]{1,0:T(8,128)(2,1)S(1)}, u32[]{:S(2)}) copy-start(bf16[272,1536]{1,0:T(8,128)(2,1)S(1)} %shard_map.150.a2_ref.a2_hbm) | copy-start | bytes 2506756
  57.1 30.0 %collective-permute-start.4 = (bf16[272,1536]{1,0:T(8,128)(2,1)S(1)}, bf16[272,1536]{1,0:T(8,128)(2,1)}, u32[]{:S(2)}, u32[]{:S(2)}) collective-permute-start(bf16[272,1536]{1,0:T(8,128)(2,1)S(1)} %shard_map.150.a2_ref.a2_hbm), channel_id=1, source_target_pairs={{0,16},{16,0},{32,48},{48,32},{64,80},{80,64},{96,112},{112,96},{1... | collective-permute-start | bytes 2506760 | tf_op jit(solution)/shard_map/ppermute | solution.py:464
  60.1 27.1 %collective-permute-start.5 = (bf16[272,1536]{1,0:T(8,128)(2,1)}, bf16[272,1536]{1,0:T(8,128)(2,1)}, u32[]{:S(2)}, u32[]{:S(2)}) collective-permute-start(bf16[272,1536]{1,0:T(8,128)(2,1)} %collective-permute-done.3.b2_ref.b2_hbm), channel_id=1, source_target_pairs={{0,496},{16,32},{32,16},{48,64},{64,48},{80,96},{96,80},{112,128},... | collective-permute-start | bytes 2506760 | tf_op jit(solution)/shard_map/ppermute | solution.py:464
  69.4 12.6 %copy-start.5 = (f32[128,1536]{1,0:T(8,128)}, f32[128,1536]{1,0:T(8,128)S(1)}, u32[]{:S(2)}) copy-start(f32[128,1536]{1,0:T(8,128)S(1)} %get-tuple-element.49.dq_hbm) | copy-start | bytes 2359300
  82.0 16.0 %all-to-all-start.1 = ((f32[64,2,128]{2,1,0:T(2,128)}), f32[64,2,128]{2,1,0:T(2,128)S(1)}, u32[]{:S(2)}, u32[]{:S(2)}) async-start(f32[64,2,128]{2,1,0:T(2,128)} %shard_map.152.sums_ref), calls=%async_computation.1 | async-start | bytes 131072 | tf_op jit(solution)/shard_map/all_to_all | solution.py:540
  98.0 0.7 copy-start.23
